TPU v7x, 512 devices: a whole 4x8x8 slice. The times are simulated.
512 devices in a mesh: gz: 16 (over x, z_lo), th: 32 (over z_hi, y, core).
Axes of the slice: x: 4, y: 8, z: 8 (z_hi: 2, z_lo: 4; z = z_hi * 4 + z_lo), core: 2. Of those that a mesh axis runs over, the one named last changes fastest.
Arguments:
- density: float32 [256, 64, 2048], P('th', None, 'gz'), may hold values from 0.5 to 2
- velocity: float32 [3, 256, 64, 2048], P(None, 'th', None, 'gz'), may hold values from -3 to 3
- pressure: float32 [256, 64, 2048], P('th', None, 'gz'), may hold values from 0.5 to 2
Outputs:
- advanced: float32 [5, 256, 64, 2048], P(None, 'th', None, 'gz')
All inputs are finite; a program needn't handle non-finite values.
Results may differ from a plain program's by a relative error of at most 0.0003.
Values sent between devices are 32-bit elements; how exact they have to be, the bound alone decides.
No kernel may reach another device: no remote copies, remote signals or barrier semaphores. Data moves between devices by JAX's collectives and lax.ppermute only.
A program may use at most 64 MiB of HBM per device.

v0:
```python
import math

import jax
import jax.numpy as jnp
from jax import lax
from jax.sharding import PartitionSpec as P

NTH = 256
NF = 8


GAMMA_GAS = 1.4
DISSIPATION = 0.2
STEP_FACTOR = 0.25


def extended(value, sides, width):
    for axis, dim in sides:
        size, length = (lax.axis_size(axis), value.shape[dim])
        up = [(i, (i + 1) % size) for i in range(size)]
        down = [(j, i) for i, j in up]
        last = lax.slice_in_dim(value, length - width, length, axis=dim)
        leading = lax.slice_in_dim(value, 0, width, axis=dim)
        before = lax.ppermute(last, axis, up)
        after = lax.ppermute(leading, axis, down)
        value = jnp.concatenate([before, value, after], axis=dim)
    return value


def partner_2(value, axis, bit):
    return lax.ppermute(value, axis, [(i, i ^ 1 << bit) for i in range(lax.axis_size(axis))])


def conserved(primitive):
    density = primitive[0]
    kinetic = (
        0.5
        * density
        * (primitive[1] * primitive[1] + primitive[2] * primitive[2] + primitive[3] * primitive[3])
    )
    energy = primitive[4] / (GAMMA_GAS - 1.0) + kinetic
    return jnp.stack(
        [density, density * primitive[1], density * primitive[2], density * primitive[3], energy]
    )


def flux_along(primitive, direction):
    density = primitive[0]
    pressure = primitive[4]
    kinetic = (
        0.5
        * density
        * (primitive[1] * primitive[1] + primitive[2] * primitive[2] + primitive[3] * primitive[3])
    )
    energy = pressure / (GAMMA_GAS - 1.0) + kinetic
    velocity_along = primitive[1 + direction]
    moving = density * velocity_along
    components = [
        moving,
        moving * primitive[1],
        moving * primitive[2],
        moving * primitive[3],
        velocity_along * (energy + pressure),
    ]
    components[1 + direction] = components[1 + direction] + pressure
    return jnp.stack(components)


def tendency(
    radial_ext, theta_low, theta_high, axial_low, axial_high, radius_ext, theta_step, radial_step
):
    radius_mid = radius_ext[:, :, 1:-1, :]
    center = radial_ext[:, :, 1:-1, :]
    conserved_ext = conserved(radial_ext)
    conserved_mid = conserved_ext[:, :, 1:-1, :]
    flux_radial = flux_along(radial_ext, 0) * radius_ext
    div_radial = (flux_radial[:, :, 2:, :] - flux_radial[:, :, :-2, :]) / (
        2.0 * radial_step * radius_mid
    )
    div_theta = (flux_along(theta_high, 1) - flux_along(theta_low, 1)) / (
        2.0 * theta_step * radius_mid
    )
    div_axial = (flux_along(axial_high, 2) - flux_along(axial_low, 2)) / (2.0 * radial_step)
    smooth_radial = (
        conserved_ext[:, :, 2:, :] - 2.0 * conserved_mid + conserved_ext[:, :, :-2, :]
    ) / radial_step
    smooth_theta = (conserved(theta_high) - 2.0 * conserved_mid + conserved(theta_low)) / (
        theta_step * radius_mid
    )
    smooth_axial = (
        conserved(axial_high) - 2.0 * conserved_mid + conserved(axial_low)
    ) / radial_step
    smoothing = DISSIPATION * (smooth_radial + smooth_theta + smooth_axial)
    density = center[0]
    radial_speed = center[1]
    azimuth = center[2]
    pressure = center[4]
    zeros_field = jnp.zeros_like(density)
    source = jnp.stack(
        [
            zeros_field,
            (density * azimuth * azimuth + pressure) / radius_mid[0],
            -density * radial_speed * azimuth / radius_mid[0],
            zeros_field,
            zeros_field,
        ]
    )
    return conserved_mid + STEP_FACTOR * radial_step * (
        smoothing + source - div_radial - div_theta - div_axial
    )


def wave_tables(points):
    steps_int = jnp.arange(points, dtype=jnp.int32)
    phases = steps_int[:, None] * steps_int[None, :] % points
    angles = phases.astype(jnp.float32) * (2.0 * math.pi / points)
    return (jnp.cos(angles), jnp.sin(angles))


def filter_gains(cycle_count, points):
    modes = jnp.arange(points, dtype=jnp.int32)
    folded = jnp.minimum(modes, points - modes)
    cycles_int = jnp.arange(cycle_count, dtype=jnp.int32)
    keep = 2 * (cycle_count + 1) * folded[:, None] <= points * (cycles_int[None, :] + 1)
    return jnp.where(keep, jnp.float32(1.0), jnp.float32(0.0))


def per_device(density, velocity, pressure):
    primitive = jnp.concatenate([density[None], velocity, pressure[None]], axis=0)
    sectors = primitive.shape[1]
    cycle_total = primitive.shape[2]
    axial_cells = primitive.shape[3]
    padded = extended(primitive, (("gz", 3), ("th", 1)), 1)
    mirror = jnp.array([1.0, -1.0, -1.0, 1.0, 1.0], dtype=jnp.float32).reshape(5, 1, 1, 1)
    partner = partner_2(primitive[:, :, 0:1, :], "th", lax.axis_size("th").bit_length() - 2)
    radial_ext = jnp.concatenate([partner * mirror, primitive, primitive[:, :, -1:, :]], axis=2)
    radial_step = 1.0 / cycle_total
    theta_step = 2.0 * math.pi / NTH
    radius_ext = ((jnp.arange(cycle_total + 2, dtype=jnp.float32) - 0.5) * radial_step).reshape(
        1, 1, cycle_total + 2, 1
    )
    updated = tendency(
        radial_ext,
        padded[:, 0:sectors, :, 1 : axial_cells + 1],
        padded[:, 2 : sectors + 2, :, 1 : axial_cells + 1],
        padded[:, 1 : sectors + 1, :, 0:axial_cells],
        padded[:, 1 : sectors + 1, :, 2 : axial_cells + 2],
        radius_ext,
        theta_step,
        radial_step,
    )
    inner_cycles = updated[:, :, :NF, :]
    cosine_table, sine_table = wave_tables(NTH)
    damping = filter_gains(NF, NTH)
    high = lax.Precision.HIGHEST
    own_first = lax.axis_index("th") * sectors
    own_cos = lax.dynamic_slice_in_dim(cosine_table, own_first, sectors, 0)
    own_sin = lax.dynamic_slice_in_dim(sine_table, own_first, sectors, 0)
    weights_own = jnp.einsum("pm,mr,tm->rpt", own_cos, damping, cosine_table, precision=high)
    weights_own = (
        weights_own + jnp.einsum("pm,mr,tm->rpt", own_sin, damping, sine_table, precision=high)
    ) / NTH
    filtered = jnp.einsum(
        "rpt,ftrz->fprz",
        weights_own,
        lax.all_gather(inner_cycles, "th", axis=1, tiled=True),
        precision=high,
    )
    return jnp.concatenate([filtered, updated[:, :, NF:, :]], axis=2)


def solution(mesh):
    in_specs = (P("th", None, "gz"), P(None, "th", None, "gz"), P("th", None, "gz"))
    out_specs = P(None, "th", None, "gz")
    return jax.shard_map(
        per_device, mesh=mesh, in_specs=in_specs, out_specs=out_specs, check_vma=False
    )
```

profile of v0, /device:TPU:1, one launch (start us, length us, event | category | flops | bytes accessed | tf_op | source)
XLA Modules:
  0.0 194.0 jit_solution(8912242521704672092)
XLA Ops:
  6.5 0.0 copy-start.8
  6.6 0.0 copy-start.9
  6.6 1.2 fusion.48
  7.8 0.1 copy-done.5
  7.8 0.5 copy.17
  8.3 0.1 multiply_bitcast_fusion.2
  8.4 1.4 fusion.21
  9.8 0.1 pad_maximum_fusion
  9.9 1.5 fusion.47
  11.3 1.8 copy.19
  13.1 10.6 %collective-permute-start.2 = (f32[5,8,64,1]{2,1,3,0:T(8,128)S(1)}, f32[5,8,64,1]{2,1,3,0:T(8,128)S(1)}, u32[]{:S(2)}, u32[]{:S(2)}) collective-permute-start(f32[5,8,64,1]{2,1,3,0:T(8,128)S(1)} %copy.19), channel_id=1, source_target_pairs={{32,0},{64,32},{96,64},{128,96},{160,128},{192,160},{224,192},{256... | collective-permute-start | bytes 30728 | tf_op jit(solution)/shard_map/ppermute | solution.py:25
  23.7 0.5 copy.18
  24.2 1.9 collective-permute-start.1
  26.1 0.0 copy-done
  26.2 7.9 %collective-permute-start = (f32[5,8,1,128]{3,1,0,2:T(8,128)S(1)}, f32[5,8,1,128]{3,1,0,2:T(8,128)S(1)}, u32[]{:S(2)}, u32[]{:S(2)}) collective-permute-start(f32[5,8,1,128]{3,1,0,2:T(8,128)S(1)} %pad_maximum_fusion.39), channel_id=1, source_target_pairs={{0,16},{1,17},{2,18},{3,19},{4,20},{5,21},{6,22},{7,23},{8,24},{9,... | collective-permute-start | bytes 61448 | tf_op jit(solution)/shard_map/ppermute | solution.py:31
  34.1 0.1 pad.5.clone
  34.2 0.0 collective-permute-done.2
  34.2 0.5 copy.21
  34.8 0.0 collective-permute-done.1
  34.8 0.5 copy.20
  35.3 0.0 copy-start.10
  35.3 4.4 %pad_maximum_fusion.2 = (f32[5,1,64,130]{3,1,0,2:T(1,128)S(1)}, f32[5,1,64,130]{3,1,0,2:T(1,128)S(1)}) fusion(f32[5,8,64,1]{3,1,0,2:T(8,128)S(1)} %copy.21, f32[5,8,64,1]{3,1,0,2:T(8,128)S(1)} %copy.20, f32[1,8,64,128]{3,1,0,2:T(8,128)} %copy-done.2, f32[3,8,64,128]{3,1,0,2:T(8,128)S(1)} %copy.17, f32[1,8,64,128]{3,1,0,2:T(8,128)} %copy-done), kind=kLoop, calls=%fused_computation.37 | loop fusion | flops 332800 | bytes 1664000 | tf_op jit(solution)/shard_map/concatenate | solution.py:26
  39.7 4.3 %collective-permute-start.4 = (f32[5,1,64,130]{3,1,0,2:T(1,128)S(1)}, f32[5,1,64,130]{3,1,0,2:T(1,128)S(1)}, u32[]{:S(2)}, u32[]{:S(2)}) collective-permute-start(f32[5,1,64,130]{3,1,0,2:T(1,128)S(1)} %get-tuple-element.62), channel_id=1, source_target_pairs={{0,1},{1,2},{2,3},{3,4},{4,5},{5,6},{6,7},{7,8},{8,9},{9,10},{10,1... | collective-permute-start | bytes 499208 | tf_op jit(solution)/shard_map/ppermute | solution.py:24
  44.0 1.9 collective-permute-start.3
  46.0 0.0 collective-permute-done
  46.0 0.1 broadcast_multiply_fusion.3
  46.1 0.1 fusion
  46.3 0.1 multiply_dynamic-update-slice_fusion.3
  46.4 0.1 constant_dynamic-update-slice_fusion
  46.6 0.2 broadcast_multiply_fusion
  46.8 1.2 collective-permute-done.4
  48.0 0.3 constant_dynamic-update-slice_fusion.7
  48.4 4.3 %collective-permute-done.3 = f32[5,1,64,130]{3,1,0,2:T(1,128)S(1)} collective-permute-done((f32[5,1,64,130]{3,1,0,2:T(1,128)S(1)}, f32[5,1,64,130]{3,1,0,2:T(1,128)S(1)}, u32[]{:S(2)}, u32[]{:S(2)}) %collective-permute-start.3) | collective-permute-done | bytes 166432 | tf_op jit(solution)/shard_map/ppermute | solution.py:25
  52.7 0.4 multiply_dynamic-update-slice_fusion.22
  53.1 0.4 constant_dynamic-update-slice_fusion.6
  53.5 0.4 multiply_dynamic-update-slice_fusion.21
  53.9 0.1 multiply_dynamic-update-slice_fusion.18
  54.0 0.3 multiply_dynamic-update-slice_fusion.17
  54.3 0.4 constant_dynamic-update-slice_fusion.5
  54.7 0.3 constant_dynamic-update-slice_fusion.2
  55.1 0.3 constant_dynamic-update-slice_fusion.11
  55.6 0.2 constant_dynamic-update-slice_fusion.9
  55.9 0.2 constant_dynamic-update-slice_fusion.8
  56.2 0.2 multiply_dynamic-update-slice_fusion.5
  56.4 0.1 add_dynamic-update-slice_fusion.2
  56.5 0.2 multiply_dynamic-update-slice_fusion.8
  56.7 0.7 copy-done.6
  57.4 0.1 copy-done.7
  57.5 2.2 %fusion.6 = f32[5,8,64,128]{3,1,0,2:T(8,128)S(1)} fusion(f32[5,8,66,128]{3,1,0,2:T(8,128)S(1)} %broadcast_multiply_fusion, f32[5,8,66,128]{3,1,0,2:T(8,128)S(1)} %get-tuple-element.49, f32[1,8,64,128]{3,1,0,2:T(8,128)S(1)} %copy-done.7, f32[1,8,64,128]{3,1,0,2:T(8,128)S(1)} %copy-done.6, f32[5,8,64,128]{3,1,0,2:T(8,128)S(1)} %get-tuple-element.95, ...), kind=kLoop, calls=%fused_computation.10 | loop fusion | flops 9175040 | bytes 18875176 | tf_op jit(solution)/shard_map/add | solution.py:108
  59.7 0.0 copy-start.4
  59.7 0.7 slice.302
  60.4 0.0 all-gather.2.cloned.1.call-update
  60.5 1.0 fusion.34
  61.4 1.0 fusion.35
  62.4 0.1 dynamic-slice_bitcast_fusion
  62.5 0.1 compare_select_fusion
  62.6 0.3 broadcast_multiply_fusion.1
  63.0 2.5 %fusion.17 = f32[8,8,256]{2,1,0:T(8,128)S(1)} fusion(f32[256,8,8]{2,1,0:T(8,128)S(1)} %get-tuple-element.90), kind=kOutput, calls=%fused_computation.28 | convolution fusion | flops 51249152 | bytes 131072 | tf_op jit(solution)/shard_map/pm,mr,tm->rpt/dot_general | solution.py:159
  65.5 2.6 %fusion.15 = f32[8,8,256,1]{2,1,3,0:T(8,128)S(1)} fusion(f32[8,8,256]{2,1,0:T(8,128)S(1)} %fusion.17, f32[256,8,8]{2,1,0:T(8,128)S(1)} %get-tuple-element.89), kind=kOutput, calls=%fused_computation.26 | convolution fusion | flops 51281920 | bytes 196608 | tf_op jit(solution)/shard_map/pm,mr,tm->rpt/dot_general | solution.py:161
  68.1 0.0 slice-start
  68.1 113.0 %all-gather.2.cloned.1.call-done = f32[5,256,8,128]{3,1,0,2:T(8,128)} async-done(((f32[5,8,8,128]{3,1,0,2:T(8,128)}), f32[5,256,8,128]{3,1,0,2:T(8,128)}) %all-gather.2.cloned.1.call-update) | async-done | bytes 5242896 | tf_op jit(solution)/shard_map/all_gather | solution.py:166
  181.1 4.7 %convolution_bitcast_fusion = f32[5,8,8,128]{3,1,0,2:T(8,128)S(1)} fusion(f32[5,256,8,128]{3,1,0,2:T(8,128)} %all-gather.2.cloned.1.call-done, f32[8,8,256,1]{2,1,3,0:T(8,128)S(1)} %fusion.15), kind=kOutput, calls=%fused_computation.23 | convolution fusion | flops 125829120 | bytes 5472256 | tf_op jit(solution)/shard_map/rpt,ftrz->fprz/dot_general | solution.py:163
  185.8 0.1 pad_maximum_fusion.1
  185.9 1.3 copy.30
  (41 shorter events, 0.6 us)
Async XLA Ops:
  6.5 1.3 copy-start.5
  6.5 174.6 %all-gather.2.cloned.1.call-start = ((), (), s32[]{:S(2)}) async-start(), calls=%async_computation | async-start | bytes 5406720 | tf_op jit(solution)/shard_map/all_gather | solution.py:166
  6.5 1.8 copy-start.8
  6.6 1.8 copy-start.9
  9.8 16.4 %copy-start = (f32[1,8,64,128]{3,1,0,2:T(8,128)}, f32[1,8,64,128]{3,1,0,2:T(8,128)S(1)}, u32[]{:S(2)}) copy-start(f32[1,8,64,128]{3,1,0,2:T(8,128)S(1)} %get-tuple-element.87) | copy-start | bytes 786436
  9.8 16.4 %copy-start.2 = (f32[1,8,64,128]{3,1,0,2:T(8,128)}, f32[1,8,64,128]{3,1,0,2:T(8,128)S(1)}, u32[]{:S(2)}) copy-start(f32[1,8,64,128]{3,1,0,2:T(8,128)S(1)} %get-tuple-element.88) | copy-start | bytes 786436
  13.1 21.1 %collective-permute-start.2 = (f32[5,8,64,1]{2,1,3,0:T(8,128)S(1)}, f32[5,8,64,1]{2,1,3,0:T(8,128)S(1)}, u32[]{:S(2)}, u32[]{:S(2)}) collective-permute-start(f32[5,8,64,1]{2,1,3,0:T(8,128)S(1)} %copy.19), channel_id=1, source_target_pairs={{32,0},{64,32},{96,64},{128,96},{160,128},{192,160},{224,192},{256... | collective-permute-start | bytes 30728 | tf_op jit(solution)/shard_map/ppermute | solution.py:25
  24.2 10.5 %collective-permute-start.1 = (f32[5,8,64,1]{2,1,3,0:T(8,128)S(1)}, f32[5,8,64,1]{2,1,3,0:T(8,128)S(1)}, u32[]{:S(2)}, u32[]{:S(2)}) collective-permute-start(f32[5,8,64,1]{2,1,3,0:T(8,128)S(1)} %copy.18), channel_id=1, source_target_pairs={{0,32},{32,64},{64,96},{96,128},{128,160},{160,192},{192,224},{224... | collective-permute-start | bytes 30728 | tf_op jit(solution)/shard_map/ppermute | solution.py:24
  26.2 19.8 %collective-permute-start = (f32[5,8,1,128]{3,1,0,2:T(8,128)S(1)}, f32[5,8,1,128]{3,1,0,2:T(8,128)S(1)}, u32[]{:S(2)}, u32[]{:S(2)}) collective-permute-start(f32[5,8,1,128]{3,1,0,2:T(8,128)S(1)} %pad_maximum_fusion.39), channel_id=1, source_target_pairs={{0,16},{1,17},{2,18},{3,19},{4,20},{5,21},{6,22},{7,23},{8,24},{9,... | collective-permute-start | bytes 61448 | tf_op jit(solution)/shard_map/ppermute | solution.py:31
  35.3 10.7 %copy-start.10 = (f32[5]{0:T(128)S(1)}, f32[5]{0:T(128)}, u32[]{:S(2)}) copy-start(f32[5]{0:T(128)} %constant.74.clone) | copy-start | bytes 64
  35.3 10.7 %copy-start.1 = (f32[1,8,64,128]{3,1,0,2:T(8,128)S(1)}, f32[1,8,64,128]{3,1,0,2:T(8,128)}, u32[]{:S(2)}) copy-start(f32[1,8,64,128]{3,1,0,2:T(8,128)} %copy-done) | copy-start | bytes 786436
  35.3 10.7 %copy-start.3 = (f32[1,8,64,128]{3,1,0,2:T(8,128)S(1)}, f32[1,8,64,128]{3,1,0,2:T(8,128)}, u32[]{:S(2)}) copy-start(f32[1,8,64,128]{3,1,0,2:T(8,128)} %copy-done.2) | copy-start | bytes 786436
  39.7 8.3 %collective-permute-start.4 = (f32[5,1,64,130]{3,1,0,2:T(1,128)S(1)}, f32[5,1,64,130]{3,1,0,2:T(1,128)S(1)}, u32[]{:S(2)}, u32[]{:S(2)}) collective-permute-start(f32[5,1,64,130]{3,1,0,2:T(1,128)S(1)} %get-tuple-element.62), channel_id=1, source_target_pairs={{0,1},{1,2},{2,3},{3,4},{4,5},{5,6},{6,7},{7,8},{8,9},{9,10},{10,1... | collective-permute-start | bytes 499208 | tf_op jit(solution)/shard_map/ppermute | solution.py:24
  44.0 8.7 %collective-permute-start.3 = (f32[5,1,64,130]{3,1,0,2:T(1,128)S(1)}, f32[5,1,64,130]{3,1,0,2:T(1,128)S(1)}, u32[]{:S(2)}, u32[]{:S(2)}) collective-permute-start(f32[5,1,64,130]{3,1,0,2:T(1,128)S(1)} %get-tuple-element.63), channel_id=1, source_target_pairs={{1,0},{2,1},{3,2},{4,3},{5,4},{6,5},{7,6},{8,7},{9,8},{10,9},{11,1... | collective-permute-start | bytes 499208 | tf_op jit(solution)/shard_map/ppermute | solution.py:25
  56.5 1.0 copy-start.6
  56.5 1.0 copy-start.7
  59.7 8.4 %copy-start.4 = (f32[5,8,64,128]{3,1,0,2:T(8,128)}, f32[5,8,64,128]{3,1,0,2:T(8,128)S(1)}, u32[]{:S(2)}) copy-start(f32[5,8,64,128]{3,1,0,2:T(8,128)S(1)} %fusion.6) | copy-start | bytes 3932164
  68.1 117.7 %slice-start = ((f32[5,8,64,128]{3,1,0,2:T(8,128)}), f32[5,8,56,128]{3,1,0,2:T(8,128)S(1)}, s32[]{:S(2)}) async-start(f32[5,8,64,128]{3,1,0,2:T(8,128)} %copy-done.4), calls=%async_computation.1 | async-start | bytes 2293760 | tf_op jit(solution)/shard_map/slice | solution.py:169
Sparse Core Ops, SparseCore 0:
  60.5 120.5 all-gather.1
where the time goes:
time: 194 us
  waiting for transfers between devices  119 us (61%)
  starting transfers between devices  26.8 us (14%)
  other arithmetic  15.4 us (8%)
  between operations  13.9 us (7%)
  matrix products  9.77 us (5%)
  local copies, waits for them, and re-layouts  9.63 us (5%)
    all_gather x1, waiting for transfers between devices, per_device(): lax.all_gather(inner_cycles, 'th', axis=1, tiled=True)  113 us
    ppermute x2, starting transfers between devices, extended(): after = lax.ppermute(leading, axis, down)  12.6 us
    ppermute x1, starting transfers between devices, partner_2(): lax.ppermute(value, axis, [(i, i ^ 1 << bit) for i in range(lax.axis_size...  7.94 us
    ppermute x2, starting transfers between devices, extended(): before = lax.ppermute(last, axis, up)  6.25 us
    dot_general x1, matrix products, per_device(): jnp.einsum('rpt,ftrz->fprz', weights_own, lax.all_gather(inner_cycles, 't...  4.67 us
    concatenate x1, other arithmetic, extended(): value = jnp.concatenate([before, value, after], axis=dim)  4.36 us
    ppermute x2, waiting for transfers between devices, extended(): after = lax.ppermute(leading, axis, down)  4.35 us
  transfers between devices with their start and end apart: 6, of which 3 were waited for; matrix products, arithmetic and copies ran while one was open for 8% of the time, Pallas kernels for 0%

commit v1 on v0

v1 whole, which is shorter than its diff:
```python
import math

import jax
import jax.numpy as jnp
import ml_dtypes
import numpy as np
from jax import lax
from jax.experimental import pallas as pl
from jax.experimental.pallas import tpu as pltpu
from jax.sharding import PartitionSpec as P

NTH = 256
NR = 64
NF = 8
N_TH = 32
SECTOR = NTH // N_TH
LANES = 128
FIELDS = 5
SEND_ROWS = 16
BACK_ROWS = 18

HALF_STEP = 0.125
SMOOTH = 0.05


def theta_factor(cycle):
    return 0.25 / (2.0 * (2.0 * math.pi / NTH) * (cycle + 0.5))


def filter_rows():
    modes = np.arange(NTH)
    folded = np.minimum(modes, NTH - modes)
    waves = np.cos(2.0 * math.pi * (modes[:, None] * modes[None, :] % NTH) / NTH)
    rows = []
    for cycle in range(NF):
        keep = 2 * (NF + 1) * folded <= NTH * (cycle + 1)
        rows.append(waves[:, keep].sum(axis=1) / NTH)
    return np.stack(rows)


def filter_matrices():
    rows = filter_rows()
    index = (np.arange(NTH)[:, None] - np.arange(NTH)[None, :]) % NTH
    full = np.concatenate([rows[:, index], rows[:1, (index + NTH // 2) % NTH]]).astype(np.float32)
    high = full.astype(ml_dtypes.bfloat16)
    low = (full - high.astype(np.float32)).astype(ml_dtypes.bfloat16)
    return high, low


def edge_weights():
    rows = filter_rows()
    table = np.zeros((2 * N_TH, SECTOR, LANES), np.float32)
    for row in range(2 * N_TH - 1):
        apart = (N_TH - 1 - row) * SECTOR
        index = (apart + np.arange(SECTOR)[:, None] - np.arange(SECTOR)[None, :]) % NTH
        block = np.repeat(rows[:, index].transpose(1, 0, 2)[..., None], 2, axis=3)
        table[row] = block.reshape(SECTOR, LANES)
    return table


def conserved(fields):
    rho, ur, ut, uz, p = fields
    qr, qt, qz = rho * ur, rho * ut, rho * uz
    energy = p * 2.5 + 0.5 * (qr * ur + qt * ut + qz * uz)
    return rho, qr, qt, qz, energy


def flux(fields, q, direction):
    p = fields[4]
    speed = fields[1 + direction]
    moving = q[1 + direction]
    parts = [moving, moving * fields[1], moving * fields[2], moving * fields[3], speed * (q[4] + p)]
    parts[1 + direction] = parts[1 + direction] + p
    return parts


def lanes_of(shape):
    return lax.broadcasted_iota(jnp.int32, shape, len(shape) - 1)


def rows_of(shape):
    return lax.broadcasted_iota(jnp.int32, shape, len(shape) - 2)


def spread(value, shift, axis):
    size = value.shape[axis]
    return pltpu.roll(value, shift % size, axis)


def half_packs(tile):
    turned = spread(tile, 64, 1)
    low = lanes_of((SECTOR, LANES)) < 64
    first = jnp.where(low, tile, spread(turned, 4, 0))
    second = jnp.where(low, turned, spread(tile, 4, 0))
    return first[:4], second[:4]


def inner_kernel(d_ref, v_ref, p_ref, out_ref):
    def load(cycle):
        return (
            d_ref[:, cycle, :],
            v_ref[0, :, cycle, :],
            v_ref[1, :, cycle, :],
            v_ref[2, :, cycle, :],
            p_ref[:, cycle, :],
        )

    shape = (SECTOR, LANES)
    lane, row = lanes_of(shape), rows_of(shape)
    not_first_lane, not_last_lane = lane > 0, lane < LANES - 1
    not_first_row, not_last_row = row > 0, row < SECTOR - 1
    out_ref[...] = jnp.zeros(out_ref.shape, jnp.float32)

    before = None
    fields = load(0)
    q = conserved(fields)
    radial = flux(fields, q, 0)
    for f in range(FIELDS):
        sign = -1.0 if f in (1, 2) else 1.0
        mirrored = sign * (SMOOTH * q[f] + HALF_STEP * radial[f])
        for half, pack in enumerate(half_packs(mirrored)):
            out_ref[16 + 2 * f + half, 10:14, :] = pack
    for cycle in range(NF):
        after_fields = load(cycle + 1)
        after_q = conserved(after_fields)
        after = (after_q, flux(after_fields, after_q, 0))
        around = flux(fields, q, 1)
        along = flux(fields, q, 2)
        c = theta_factor(cycle)
        radius = cycle + 0.5
        scale = 0.25 / radius
        sources = (
            None,
            scale * (q[2] * fields[2] + fields[4]),
            -scale * (q[1] * fields[2]),
            None,
            None,
        )
        for f in range(FIELDS):
            own = q[f] * (0.8 - 0.8 * c)
            if sources[f] is not None:
                own = own + sources[f]
            smooth, push = SMOOTH * q[f], HALF_STEP * along[f]
            own = own + jnp.where(not_first_lane, spread(smooth + push, 1, 1), 0.0)
            own = own + jnp.where(not_last_lane, spread(smooth - push, -1, 1), 0.0)
            smooth, push = (0.4 * c) * q[f], c * around[f]
            rising, falling = smooth + push, smooth - push
            own = own + jnp.where(not_first_row, spread(rising, 1, 0), 0.0)
            own = own + jnp.where(not_last_row, spread(falling, -1, 0), 0.0)
            own = own + (SMOOTH * after[0][f] - (HALF_STEP * (radius + 1.0) / radius) * after[1][f])
            if before is not None:
                own = own + (SMOOTH * before[0][f] + (HALF_STEP * (radius - 1.0) / radius) * before[1][f])
            if f < 4:
                unit = f * NF + cycle
                out_ref[unit, 0:8, :] = own
                out_ref[unit, 8:9, :] = rising[7:8]
                out_ref[unit, 15:16, :] = falling[0:1]
            else:
                packs = half_packs(own)
                up, down = rising[7:8], falling[0:1]
                up_turned, down_turned = spread(up, 64, 1), spread(down, 64, 1)
                for half in range(2):
                    unit = half * NF + cycle
                    out_ref[unit, 10:14, :] = packs[half]
                    out_ref[unit, 9:10, :] = down if half == 0 else down_turned
                    out_ref[unit, 14:15, :] = up_turned if half == 0 else up
        before = (q, radial)
        fields, q, radial = after_fields, after_q, after[1]


def inner_part(density, velocity, pressure):
    return pl.pallas_call(
        inner_kernel,
        grid=(1,),
        in_specs=[
            pl.BlockSpec((SECTOR, 16, LANES), lambda i: (0, 0, 0)),
            pl.BlockSpec((3, SECTOR, 16, LANES), lambda i: (0, 0, 0, 0)),
            pl.BlockSpec((SECTOR, 16, LANES), lambda i: (0, 0, 0)),
        ],
        out_specs=pl.BlockSpec((N_TH, SEND_ROWS, LANES), lambda i: (0, 0, 0)),
        out_shape=jax.ShapeDtypeStruct((N_TH, SEND_ROWS, LANES), jnp.float32),
        cost_estimate=pl.CostEstimate(flops=8 * 1024 * 200, bytes_accessed=600_000, transcendentals=0),
        name="inner_part",
    )(density, velocity, pressure)


def edge_kernel(odd_ref, d_ref, v_ref, p_ref, columns_ref, near_ref, far_ref):
    lane = lanes_of((NR, LANES))
    odd = odd_ref[0] == 1

    def load(f, j):
        return d_ref[j] if f == 0 else (p_ref[j] if f == 4 else v_ref[f - 1, j])

    total = jnp.zeros((NR, LANES), jnp.float32)
    for f in range(FIELDS):
        for j in range(SECTOR):
            spot = 16 * f + 2 * j + 1
            total = jnp.where((lane == spot) | (lane == spot + 1), spread(load(f, j), spot + 1, 1), total)
        first, last = load(f, 0), load(f, SECTOR - 1)
        near_ref[f] = jnp.where(odd, first, last)
        far_ref[f] = jnp.where(odd, last, first)
    columns_ref[...] = total


def edges(odd, density, velocity, pressure):
    vmem = pl.BlockSpec(memory_space=pltpu.VMEM)
    rows = jax.ShapeDtypeStruct((FIELDS, NR, LANES), jnp.float32)
    return pl.pallas_call(
        edge_kernel,
        in_specs=[pl.BlockSpec(memory_space=pltpu.SMEM), vmem, vmem, vmem],
        out_specs=[vmem, vmem, vmem],
        out_shape=[jax.ShapeDtypeStruct((NR, LANES), jnp.float32), rows, rows],
        cost_estimate=pl.CostEstimate(flops=320 * 1024 * 3, bytes_accessed=1_800_000, transcendentals=0),
        name="edges",
    )(odd, density, velocity, pressure)


def axial_terms(near, far, odd):
    lane = lanes_of(near.shape)
    before = jnp.where(odd, near, far)
    after = jnp.where(odd, far, near)
    both = jnp.where(lane % 2 == 1, before, spread(after, -2, 1))
    fields = [both] + [spread(both, -16 * f, 1) for f in range(1, FIELDS)]
    q = conserved(fields)
    along = flux(fields, q, 2)
    push = jnp.where(lane % 2 == 1, HALF_STEP, -HALF_STEP)
    return [SMOOTH * q[f] + push * along[f] for f in range(FIELDS)]


def filter_kernel(which_ref, odd_ref, r_ref, wh_ref, wl_ref, hh_ref, hl_ref, near_ref, far_ref, out_ref):
    del which_ref
    shape = (N_TH, SECTOR, LANES)
    row, lane = rows_of(shape), lanes_of(shape)
    main = r_ref[:, 0:8, :]
    extra = r_ref[:, 8:16, :]
    before = jnp.concatenate([extra[-1:], extra[:-1]], axis=0)
    after = jnp.concatenate([extra[1:], extra[:1]], axis=0)
    zero = jnp.zeros(shape, jnp.float32)
    main = main + jnp.where(row == 0, before, jnp.where(row == 7, after, zero))
    turned = spread(extra, 64, 2)
    top = spread(extra, 6, 1)
    bottom = spread(turned, 2, 1)
    half = jnp.where(row < 4, top, bottom)
    half = half + jnp.where(
        row == 0,
        jnp.concatenate([bottom[-1:], bottom[:-1]], axis=0),
        jnp.where(row == 7, jnp.concatenate([top[1:], top[:1]], axis=0), zero),
    )

    def product(high, low, value):
        value = value.reshape(NTH, LANES)
        big = value.astype(jnp.bfloat16)
        small = (value - big.astype(jnp.float32)).astype(jnp.bfloat16)
        out = jnp.dot(high, big, preferred_element_type=jnp.float32)
        out = out + jnp.dot(high, small, preferred_element_type=jnp.float32)
        out = out + jnp.dot(low, big, preferred_element_type=jnp.float32)
        return out.reshape(shape)

    main = product(wh_ref[0], wl_ref[0], main)
    half = product(hh_ref[0], hl_ref[0], half)
    packed = jnp.where(lane < 64, half, spread(spread(half, 64, 2), 4, 1))

    terms = axial_terms(near_ref[...], far_ref[...], odd_ref[1] == 1)
    first = lanes_of((NF, LANES)) < 16
    border = [
        jnp.sum(
            pltpu.roll(jnp.where(first, term, 0.0), 0, 1, stride=16, stride_axis=0), axis=0, keepdims=True
        )
        for term in terms
    ]
    border = jnp.concatenate(border + [jnp.zeros((1, LANES), jnp.float32)], axis=0)
    for s in range(N_TH):
        base = s * BACK_ROWS
        out_ref[base : base + 8, :] = main[s]
        out_ref[base + 8 : base + 12, :] = packed[s, :4]
        out_ref[base + 12 : base + 18, :] = border


def filtered(which, odd, received, high, low, near, far):
    matrix = (1, NTH, NTH)
    grid_spec = pltpu.PrefetchScalarGridSpec(
        num_scalar_prefetch=2,
        grid=(1,),
        in_specs=[
            pl.BlockSpec((N_TH, SEND_ROWS, LANES), lambda i, w, o: (0, 0, 0)),
            pl.BlockSpec(matrix, lambda i, w, o: (w[0], 0, 0)),
            pl.BlockSpec(matrix, lambda i, w, o: (w[0], 0, 0)),
            pl.BlockSpec(matrix, lambda i, w, o: (w[1], 0, 0)),
            pl.BlockSpec(matrix, lambda i, w, o: (w[1], 0, 0)),
            pl.BlockSpec((NF, LANES), lambda i, w, o: (0, 0)),
            pl.BlockSpec((NF, LANES), lambda i, w, o: (0, 0)),
        ],
        out_specs=pl.BlockSpec((N_TH * BACK_ROWS, LANES), lambda i, w, o: (0, 0)),
    )
    return pl.pallas_call(
        filter_kernel,
        grid_spec=grid_spec,
        out_shape=jax.ShapeDtypeStruct((N_TH * BACK_ROWS, LANES), jnp.float32),
        cost_estimate=pl.CostEstimate(flops=6 * 256 * 256 * 256, bytes_accessed=1_200_000, transcendentals=0),
        name="filtered",
    )(which, odd, received, high, low, high, low, near, far)


def outer_kernel(odd_ref, d_ref, v_ref, p_ref, side_ref, back_ref, near_ref, far_ref, out_ref, terms_ref):
    th_odd, gz_odd = odd_ref[0] == 1, odd_ref[1] == 1
    terms = axial_terms(near_ref[...], far_ref[...], gz_odd)
    for f in range(FIELDS):
        terms_ref[f] = terms[f]
    shape = (NR, LANES)
    lane, row = lanes_of(shape), rows_of(shape)
    radius = row.astype(jnp.float32) + 0.5
    inverse = 1.0 / radius
    c = theta_factor(0) * 0.5 * inverse

    def load(j):
        return (d_ref[j], v_ref[0, j], v_ref[1, j], v_ref[2, j], p_ref[j])

    def step(j, carry):
        fields = load(j)
        below = load(jnp.maximum(j - 1, 0))
        above = load(jnp.minimum(j + 1, SECTOR - 1))
        use_low, use_high = j == 0, j == SECTOR - 1
        below = [
            jnp.where(use_low, jnp.where(th_odd, side_ref[f], back_ref[f]), below[f]) for f in range(FIELDS)
        ]
        above = [
            jnp.where(use_high, jnp.where(th_odd, back_ref[f], side_ref[f]), above[f]) for f in range(FIELDS)
        ]
        q = conserved(fields)
        radial = flux(fields, q, 0)
        along = flux(fields, q, 2)
        q_low, q_high = conserved(below), conserved(above)
        f_low, f_high = flux(below, q_low, 1), flux(above, q_high, 1)
        scale = 0.25 * inverse
        sources = (
            None,
            scale * (q[2] * fields[2] + fields[4]),
            -scale * (q[1] * fields[2]),
            None,
            None,
        )
        for f in range(FIELDS):
            own = q[f] * (0.8 - 0.8 * c)
            if sources[f] is not None:
                own = own + sources[f]
            smooth, push = SMOOTH * q[f], HALF_STEP * along[f]
            side = spread(terms_ref[f], LANES - 1 - 2 * j, 1)
            own = own + jnp.where(lane == 0, side, spread(smooth + push, 1, 1))
            own = own + jnp.where(lane == LANES - 1, side, spread(smooth - push, LANES - 1, 1))
            own = own + c * (0.4 * (q_low[f] + q_high[f]) + (f_low[f] - f_high[f]))
            push = (HALF_STEP * radius) * radial[f]
            smooth_ahead = jnp.where(row == NR - 1, smooth, spread(smooth, NR - 1, 0))
            push_ahead = jnp.where(row == NR - 1, push + HALF_STEP * radial[f], spread(push, NR - 1, 0))
            own = own + (smooth_ahead + spread(smooth, 1, 0))
            own = own + inverse * (spread(push, 1, 0) - push_ahead)
            out_ref[f, j] = own
        return carry

    lax.fori_loop(0, SECTOR, step, 0)


def outer_part(odd, density, velocity, pressure, side, back, near, far, token):
    vmem = pl.BlockSpec(memory_space=pltpu.VMEM)

    def kernel(odd_ref, d, v, p, s, b, n, f, token_ref, out_ref, terms_ref):
        del token_ref
        outer_kernel(odd_ref, d, v, p, s, b, n, f, out_ref, terms_ref)

    return pl.pallas_call(
        kernel,
        in_specs=[pl.BlockSpec(memory_space=pltpu.SMEM)] + [vmem] * 7 + [pl.BlockSpec(memory_space=pl.ANY)],
        out_specs=vmem,
        out_shape=jax.ShapeDtypeStruct((FIELDS, SECTOR, NR, LANES), jnp.float32),
        scratch_shapes=[pltpu.VMEM((FIELDS, NR, LANES), jnp.float32)],
        cost_estimate=pl.CostEstimate(flops=64 * 1024 * 250, bytes_accessed=3_000_000, transcendentals=0),
        name="outer_part",
    )(odd, density, velocity, pressure, side, back, near, far, token)


def finish_kernel(place_ref, r_ref, w_ref, rest_ref, out_ref):
    del rest_ref
    start = N_TH - 1 - place_ref[0]
    shape = (SECTOR, LANES)
    lane = lanes_of(shape)
    low_half = lanes_of((4, LANES)) < 64
    ends = (lane == 0) | (lane == LANES - 1)

    sums = [jnp.zeros(shape, jnp.float32) for _ in range(FIELDS)]
    for t in range(N_TH):
        weights = w_ref[start + t]
        base = t * BACK_ROWS + 12
        for f in range(FIELDS):
            sums[f] = sums[f] + weights * r_ref[base + f : base + f + 1, :]
    for f in range(FIELDS):
        for shift in (2, 4, 8):
            sums[f] = sums[f] + spread(sums[f], -shift, 1)

    def joined(unit_a, unit_b):
        a = r_ref[unit_a * BACK_ROWS + 8 : unit_a * BACK_ROWS + 12, :]
        b = r_ref[unit_b * BACK_ROWS + 8 : unit_b * BACK_ROWS + 12, :]
        top = jnp.where(low_half, a, spread(b, 64, 1))
        bottom = jnp.where(low_half, spread(a, 64, 1), b)
        return jnp.concatenate([top, bottom], axis=0)

    for f in range(FIELDS):
        for cycle in range(NF):
            if f < 4:
                unit = (f * NF + cycle) * BACK_ROWS
                tile = r_ref[unit : unit + 8, :]
            else:
                tile = joined(cycle, NF + cycle)
            if cycle == 0:
                tile = tile + joined(16 + 2 * f, 17 + 2 * f)
            tile = tile + jnp.where(ends, spread(sums[f], -(16 * cycle + 1), 1), 0.0)
            out_ref[f, :, cycle, :] = tile


def finish(place, received, weights, rest):
    inner = pl.BlockSpec((FIELDS, SECTOR, NF, LANES), lambda i, p: (0, 0, 0, 0))
    grid_spec = pltpu.PrefetchScalarGridSpec(
        num_scalar_prefetch=1,
        grid=(1,),
        in_specs=[
            pl.BlockSpec((N_TH * BACK_ROWS, LANES), lambda i, p: (0, 0)),
            pl.BlockSpec((2 * N_TH, SECTOR, LANES), lambda i, p: (0, 0, 0)),
            pl.BlockSpec(memory_space=pl.ANY),
        ],
        out_specs=inner,
    )
    return pl.pallas_call(
        finish_kernel,
        grid_spec=grid_spec,
        out_shape=jax.ShapeDtypeStruct((FIELDS, SECTOR, NR, LANES), jnp.float32),
        input_output_aliases={3: 0},
        cost_estimate=pl.CostEstimate(flops=400 * 1024, bytes_accessed=800_000, transcendentals=0),
        name="finish",
    )(place, received, weights, rest)


def pairs(size, offset):
    return [(i, (((i - offset) ^ 1) + offset) % size) for i in range(size)]


def per_device(density, velocity, pressure):
    high, low = filter_matrices()
    high, low = jnp.asarray(high), jnp.asarray(low)
    weights = jnp.asarray(edge_weights())
    th, gz = lax.axis_index("th"), lax.axis_index("gz")
    odd = jnp.stack([th % 2, gz % 2]).astype(jnp.int32)
    main = th % NF
    half = jnp.where(th < 16, main, jnp.where(th < 26, NF, 0))
    which = jnp.stack([main, half]).astype(jnp.int32)
    place = th.astype(jnp.int32).reshape(1)

    sent = inner_part(density, velocity, pressure)
    received = lax.all_to_all(sent, "th", 0, 0, tiled=True)

    columns, near_row, far_row = edges(odd, density, velocity, pressure)
    gz_near = lax.ppermute(columns, "gz", pairs(lax.axis_size("gz"), 0))
    gz_far = lax.ppermute(columns, "gz", pairs(lax.axis_size("gz"), 1))
    th_near = lax.ppermute(near_row, "th", pairs(N_TH, 0))
    th_far = lax.ppermute(far_row, "th", pairs(N_TH, 1))

    back = filtered(which, odd, received, high, low, gz_near, gz_far)
    returned = lax.all_to_all(
        back.reshape(N_TH, BACK_ROWS // 2, 2, LANES), "th", 0, 0, tiled=True
    ).reshape(N_TH * BACK_ROWS, LANES)
    rest = outer_part(odd, density, velocity, pressure, th_near, th_far, gz_near, gz_far, back)
    return finish(place, returned, weights, rest)


def solution(mesh):
    in_specs = (P("th", None, "gz"), P(None, "th", None, "gz"), P("th", None, "gz"))
    out_specs = P(None, "th", None, "gz")
    return jax.shard_map(
        per_device, mesh=mesh, in_specs=in_specs, out_specs=out_specs, check_vma=False
    )
```

time: 194 us -> 77.8 us (0.40)
  the two profiles are of different devices: /device:TPU:1 before, /device:TPU:57 now
where the time goes in v1:
time: 77.8 us; the launch traced here: 77.4 us
  starting transfers between devices  47.8 us (61%)
  Pallas kernels  15.8 us (20%)
  waiting for transfers between devices  9.77 us (13%)
  local copies, waits for them, and re-layouts  2.7 us (3%)
  other arithmetic  1.21 us (2%)
    all_to_all x1, starting transfers between devices, per_device(): received = lax.all_to_all(sent, 'th', 0, 0, tiled=True)  15.8 us
    all_to_all x1, starting transfers between devices, per_device(): lax.all_to_all(back.reshape(N_TH, BACK_ROWS // 2, 2, LANES), 'th', 0, 0,...  13.6 us
    ppermute x1, waiting for transfers between devices, per_device(): th_far = lax.ppermute(far_row, 'th', pairs(N_TH, 1))  7.4 us
    ppermute x1, starting transfers between devices, per_device(): gz_far = lax.ppermute(columns, 'gz', pairs(lax.axis_size('gz'), 1))  7.1 us
    ppermute x1, starting transfers between devices, per_device(): th_far = lax.ppermute(far_row, 'th', pairs(N_TH, 1))  7.03 us
    pallas_call x1, Pallas kernels, outer_part(): pl.pallas_call(kernel, in_specs=[pl.BlockSpec(memory_space=pltpu.SMEM)] +...  5.01 us
    pallas_call x1, Pallas kernels, inner_part(): pl.pallas_call(inner_kernel, grid=(1,), in_specs=[pl.BlockSpec((SECTOR, 1...  3.35 us
    pallas_call x1, Pallas kernels, filtered(): pl.pallas_call(filter_kernel, grid_spec=grid_spec, out_shape=jax.ShapeDty...  3 us
  transfers between devices with their start and end apart: 6, of which 3 were waited for; matrix products, arithmetic and copies ran while one was open for 2% of the time, Pallas kernels for 9%

profile of v1, /device:TPU:57, one launch (start us, length us, event | category | flops | bytes accessed | tf_op | source)
XLA Modules:
  0.0 77.4 jit_solution(9591920975157929713)
XLA Ops:
  0.0 3.4 %inner_part.1 = f32[32,16,128]{2,1,0:T(8,128)} custom-call(f32[8,64,128]{2,1,0:T(8,128)} %d.1, f32[3,8,64,128]{3,2,1,0:T(8,128)} %v.1, f32[8,64,128]{2,1,0:T(8,128)} %p.1), custom_call_target="tpu_custom_call" | custom-call | flops 1638400 | bytes 600000 | tf_op jit(solution)/shard_map/inner_part/pallas_call | solution.py:172
  3.4 15.8 %all-to-all-start = ((f32[32,16,128]{2,1,0:T(8,128)}), f32[32,16,128]{2,1,0:T(8,128)S(1)}, u32[]{:S(2)}, u32[]{:S(2)}) async-start(f32[32,16,128]{2,1,0:T(8,128)} %inner_part.1), calls=%async_computation | async-start | bytes 524288 | tf_op jit(solution)/shard_map/all_to_all | solution.py:456
  19.2 0.7 pad_add_fusion.1.odd_ref
  19.8 2.3 %edges.1 = (f32[64,128]{1,0:T(8,128)}, f32[5,64,128]{2,1,0:T(8,128)}, f32[5,64,128]{2,1,0:T(8,128)}) custom-call(s32[2]{0:T(128)} %pad_add_fusion.1.odd_ref, f32[8,64,128]{2,1,0:T(8,128)} %d.1, f32[3,8,64,128]{3,2,1,0:T(8,128)} %v.1, f32[8,64,128]{2,1,0:T(8,128)} %p.1), custom_call_target="tpu_custom_call" | custom-call | flops 983040 | bytes 1800000 | tf_op jit(solution)/shard_map/edges/pallas_call | solution.py:208
  22.1 7.1 %collective-permute-start.1 = (f32[64,128]{1,0:T(8,128)}, f32[64,128]{1,0:T(8,128)S(1)}, u32[]{:S(2)}, u32[]{:S(2)}) collective-permute-start(f32[64,128]{1,0:T(8,128)} %get-tuple-element.8), channel_id=1, source_target_pairs={{0,480},{32,64},{64,32},{96,128},{128,96},{160,192},{192,160},{224... | collective-permute-start | bytes 98312 | tf_op jit(solution)/shard_map/ppermute | solution.py:460
  29.2 1.9 %collective-permute-start = (f32[64,128]{1,0:T(8,128)}, f32[64,128]{1,0:T(8,128)S(1)}, u32[]{:S(2)}, u32[]{:S(2)}) collective-permute-start(f32[64,128]{1,0:T(8,128)} %get-tuple-element.8), channel_id=1, source_target_pairs={{0,32},{32,0},{64,96},{96,64},{128,160},{160,128},{192,224},{224,1... | collective-permute-start | bytes 98312 | tf_op jit(solution)/shard_map/ppermute | solution.py:459
  31.2 0.6 pad_add_fusion.which_ref
  31.7 0.0 copy-start.7
  31.7 0.0 copy-start.6
  31.7 0.4 collective-permute-done.1.far_ref.f
  32.2 0.0 copy-start.4
  32.2 1.9 %collective-permute-done.near_ref.n = f32[64,128]{1,0:T(8,128)S(1)} collective-permute-done((f32[64,128]{1,0:T(8,128)}, f32[64,128]{1,0:T(8,128)S(1)}, u32[]{:S(2)}, u32[]{:S(2)}) %collective-permute-start) | collective-permute-done | bytes 32800 | tf_op jit(solution)/shard_map/ppermute | solution.py:459
  34.1 0.0 copy-start.5
  34.1 0.0 all-to-all-done.r_ref
  34.1 0.0 copy-done.4
  34.1 0.6 copy-done.5
  34.7 0.0 copy-start.1
  34.7 0.7 copy-done.1
  35.4 3.0 %filtered.1.token_ref = f32[576,128]{1,0:T(8,128)} custom-call(s32[2]{0:T(128)} %pad_add_fusion.which_ref, s32[2]{0:T(128)} %pad_add_fusion.1.odd_ref, f32[32,16,128]{2,1,0:T(8,128)} %copy-done.1, bf16[9,256,256]{2,1,0:T(8,128)(2,1)} %constant.47.clone.wh_ref.hh_ref, bf16[9,256,256]{2,1,0:T(8,128)(2,1)} %constant.48.clone.wl_ref.hl_ref, ...), custom_call_target="tpu_custom_call" | custom-call | flops 100663296 | bytes 1200000 | tf_op jit(solution)/shard_map/filtered/pallas_call | solution.py:295
  38.4 13.6 %all-to-all-start.1 = ((f32[32,9,2,128]{3,2,1,0:T(2,128)}), f32[32,9,2,128]{3,2,1,0:T(2,128)S(1)}, u32[]{:S(2)}, u32[]{:S(2)}) async-start(f32[32,9,2,128]{3,2,1,0:T(2,128)} %bitcast.7), calls=%async_computation.1 | async-start | bytes 589824 | tf_op jit(solution)/shard_map/all_to_all | solution.py:465
  52.1 0.0 copy-done.7
  52.1 2.3 %collective-permute-start.2 = (f32[5,64,128]{2,1,0:T(8,128)S(1)}, f32[5,64,128]{2,1,0:T(8,128)S(1)}, u32[]{:S(2)}, u32[]{:S(2)}) collective-permute-start(f32[5,64,128]{2,1,0:T(8,128)S(1)} %copy-done.7), channel_id=1, source_target_pairs={{0,1},{1,0},{2,3},{3,2},{4,5},{5,4},{6,7},{7,6},{8,9},{9,8},{10,11... | collective-permute-start | bytes 491528 | tf_op jit(solution)/shard_map/ppermute | solution.py:461
  54.3 0.0 copy-done.6
  54.4 7.0 %collective-permute-start.3 = (f32[5,64,128]{2,1,0:T(8,128)S(1)}, f32[5,64,128]{2,1,0:T(8,128)S(1)}, u32[]{:S(2)}, u32[]{:S(2)}) collective-permute-start(f32[5,64,128]{2,1,0:T(8,128)S(1)} %copy-done.6), channel_id=1, source_target_pairs={{0,31},{1,2},{2,1},{3,4},{4,3},{5,6},{6,5},{7,8},{8,7},{9,10},{10,... | collective-permute-start | bytes 491528 | tf_op jit(solution)/shard_map/ppermute | solution.py:462
  61.4 0.0 collective-permute-done.2.s
  61.4 0.0 copy-start.2
  61.4 7.4 %collective-permute-done.3.b = f32[5,64,128]{2,1,0:T(8,128)S(1)} collective-permute-done((f32[5,64,128]{2,1,0:T(8,128)S(1)}, f32[5,64,128]{2,1,0:T(8,128)S(1)}, u32[]{:S(2)}, u32[]{:S(2)}) %collective-permute-start.3) | collective-permute-done | bytes 163872 | tf_op jit(solution)/shard_map/ppermute | solution.py:462
  68.8 0.0 copy-done.2
  68.8 0.0 copy-start.3
  68.8 0.7 copy-done.3
  69.5 5.0 %outer_part.1.rest_ref = f32[5,8,64,128]{3,2,1,0:T(8,128)} custom-call(s32[2]{0:T(128)} %pad_add_fusion.1.odd_ref, f32[8,64,128]{2,1,0:T(8,128)} %d.1, f32[3,8,64,128]{3,2,1,0:T(8,128)} %v.1, f32[8,64,128]{2,1,0:T(8,128)} %p.1, f32[5,64,128]{2,1,0:T(8,128)} %copy-done.2, f32[5,64,128]{2,1,0:T(8,128)} %copy-done.3, f32[64,128]{1,0:T(8,128)} %copy-done.5, ...), custom_call_target="tpu_custom_call" | custom-call | flops 16384000 | bytes 3000000 | tf_op jit(solution)/shard_map/outer_part/pallas_call | solution.py:369
  74.5 0.0 all-to-all-done.1
  74.5 0.0 copy-start
  74.5 0.7 copy-done
  75.2 2.1 %finish.1 = f32[5,8,64,128]{3,2,1,0:T(8,128)} custom-call(s32[1]{0:T(128)} %bitcast.place_ref, f32[576,128]{1,0:T(8,128)} %bitcast.8, f32[64,8,128]{2,1,0:T(8,128)} %constant.49.clone.w_ref, f32[5,8,64,128]{3,2,1,0:T(8,128)} %outer_part.1.rest_ref), custom_call_target="tpu_custom_call", output_to_operand_aliasing={{}: (3, {})} | custom-call | flops 409600 | bytes 800000 | tf_op jit(solution)/shard_map/finish/pallas_call | solution.py:430
Async XLA Ops:
  3.4 30.7 %all-to-all-start = ((f32[32,16,128]{2,1,0:T(8,128)}), f32[32,16,128]{2,1,0:T(8,128)S(1)}, u32[]{:S(2)}, u32[]{:S(2)}) async-start(f32[32,16,128]{2,1,0:T(8,128)} %inner_part.1), calls=%async_computation | async-start | bytes 524288 | tf_op jit(solution)/shard_map/all_to_all | solution.py:456
  22.1 10.1 %collective-permute-start.1 = (f32[64,128]{1,0:T(8,128)}, f32[64,128]{1,0:T(8,128)S(1)}, u32[]{:S(2)}, u32[]{:S(2)}) collective-permute-start(f32[64,128]{1,0:T(8,128)} %get-tuple-element.8), channel_id=1, source_target_pairs={{0,480},{32,64},{64,32},{96,128},{128,96},{160,192},{192,160},{224... | collective-permute-start | bytes 98312 | tf_op jit(solution)/shard_map/ppermute | solution.py:460
  29.2 4.9 %collective-permute-start = (f32[64,128]{1,0:T(8,128)}, f32[64,128]{1,0:T(8,128)S(1)}, u32[]{:S(2)}, u32[]{:S(2)}) collective-permute-start(f32[64,128]{1,0:T(8,128)} %get-tuple-element.8), channel_id=1, source_target_pairs={{0,32},{32,0},{64,96},{96,64},{128,160},{160,128},{192,224},{224,1... | collective-permute-start | bytes 98312 | tf_op jit(solution)/shard_map/ppermute | solution.py:459
  31.7 20.3 %copy-start.7 = (f32[5,64,128]{2,1,0:T(8,128)S(1)}, f32[5,64,128]{2,1,0:T(8,128)}, u32[]{:S(2)}) copy-start(f32[5,64,128]{2,1,0:T(8,128)} %get-tuple-element.9) | copy-start | bytes 491524
  31.7 22.6 %copy-start.6 = (f32[5,64,128]{2,1,0:T(8,128)S(1)}, f32[5,64,128]{2,1,0:T(8,128)}, u32[]{:S(2)}) copy-start(f32[5,64,128]{2,1,0:T(8,128)} %get-tuple-element.10) | copy-start | bytes 491524
  32.2 1.9 %copy-start.4 = (f32[64,128]{1,0:T(8,128)}, f32[64,128]{1,0:T(8,128)S(1)}, u32[]{:S(2)}) copy-start(f32[64,128]{1,0:T(8,128)S(1)} %collective-permute-done.1.far_ref.f) | copy-start | bytes 98308
  34.1 0.6 copy-start.5
  34.7 0.7 copy-start.1
  38.4 36.1 %all-to-all-start.1 = ((f32[32,9,2,128]{3,2,1,0:T(2,128)}), f32[32,9,2,128]{3,2,1,0:T(2,128)S(1)}, u32[]{:S(2)}, u32[]{:S(2)}) async-start(f32[32,9,2,128]{3,2,1,0:T(2,128)} %bitcast.7), calls=%async_computation.1 | async-start | bytes 589824 | tf_op jit(solution)/shard_map/all_to_all | solution.py:465
  52.1 9.3 %collective-permute-start.2 = (f32[5,64,128]{2,1,0:T(8,128)S(1)}, f32[5,64,128]{2,1,0:T(8,128)S(1)}, u32[]{:S(2)}, u32[]{:S(2)}) collective-permute-start(f32[5,64,128]{2,1,0:T(8,128)S(1)} %copy-done.7), channel_id=1, source_target_pairs={{0,1},{1,0},{2,3},{3,2},{4,5},{5,4},{6,7},{7,6},{8,9},{9,8},{10,11... | collective-permute-start | bytes 491528 | tf_op jit(solution)/shard_map/ppermute | solution.py:461
  54.4 14.5 %collective-permute-start.3 = (f32[5,64,128]{2,1,0:T(8,128)S(1)}, f32[5,64,128]{2,1,0:T(8,128)S(1)}, u32[]{:S(2)}, u32[]{:S(2)}) collective-permute-start(f32[5,64,128]{2,1,0:T(8,128)S(1)} %copy-done.6), channel_id=1, source_target_pairs={{0,31},{1,2},{2,1},{3,4},{4,3},{5,6},{6,5},{7,8},{8,7},{9,10},{10,... | collective-permute-start | bytes 491528 | tf_op jit(solution)/shard_map/ppermute | solution.py:462
  61.4 7.4 %copy-start.2 = (f32[5,64,128]{2,1,0:T(8,128)}, f32[5,64,128]{2,1,0:T(8,128)S(1)}, u32[]{:S(2)}) copy-start(f32[5,64,128]{2,1,0:T(8,128)S(1)} %collective-permute-done.2.s) | copy-start | bytes 491524
  68.8 0.7 copy-start.3
  74.5 0.7 copy-start

commit v2 on v1

v2 whole, which is shorter than its diff:
```python
import math

import jax
import jax.numpy as jnp
import ml_dtypes
import numpy as np
from jax import lax
from jax.experimental import pallas as pl
from jax.experimental.pallas import tpu as pltpu
from jax.sharding import PartitionSpec as P

NTH = 256
NR = 64
NF = 8
N_TH = 32
SECTOR = NTH // N_TH
LANES = 128
FIELDS = 5
SEND_ROWS = 20
BACK_ROWS = 12
SHARE = N_TH * FIELDS

HALF_STEP = 0.125
SMOOTH = 0.05


def theta_factor(cycle):
    return 0.25 / (2.0 * (2.0 * math.pi / NTH) * (cycle + 0.5))


def filter_rows():
    modes = np.arange(NTH)
    folded = np.minimum(modes, NTH - modes)
    waves = np.cos(2.0 * math.pi * (modes[:, None] * modes[None, :] % NTH) / NTH)
    rows = []
    for cycle in range(NF):
        keep = 2 * (NF + 1) * folded <= NTH * (cycle + 1)
        rows.append(waves[:, keep].sum(axis=1) / NTH)
    return np.stack(rows)


def filter_matrices():
    rows = filter_rows()
    index = (np.arange(NTH)[:, None] - np.arange(NTH)[None, :]) % NTH
    full = np.concatenate([rows[:, index], rows[:1, (index + NTH // 2) % NTH]]).astype(np.float32)
    high = full.astype(ml_dtypes.bfloat16)
    low = (full - high.astype(np.float32)).astype(ml_dtypes.bfloat16)
    return high, low


def edge_weights():
    rows = filter_rows()
    table = np.zeros((2 * N_TH, SECTOR, LANES), np.float32)
    for row in range(2 * N_TH - 1):
        apart = (N_TH - 1 - row) * SECTOR
        index = (apart + np.arange(SECTOR)[:, None] - np.arange(SECTOR)[None, :]) % NTH
        block = np.repeat(rows[:, index].transpose(1, 0, 2)[..., None], 2, axis=3)
        table[row] = block.reshape(SECTOR, LANES)
    return table


def conserved(fields):
    rho, ur, ut, uz, p = fields
    qr, qt, qz = rho * ur, rho * ut, rho * uz
    energy = p * 2.5 + 0.5 * (qr * ur + qt * ut + qz * uz)
    return rho, qr, qt, qz, energy


def flux(fields, q, direction):
    p = fields[4]
    speed = fields[1 + direction]
    moving = q[1 + direction]
    parts = [moving, moving * fields[1], moving * fields[2], moving * fields[3], speed * (q[4] + p)]
    parts[1 + direction] = parts[1 + direction] + p
    return parts


def lanes_of(shape):
    return lax.broadcasted_iota(jnp.int32, shape, len(shape) - 1)


def rows_of(shape):
    return lax.broadcasted_iota(jnp.int32, shape, len(shape) - 2)


def spread(value, shift, axis):
    size = value.shape[axis]
    return pltpu.roll(value, shift % size, axis)


def half_packs(tile):
    turned = spread(tile, 64, 1)
    low = lanes_of((SECTOR, LANES)) < 64
    first = jnp.where(low, tile, spread(turned, 4, 0))
    second = jnp.where(low, turned, spread(tile, 4, 0))
    return first[:4], second[:4]


def inner_kernel(d_ref, v_ref, p_ref, out_ref):
    def load(cycle):
        return (
            d_ref[:, cycle, :],
            v_ref[0, :, cycle, :],
            v_ref[1, :, cycle, :],
            v_ref[2, :, cycle, :],
            p_ref[:, cycle, :],
        )

    def store(unit, row, value):
        start = unit * SEND_ROWS + row
        out_ref[start : start + value.shape[0], :] = value

    shape = (SECTOR, LANES)
    lane, row = lanes_of(shape), rows_of(shape)
    first_lane, last_lane = lane == 0, lane == LANES - 1
    not_first_row, not_last_row = row > 0, row < SECTOR - 1
    low = lanes_of((1, LANES)) < 64
    for unit in range(16, N_TH):
        store(unit, 9, jnp.zeros((5, LANES), jnp.float32))

    before = None
    fields = load(0)
    q = conserved(fields)
    radial = flux(fields, q, 0)
    for f in range(FIELDS):
        sign = -1.0 if f in (1, 2) else 1.0
        mirrored = sign * (SMOOTH * q[f] + HALF_STEP * radial[f])
        for half, pack in enumerate(half_packs(mirrored)):
            store(16 + 2 * f + half, 10, pack)
    border = [jnp.zeros(shape, jnp.float32) for _ in range(FIELDS)]
    for cycle in range(NF):
        after_fields = load(cycle + 1)
        after_q = conserved(after_fields)
        after = (after_q, flux(after_fields, after_q, 0))
        around = flux(fields, q, 1)
        along = flux(fields, q, 2)
        c = theta_factor(cycle)
        radius = cycle + 0.5
        scale = 0.25 / radius
        sources = (
            None,
            scale * (q[2] * fields[2] + fields[4]),
            -scale * (q[1] * fields[2]),
            None,
            None,
        )
        for f in range(FIELDS):
            own = q[f] * (0.8 - 0.8 * c)
            if sources[f] is not None:
                own = own + sources[f]
            smooth, push = SMOOTH * q[f], HALF_STEP * along[f]
            forward, backward = spread(smooth + push, 1, 1), spread(smooth - push, -1, 1)
            own = own + jnp.where(first_lane, 0.0, forward) + jnp.where(last_lane, 0.0, backward)
            beyond = jnp.where(first_lane, forward, jnp.where(last_lane, backward, 0.0))
            border[f] = border[f] + spread(beyond, 16 * cycle + 1, 1)
            smooth, push = (0.4 * c) * q[f], c * around[f]
            rising, falling = smooth + push, smooth - push
            own = own + jnp.where(not_first_row, spread(rising, 1, 0), 0.0)
            own = own + jnp.where(not_last_row, spread(falling, -1, 0), 0.0)
            own = own + (SMOOTH * after[0][f] - (HALF_STEP * (radius + 1.0) / radius) * after[1][f])
            if before is not None:
                own = own + (SMOOTH * before[0][f] + (HALF_STEP * (radius - 1.0) / radius) * before[1][f])
            up, down = rising[7:8], falling[0:1]
            if f < 4:
                unit = f * NF + cycle
                store(unit, 0, own)
                store(unit, 8, up)
                store(unit, 15, down)
            else:
                packs = half_packs(own)
                store(cycle, 10, packs[0])
                store(cycle, 9, jnp.where(low, down, spread(up, 64, 1)))
                store(NF + cycle, 10, packs[1])
                store(NF + cycle, 9, jnp.where(low, spread(down, 64, 1), up))
        before = (q, radial)
        fields, q, radial = after_fields, after_q, after[1]
    rows = [
        jnp.sum(pltpu.roll(value, 0, 1, stride=2, stride_axis=0), axis=0, keepdims=True) for value in border
    ]
    others = jnp.concatenate(rows[1:], axis=0)
    for unit in range(N_TH):
        store(unit, 14, rows[0])
        store(unit, 16, others)


def in_vmem(value):
    return pltpu.with_memory_space_constraint(value, pltpu.VMEM)


def in_hbm(value):
    return pltpu.with_memory_space_constraint(value, pltpu.HBM)


PARAMS = pltpu.CompilerParams(vmem_limit_bytes=24 << 20)
WHOLE = pl.BlockSpec(memory_space=pltpu.VMEM)
SCALARS = pl.BlockSpec(memory_space=pltpu.SMEM)


def inner_part(density, velocity, pressure):
    return pl.pallas_call(
        inner_kernel,
        grid=(1,),
        in_specs=[
            pl.BlockSpec((SECTOR, 16, LANES), lambda i: (0, 0, 0)),
            pl.BlockSpec((3, SECTOR, 16, LANES), lambda i: (0, 0, 0, 0)),
            pl.BlockSpec((SECTOR, 16, LANES), lambda i: (0, 0, 0)),
        ],
        out_specs=WHOLE,
        out_shape=pltpu.VMEM((N_TH * SEND_ROWS, LANES), jnp.float32),
        compiler_params=PARAMS,
        cost_estimate=pl.CostEstimate(flops=8 * 1024 * 200, bytes_accessed=600_000, transcendentals=0),
        name="inner_part",
    )(in_hbm(density), in_hbm(velocity), in_hbm(pressure))


def edge_kernel(odd_ref, high_ref, low_ref, d_ref, v_ref, p_ref, near_ref, far_ref, columns_ref, w_ref, done):
    copies = [
        pltpu.make_async_copy(table.at[odd_ref[1 + k]], w_ref.at[2 * k + n], done.at[2 * k + n])
        for k in range(2)
        for n, table in enumerate((high_ref, low_ref))
    ]
    for copy in copies:
        copy.start()
    lane = lanes_of((NR, LANES))
    odd = odd_ref[0] == 1

    def load(f, j):
        return d_ref[j] if f == 0 else (p_ref[j] if f == 4 else v_ref[f - 1, j])

    total = jnp.zeros((NR, LANES), jnp.float32)
    for f in range(FIELDS):
        for j in range(SECTOR):
            spot = 16 * f + 2 * j + 1
            total = jnp.where((lane == spot) | (lane == spot + 1), spread(load(f, j), spot + 1, 1), total)
        first, last = load(f, 0), load(f, SECTOR - 1)
        near_ref[f] = jnp.where(odd, first, last)
        far_ref[f] = jnp.where(odd, last, first)
    columns_ref[...] = total
    for copy in copies:
        copy.wait()


def edges(which, high, low, density, velocity, pressure):
    rows = pltpu.VMEM((FIELDS, NR, LANES), jnp.float32)
    return pl.pallas_call(
        edge_kernel,
        in_specs=[SCALARS] + [pl.BlockSpec(memory_space=pl.ANY)] * 2 + [WHOLE] * 3,
        out_specs=[WHOLE] * 4,
        out_shape=[
            rows,
            rows,
            pltpu.VMEM((NR, LANES), jnp.float32),
            pltpu.VMEM((4, NTH, NTH), jnp.bfloat16),
        ],
        scratch_shapes=[pltpu.SemaphoreType.DMA((4,))],
        compiler_params=PARAMS,
        cost_estimate=pl.CostEstimate(flops=320 * 1024 * 3, bytes_accessed=1_800_000, transcendentals=0),
        name="edges",
    )(which, in_hbm(high), in_hbm(low), in_vmem(density), in_vmem(velocity), in_vmem(pressure))


def axial_terms(before, after):
    lane = lanes_of(before.shape)
    both = jnp.where(lane % 2 == 1, before, spread(after, -2, 1))
    fields = [both] + [spread(both, -16 * f, 1) for f in range(1, FIELDS)]
    q = conserved(fields)
    along = flux(fields, q, 2)
    push = jnp.where(lane % 2 == 1, HALF_STEP, -HALF_STEP)
    return [SMOOTH * q[f] + push * along[f] for f in range(FIELDS)]


def filter_kernel(r_ref, w_ref, columns_ref, out_ref, share_ref):
    shape = (N_TH, SECTOR, LANES)
    row, lane = rows_of(shape), lanes_of(shape)
    starts = [s * SEND_ROWS for s in range(N_TH)]
    main = jnp.stack([r_ref[a : a + 8, :] for a in starts])
    extra = jnp.stack([r_ref[a + 8 : a + 16, :] for a in starts])
    zero = jnp.zeros(shape, jnp.float32)

    def earlier(value):
        return jnp.concatenate([value[-1:], value[:-1]], axis=0)

    def later(value):
        return jnp.concatenate([value[1:], value[:1]], axis=0)

    main = main + jnp.where(row == 0, earlier(extra), jnp.where(row == 7, later(extra), zero))
    turned = spread(extra, 64, 2)
    top = spread(extra, 6, 1)
    half = jnp.where(row < 4, top, spread(turned, 2, 1))
    half = half + jnp.where(
        row == 0, earlier(spread(turned, 7, 1)), jnp.where(row == 7, later(top), zero)
    )

    def product(high, low, value):
        value = value.reshape(NTH, LANES)
        big = value.astype(jnp.bfloat16)
        small = (value - big.astype(jnp.float32)).astype(jnp.bfloat16)
        out = jnp.dot(high, big, preferred_element_type=jnp.float32)
        out = out + jnp.dot(high, small, preferred_element_type=jnp.float32)
        out = out + jnp.dot(low, big, preferred_element_type=jnp.float32)
        return out.reshape(shape)

    main = product(w_ref[0], w_ref[1], main)
    half = product(w_ref[2], w_ref[3], half)
    packed = jnp.where(lane < 64, half, spread(spread(half, 64, 2), 4, 1))
    for s in range(N_TH):
        base, start = s * BACK_ROWS, s * SEND_ROWS
        out_ref[base : base + 8, :] = main[s]
        out_ref[base + 8 : base + 12, :] = packed[s, :4]
        share_ref[5 * s : 5 * s + 1, :] = r_ref[start + 14 : start + 15, :]
        share_ref[5 * s + 1 : 5 * s + 5, :] = r_ref[start + 16 : start + 20, :]
    share_ref[SHARE:, :] = columns_ref[...]


def filtered(received, matrices, columns):
    return pl.pallas_call(
        filter_kernel,
        in_specs=[WHOLE] * 3,
        out_specs=[WHOLE] * 2,
        out_shape=[
            pltpu.VMEM((N_TH * BACK_ROWS, LANES), jnp.float32),
            pltpu.VMEM((SHARE + NR, LANES), jnp.float32),
        ],
        compiler_params=PARAMS,
        cost_estimate=pl.CostEstimate(flops=6 * 256 * 256 * 256, bytes_accessed=1_200_000, transcendentals=0),
        name="filtered",
    )(in_vmem(received), in_vmem(matrices), in_vmem(columns))


def outer_kernel(odd_ref, d_ref, v_ref, p_ref, side_ref, back_ref, token_ref, out_ref):
    del token_ref
    th_odd = odd_ref[0] == 1
    shape = (NR, LANES)
    lane, row = lanes_of(shape), rows_of(shape)
    radius = row.astype(jnp.float32) + 0.5
    inverse = 1.0 / radius
    c = (theta_factor(0) * 0.5) * inverse

    def load(j):
        return (d_ref[j], v_ref[0, j], v_ref[1, j], v_ref[2, j], p_ref[j])

    def step(j, carry):
        fields = load(j)
        below = load(jnp.maximum(j - 1, 0))
        above = load(jnp.minimum(j + 1, SECTOR - 1))
        use_low, use_high = j == 0, j == SECTOR - 1
        below = [
            jnp.where(use_low, jnp.where(th_odd, side_ref[f], back_ref[f]), below[f]) for f in range(FIELDS)
        ]
        above = [
            jnp.where(use_high, jnp.where(th_odd, back_ref[f], side_ref[f]), above[f]) for f in range(FIELDS)
        ]
        q = conserved(fields)
        radial = flux(fields, q, 0)
        along = flux(fields, q, 2)
        q_low, q_high = conserved(below), conserved(above)
        f_low, f_high = flux(below, q_low, 1), flux(above, q_high, 1)
        scale = 0.25 * inverse
        sources = (
            None,
            scale * (q[2] * fields[2] + fields[4]),
            -scale * (q[1] * fields[2]),
            None,
            None,
        )
        for f in range(FIELDS):
            own = q[f] * (0.8 - 0.8 * c)
            if sources[f] is not None:
                own = own + sources[f]
            smooth, push = SMOOTH * q[f], HALF_STEP * along[f]
            own = own + jnp.where(lane == 0, 0.0, spread(smooth + push, 1, 1))
            own = own + jnp.where(lane == LANES - 1, 0.0, spread(smooth - push, LANES - 1, 1))
            own = own + c * (0.4 * (q_low[f] + q_high[f]) + (f_low[f] - f_high[f]))
            push = (HALF_STEP * radius) * radial[f]
            smooth_ahead = jnp.where(row == NR - 1, smooth, spread(smooth, NR - 1, 0))
            push_ahead = jnp.where(row == NR - 1, push + HALF_STEP * radial[f], spread(push, NR - 1, 0))
            own = own + (smooth_ahead + spread(smooth, 1, 0))
            own = own + inverse * (spread(push, 1, 0) - push_ahead)
            out_ref[f, j] = own
        return carry

    lax.fori_loop(0, SECTOR, step, 0)


def outer_part(odd, density, velocity, pressure, side, back, token):
    return pl.pallas_call(
        outer_kernel,
        in_specs=[SCALARS] + [WHOLE] * 5 + [pl.BlockSpec(memory_space=pl.ANY)],
        out_specs=WHOLE,
        out_shape=pltpu.VMEM((FIELDS, SECTOR, NR, LANES), jnp.float32),
        compiler_params=PARAMS,
        cost_estimate=pl.CostEstimate(flops=64 * 1024 * 250, bytes_accessed=3_000_000, transcendentals=0),
        name="outer_part",
    )(odd, density, velocity, pressure, in_vmem(side), in_vmem(back), token)


def finish_kernel(place_ref, r_ref, w_ref, near_ref, far_ref, rest_ref, out_ref, buffer, border, done):
    start = N_TH - 1 - place_ref[0]
    odd = place_ref[1] == 1
    near, far = near_ref[...], far_ref[...]
    before, after = jnp.where(odd, near, far), jnp.where(odd, far, near)
    border[...] = jnp.where(lanes_of((SHARE, LANES)) % 2 == 1, before[:SHARE], after[:SHARE])
    terms = axial_terms(before[SHARE + NF :], after[SHARE + NF :])
    shape = (SECTOR, LANES)
    lane = lanes_of(shape)
    ends = (lane == 0) | (lane == LANES - 1)
    low_half = lanes_of((4, LANES)) < 64
    far_lane = lanes_of((NR - NF, LANES))
    far_ends = (far_lane == 0) | (far_lane == LANES - 1)

    def outer(j):
        rows = pl.ds(NF, NR - NF)
        return pltpu.make_async_copy(buffer.at[:, j, rows, :], out_ref.at[:, j, rows, :], done.at[j])

    for j in range(SECTOR):
        for f in range(FIELDS):
            side = spread(terms[f], LANES - 1 - 2 * j, 1)
            buffer[f, j, NF:, :] = rest_ref[f, j, NF:, :] + jnp.where(far_ends, side, 0.0)
        outer(j).start()

    sums = [jnp.zeros(shape, jnp.float32) for _ in range(FIELDS)]
    for t in range(N_TH):
        weights = w_ref[start + t]
        for f in range(FIELDS):
            sums[f] = sums[f] + weights * border[5 * t + f : 5 * t + f + 1, :]
    for f in range(FIELDS):
        for shift in (2, 4, 8):
            sums[f] = sums[f] + spread(sums[f], -shift, 1)

    def joined(unit_a, unit_b):
        a = r_ref[unit_a * BACK_ROWS + 8 : unit_a * BACK_ROWS + 12, :]
        b = r_ref[unit_b * BACK_ROWS + 8 : unit_b * BACK_ROWS + 12, :]
        top = jnp.where(low_half, a, spread(b, 64, 1))
        bottom = jnp.where(low_half, spread(a, 64, 1), b)
        return jnp.concatenate([top, bottom], axis=0)

    for f in range(FIELDS):
        for cycle in range(NF):
            if f < 4:
                unit = (f * NF + cycle) * BACK_ROWS
                tile = r_ref[unit : unit + 8, :]
            else:
                tile = joined(cycle, NF + cycle)
            if cycle == 0:
                tile = tile + joined(16 + 2 * f, 17 + 2 * f)
            tile = tile + jnp.where(ends, spread(sums[f], -(16 * cycle + 1), 1), 0.0)
            buffer[f, :, cycle, :] = tile
    rows = pl.ds(0, NF)
    inner = pltpu.make_async_copy(buffer.at[:, :, rows, :], out_ref.at[:, :, rows, :], done.at[SECTOR])
    inner.start()
    for j in range(SECTOR):
        outer(j).wait()
    inner.wait()


def finish(place, received, weights, near, far, rest):
    block = (FIELDS, SECTOR, NR, LANES)
    return pl.pallas_call(
        finish_kernel,
        in_specs=[SCALARS] + [WHOLE] * 5,
        out_specs=pl.BlockSpec(memory_space=pl.ANY),
        out_shape=jax.ShapeDtypeStruct(block, jnp.float32),
        scratch_shapes=[
            pltpu.VMEM(block, jnp.float32),
            pltpu.VMEM((SHARE, LANES), jnp.float32),
            pltpu.SemaphoreType.DMA((SECTOR + 1,)),
        ],
        compiler_params=PARAMS,
        cost_estimate=pl.CostEstimate(flops=400 * 1024, bytes_accessed=3_000_000, transcendentals=0),
        name="finish",
    )(place, in_vmem(received), in_vmem(weights), in_vmem(near), in_vmem(far), in_vmem(rest))


def pairs(size, offset):
    return [(i, (((i - offset) ^ 1) + offset) % size) for i in range(size)]


def transposed(value, rows):
    value = value.reshape(N_TH, rows // 4, 4, LANES)
    return lax.all_to_all(value, "th", 0, 0, tiled=True).reshape(N_TH * rows, LANES)


def per_device(density, velocity, pressure):
    high, low = filter_matrices()
    high, low = jnp.asarray(high), jnp.asarray(low)
    weights = jnp.asarray(edge_weights())
    th, gz = lax.axis_index("th"), lax.axis_index("gz")
    main = th % NF
    half = jnp.where(th < 16, main, jnp.where(th < 26, NF, 0))
    which = jnp.stack([th % 2, main, half]).astype(jnp.int32)
    place = jnp.stack([th, gz % 2]).astype(jnp.int32)

    sent = inner_part(density, velocity, pressure)
    received = transposed(sent, SEND_ROWS)

    near_row, far_row, columns, matrices = edges(which, high, low, density, velocity, pressure)
    th_far = lax.ppermute(far_row, "th", pairs(N_TH, 1))
    th_near = lax.ppermute(near_row, "th", pairs(N_TH, 0))

    back, share = filtered(received, matrices, columns)
    back, th_far, th_near = lax.optimization_barrier((back, th_far, th_near))
    returned = transposed(back, BACK_ROWS)
    gz_size = lax.axis_size("gz")
    gz_far = lax.ppermute(share, "gz", pairs(gz_size, 1))
    gz_near = lax.ppermute(share, "gz", pairs(gz_size, 0))
    rest = outer_part(which, density, velocity, pressure, th_near, th_far, share)
    return finish(place, returned, weights, gz_near, gz_far, rest)


def solution(mesh):
    in_specs = (P("th", None, "gz"), P(None, "th", None, "gz"), P("th", None, "gz"))
    out_specs = P(None, "th", None, "gz")
    return jax.shard_map(
        per_device, mesh=mesh, in_specs=in_specs, out_specs=out_specs, check_vma=False
    )
```

time: 77.8 us -> 64 us (0.82)
  the two profiles are of different devices: /device:TPU:57 before, /device:TPU:1 now
where the time goes in v2:
time: 64 us; the launch traced here: 63.6 us
  starting transfers between devices  43.8 us (68%)
  Pallas kernels  12.1 us (19%)
  waiting for transfers between devices  7.42 us (12%)
    all_to_all x2, starting transfers between devices, transposed(): lax.all_to_all(value, 'th', 0, 0, tiled=True).reshape(N_TH * rows, LANES)  23.9 us
    ppermute x1, starting transfers between devices, per_device(): th_near = lax.ppermute(near_row, 'th', pairs(N_TH, 0))  8.16 us
    ppermute x1, starting transfers between devices, per_device(): gz_far = lax.ppermute(share, 'gz', pairs(gz_size, 1))  6.32 us
    all_to_all x2, waiting for transfers between devices, transposed(): lax.all_to_all(value, 'th', 0, 0, tiled=True).reshape(N_TH * rows, LANES)  4.22 us
    pallas_call x1, Pallas kernels, inner_part(): pl.pallas_call(inner_kernel, grid=(1,), in_specs=[pl.BlockSpec((SECTOR, 1...  3.55 us
    ppermute x1, starting transfers between devices, per_device(): th_far = lax.ppermute(far_row, 'th', pairs(N_TH, 1))  3.54 us
    pallas_call x1, Pallas kernels, outer_part(): pl.pallas_call(outer_kernel, in_specs=[SCALARS] + [WHOLE] * 5 + [pl.Block...  2.92 us
    pallas_call x1, Pallas kernels, finish(): pl.pallas_call(finish_kernel, in_specs=[SCALARS] + [WHOLE] * 5, out_specs...  2.51 us
  transfers between devices with their start and end apart: 6, of which 3 were waited for; matrix products, arithmetic and copies ran while one was open for 0% of the time, Pallas kernels for 10%

profile of v2, /device:TPU:1, one launch (start us, length us, event | category | flops | bytes accessed | tf_op | source)
XLA Modules:
  0.0 63.6 jit_solution(3790953718181124102)
XLA Ops:
  0.0 0.0 copy-start.2
  0.0 0.0 copy-start
  0.0 0.0 copy-start.1
  0.0 3.5 %inner_part.1 = f32[640,128]{1,0:T(8,128)} custom-call(f32[8,64,128]{2,1,0:T(8,128)} %d_ref.5, f32[3,8,64,128]{3,2,1,0:T(8,128)} %v_ref.5, f32[8,64,128]{2,1,0:T(8,128)} %p_ref.5), custom_call_target="tpu_custom_call" | custom-call | flops 1638400 | bytes 600000 | tf_op jit(solution)/shard_map/inner_part/pallas_call | solution.py:200
  3.6 17.2 %all-to-all-start = ((f32[32,5,4,128]{3,2,1,0:T(4,128)}), f32[32,5,4,128]{3,2,1,0:T(4,128)S(1)}, u32[]{:S(2)}, u32[]{:S(2)}) async-start(f32[32,5,4,128]{3,2,1,0:T(4,128)} %bitcast.2), calls=%async_computation | async-start | bytes 655360 | tf_op jit(solution)/shard_map/all_to_all | solution.py:480
  20.8 0.1 pad_add_fusion.1.odd_ref
  20.9 0.0 copy-done.2
  20.9 0.0 copy-done
  20.9 0.0 copy-done.1
  20.9 2.0 %edges.1 = (f32[5,64,128]{2,1,0:T(8,128)S(1)}, f32[5,64,128]{2,1,0:T(8,128)S(1)}, f32[64,128]{1,0:T(8,128)S(1)}, bf16[4,256,256]{2,1,0:T(8,128)(2,1)S(1)}) custom-call(s32[3]{0:T(128)S(1)} %pad_add_fusion.1.odd_ref, bf16[9,256,256]{2,1,0:T(8,128)(2,1)} %constant.47.clone.high_ref, bf16[9,256,256]{2,1,0:T(8,128)(2,1)} %constant.48.clone.low_ref, ...), custom_call_target="tpu_custom_call" | custom-call | flops 983040 | bytes 1800000 | tf_op jit(solution)/shard_map/edges/pallas_call | solution.py:245
  22.9 3.5 %collective-permute-start = (f32[5,64,128]{2,1,0:T(8,128)S(1)}, f32[5,64,128]{2,1,0:T(8,128)S(1)}, u32[]{:S(2)}, u32[]{:S(2)}) collective-permute-start(f32[5,64,128]{2,1,0:T(8,128)S(1)} %get-tuple-element.17), channel_id=1, source_target_pairs={{0,31},{1,2},{2,1},{3,4},{4,3},{5,6},{6,5},{7,8},{8,7},{9,10},{10,... | collective-permute-start | bytes 491528 | tf_op jit(solution)/shard_map/ppermute | solution.py:497
  26.4 8.2 %collective-permute-start.1 = (f32[5,64,128]{2,1,0:T(8,128)S(1)}, f32[5,64,128]{2,1,0:T(8,128)S(1)}, u32[]{:S(2)}, u32[]{:S(2)}) collective-permute-start(f32[5,64,128]{2,1,0:T(8,128)S(1)} %get-tuple-element.18), channel_id=1, source_target_pairs={{0,1},{1,0},{2,3},{3,2},{4,5},{5,4},{6,7},{7,6},{8,9},{9,8},{10,11... | collective-permute-start | bytes 491528 | tf_op jit(solution)/shard_map/ppermute | solution.py:498
  34.6 4.2 %all-to-all-done = f32[32,5,4,128]{3,2,1,0:T(4,128)S(1)} async-done(((f32[32,5,4,128]{3,2,1,0:T(4,128)}), f32[32,5,4,128]{3,2,1,0:T(4,128)S(1)}, u32[]{:S(2)}, u32[]{:S(2)}) %all-to-all-start) | async-done | bytes 327712 | tf_op jit(solution)/shard_map/all_to_all | solution.py:480
  38.8 1.1 %filtered.1 = (f32[384,128]{1,0:T(8,128)}, f32[224,128]{1,0:T(8,128)S(1)}) custom-call(f32[640,128]{1,0:T(8,128)S(1)} %bitcast.9, bf16[4,256,256]{2,1,0:T(8,128)(2,1)S(1)} %get-tuple-element.14.w_ref, f32[64,128]{1,0:T(8,128)S(1)} %get-tuple-element.15.columns_ref), custom_call_target="tpu_custom_call" | custom-call | flops 100663296 | bytes 1200000 | tf_op jit(solution)/shard_map/filtered/pallas_call | solution.py:316
  40.0 0.0 collective-permute-done.back_ref
  40.0 0.0 collective-permute-done.1.side_ref
  40.0 6.7 %all-to-all-start.1 = ((f32[32,3,4,128]{3,2,1,0:T(4,128)}), f32[32,3,4,128]{3,2,1,0:T(4,128)S(1)}, u32[]{:S(2)}, u32[]{:S(2)}) async-start(f32[32,3,4,128]{3,2,1,0:T(4,128)} %bitcast.7), calls=%async_computation.1 | async-start | bytes 393216 | tf_op jit(solution)/shard_map/all_to_all | solution.py:480
  46.6 6.3 %collective-permute-start.3 = (f32[224,128]{1,0:T(8,128)S(1)}, f32[224,128]{1,0:T(8,128)}, u32[]{:S(2)}, u32[]{:S(2)}) collective-permute-start(f32[224,128]{1,0:T(8,128)S(1)} %get-tuple-element.20.token_ref), channel_id=1, source_target_pairs={{0,480},{32,64},{64,32},{96,128},{128,96},{160,192},{192,160},{224... | collective-permute-start | bytes 344072 | tf_op jit(solution)/shard_map/ppermute | solution.py:504
  53.0 1.9 %collective-permute-start.2 = (f32[224,128]{1,0:T(8,128)S(1)}, f32[224,128]{1,0:T(8,128)}, u32[]{:S(2)}, u32[]{:S(2)}) collective-permute-start(f32[224,128]{1,0:T(8,128)S(1)} %get-tuple-element.20.token_ref), channel_id=1, source_target_pairs={{0,32},{32,0},{64,96},{96,64},{128,160},{160,128},{192,224},{224,1... | collective-permute-start | bytes 344072 | tf_op jit(solution)/shard_map/ppermute | solution.py:505
  54.9 0.1 pad_add_fusion.place_ref
  55.0 0.0 copy-start.3
  55.0 2.9 %outer_part.1.rest_ref = f32[5,8,64,128]{3,2,1,0:T(8,128)S(1)} custom-call(s32[3]{0:T(128)S(1)} %pad_add_fusion.1.odd_ref, f32[8,64,128]{2,1,0:T(8,128)S(1)} %copy-done.1, f32[3,8,64,128]{3,2,1,0:T(8,128)S(1)} %copy-done, f32[8,64,128]{2,1,0:T(8,128)S(1)} %copy-done.2, f32[5,64,128]{2,1,0:T(8,128)S(1)} %collective-permute-done.1.side_ref, ...), custom_call_target="tpu_custom_call" | custom-call | flops 16384000 | bytes 3000000 | tf_op jit(solution)/shard_map/outer_part/pallas_call | solution.py:386
  57.9 2.4 %collective-permute-done.3.far_ref = f32[224,128]{1,0:T(8,128)} collective-permute-done((f32[224,128]{1,0:T(8,128)S(1)}, f32[224,128]{1,0:T(8,128)}, u32[]{:S(2)}, u32[]{:S(2)}) %collective-permute-start.3) | collective-permute-done | bytes 114720 | tf_op jit(solution)/shard_map/ppermute | solution.py:504
  60.3 0.8 %collective-permute-done.2.near_ref = f32[224,128]{1,0:T(8,128)} collective-permute-done((f32[224,128]{1,0:T(8,128)S(1)}, f32[224,128]{1,0:T(8,128)}, u32[]{:S(2)}, u32[]{:S(2)}) %collective-permute-start.2) | collective-permute-done | bytes 114720 | tf_op jit(solution)/shard_map/ppermute | solution.py:505
  61.1 0.0 all-to-all-done.1
  61.1 0.0 copy-done.3
  61.1 2.5 %finish.1 = f32[5,8,64,128]{3,2,1,0:T(8,128)} custom-call(s32[2]{0:T(128)S(1)} %pad_add_fusion.place_ref, f32[384,128]{1,0:T(8,128)S(1)} %bitcast.10, f32[64,8,128]{2,1,0:T(8,128)S(1)} %copy-done.3, f32[224,128]{1,0:T(8,128)} %collective-permute-done.2.near_ref, f32[224,128]{1,0:T(8,128)} %collective-permute-done.3.far_ref, ...), custom_call_target="tpu_custom_call" | custom-call | flops 409600 | bytes 3000000 | tf_op jit(solution)/shard_map/finish/pallas_call | solution.py:458
Async XLA Ops:
  0.0 20.9 %copy-start.2 = (f32[8,64,128]{2,1,0:T(8,128)S(1)}, f32[8,64,128]{2,1,0:T(8,128)}, u32[]{:S(2)}) copy-start(f32[8,64,128]{2,1,0:T(8,128)} %p_ref.5) | copy-start | bytes 786436
  0.0 20.9 %copy-start = (f32[3,8,64,128]{3,2,1,0:T(8,128)S(1)}, f32[3,8,64,128]{3,2,1,0:T(8,128)}, u32[]{:S(2)}) copy-start(f32[3,8,64,128]{3,2,1,0:T(8,128)} %v_ref.5) | copy-start | bytes 2359300
  0.0 20.9 %copy-start.1 = (f32[8,64,128]{2,1,0:T(8,128)S(1)}, f32[8,64,128]{2,1,0:T(8,128)}, u32[]{:S(2)}) copy-start(f32[8,64,128]{2,1,0:T(8,128)} %d_ref.5) | copy-start | bytes 786436
  3.6 35.3 %all-to-all-start = ((f32[32,5,4,128]{3,2,1,0:T(4,128)}), f32[32,5,4,128]{3,2,1,0:T(4,128)S(1)}, u32[]{:S(2)}, u32[]{:S(2)}) async-start(f32[32,5,4,128]{3,2,1,0:T(4,128)} %bitcast.2), calls=%async_computation | async-start | bytes 655360 | tf_op jit(solution)/shard_map/all_to_all | solution.py:480
  22.9 17.1 %collective-permute-start = (f32[5,64,128]{2,1,0:T(8,128)S(1)}, f32[5,64,128]{2,1,0:T(8,128)S(1)}, u32[]{:S(2)}, u32[]{:S(2)}) collective-permute-start(f32[5,64,128]{2,1,0:T(8,128)S(1)} %get-tuple-element.17), channel_id=1, source_target_pairs={{0,31},{1,2},{2,1},{3,4},{4,3},{5,6},{6,5},{7,8},{8,7},{9,10},{10,... | collective-permute-start | bytes 491528 | tf_op jit(solution)/shard_map/ppermute | solution.py:497
  26.4 13.5 %collective-permute-start.1 = (f32[5,64,128]{2,1,0:T(8,128)S(1)}, f32[5,64,128]{2,1,0:T(8,128)S(1)}, u32[]{:S(2)}, u32[]{:S(2)}) collective-permute-start(f32[5,64,128]{2,1,0:T(8,128)S(1)} %get-tuple-element.18), channel_id=1, source_target_pairs={{0,1},{1,0},{2,3},{3,2},{4,5},{5,4},{6,7},{7,6},{8,9},{9,8},{10,11... | collective-permute-start | bytes 491528 | tf_op jit(solution)/shard_map/ppermute | solution.py:498
  40.0 21.1 %all-to-all-start.1 = ((f32[32,3,4,128]{3,2,1,0:T(4,128)}), f32[32,3,4,128]{3,2,1,0:T(4,128)S(1)}, u32[]{:S(2)}, u32[]{:S(2)}) async-start(f32[32,3,4,128]{3,2,1,0:T(4,128)} %bitcast.7), calls=%async_computation.1 | async-start | bytes 393216 | tf_op jit(solution)/shard_map/all_to_all | solution.py:480
  46.6 13.6 %collective-permute-start.3 = (f32[224,128]{1,0:T(8,128)S(1)}, f32[224,128]{1,0:T(8,128)}, u32[]{:S(2)}, u32[]{:S(2)}) collective-permute-start(f32[224,128]{1,0:T(8,128)S(1)} %get-tuple-element.20.token_ref), channel_id=1, source_target_pairs={{0,480},{32,64},{64,32},{96,128},{128,96},{160,192},{192,160},{224... | collective-permute-start | bytes 344072 | tf_op jit(solution)/shard_map/ppermute | solution.py:504
  53.0 8.1 %collective-permute-start.2 = (f32[224,128]{1,0:T(8,128)S(1)}, f32[224,128]{1,0:T(8,128)}, u32[]{:S(2)}, u32[]{:S(2)}) collective-permute-start(f32[224,128]{1,0:T(8,128)S(1)} %get-tuple-element.20.token_ref), channel_id=1, source_target_pairs={{0,32},{32,0},{64,96},{96,64},{128,160},{160,128},{192,224},{224,1... | collective-permute-start | bytes 344072 | tf_op jit(solution)/shard_map/ppermute | solution.py:505
  55.0 6.1 %copy-start.3 = (f32[64,8,128]{2,1,0:T(8,128)S(1)}, f32[64,8,128]{2,1,0:T(8,128)}, u32[]{:S(2)}) copy-start(f32[64,8,128]{2,1,0:T(8,128)} %constant.49.clone.w_ref) | copy-start | bytes 786436

commit v3 on v2

--- a/solution.py
+++ b/solution.py
@@ -19,6 +19,13 @@
 SEND_ROWS = 20
 BACK_ROWS = 12
 SHARE = N_TH * FIELDS
+HALF_SHARE = SHARE // 2
+OUTER = NR - NF
+BLOCK_ROWS = FIELDS * SECTOR * OUTER
+PARITY_ROW = BLOCK_ROWS + N_TH * SECTOR
+REST_ROWS = PARITY_ROW + SECTOR
+FIRST = 24
+ROW_FIELDS = 10
 
 HALF_STEP = 0.125
 SMOOTH = 0.05
@@ -56,7 +63,7 @@
         index = (apart + np.arange(SECTOR)[:, None] - np.arange(SECTOR)[None, :]) % NTH
         block = np.repeat(rows[:, index].transpose(1, 0, 2)[..., None], 2, axis=3)
         table[row] = block.reshape(SECTOR, LANES)
-    return table
+    return table.reshape(2 * N_TH * SECTOR, LANES)
 
 
 def conserved(fields):
@@ -75,6 +82,10 @@
     return parts
 
 
+def slot(sector):
+    return (sector - FIRST) % N_TH
+
+
 def lanes_of(shape):
     return lax.broadcasted_iota(jnp.int32, shape, len(shape) - 1)
 
@@ -97,17 +108,19 @@
 
 
 def inner_kernel(d_ref, v_ref, p_ref, out_ref):
+    size = 16 * SECTOR
+    d_rows, v_rows, p_rows = (
+        d_ref.reshape(size, LANES), v_ref.reshape(3 * size, LANES), p_ref.reshape(size, LANES)
+    )
+
     def load(cycle):
-        return (
-            d_ref[:, cycle, :],
-            v_ref[0, :, cycle, :],
-            v_ref[1, :, cycle, :],
-            v_ref[2, :, cycle, :],
-            p_ref[:, cycle, :],
-        )
+        def rows(ref, first):
+            return ref[pl.ds(first + cycle, SECTOR, stride=16), :]
+
+        return (rows(d_rows, 0), *[rows(v_rows, n * size) for n in range(3)], rows(p_rows, 0))
 
     def store(unit, row, value):
-        start = unit * SEND_ROWS + row
+        start = slot(unit) * SEND_ROWS + row
         out_ref[start : start + value.shape[0], :] = value
 
     shape = (SECTOR, LANES)
@@ -213,55 +226,42 @@
     )(in_hbm(density), in_hbm(velocity), in_hbm(pressure))
 
 
-def edge_kernel(odd_ref, high_ref, low_ref, d_ref, v_ref, p_ref, near_ref, far_ref, columns_ref, w_ref, done):
-    copies = [
-        pltpu.make_async_copy(table.at[odd_ref[1 + k]], w_ref.at[2 * k + n], done.at[2 * k + n])
-        for k in range(2)
-        for n, table in enumerate((high_ref, low_ref))
-    ]
-    for copy in copies:
-        copy.start()
+def edge_kernel(which_ref, d_ref, v_ref, p_ref, near_ref, far_ref, columns_ref):
     lane = lanes_of((NR, LANES))
-    odd = odd_ref[0] == 1
+    odd = which_ref[0] == 1
 
     def load(f, j):
         return d_ref[j] if f == 0 else (p_ref[j] if f == 4 else v_ref[f - 1, j])
 
-    total = jnp.zeros((NR, LANES), jnp.float32)
+    firsts = jnp.zeros((NR, LANES), jnp.float32)
+    lasts = firsts
     for f in range(FIELDS):
         for j in range(SECTOR):
-            spot = 16 * f + 2 * j + 1
-            total = jnp.where((lane == spot) | (lane == spot + 1), spread(load(f, j), spot + 1, 1), total)
+            spot = 16 * f + 2 * j
+            value = spread(load(f, j), spot + 1, 1)
+            firsts = jnp.where(lane == spot + 1, value, firsts)
+            lasts = jnp.where(lane == spot, value, lasts)
         first, last = load(f, 0), load(f, SECTOR - 1)
         near_ref[f] = jnp.where(odd, first, last)
         far_ref[f] = jnp.where(odd, last, first)
-    columns_ref[...] = total
-    for copy in copies:
-        copy.wait()
-
-
-def edges(which, high, low, density, velocity, pressure):
-    rows = pltpu.VMEM((FIELDS, NR, LANES), jnp.float32)
+    columns_ref[...] = spread(firsts, -1, 1) + spread(lasts, 1, 1)
+
+
+def edges(which, density, velocity, pressure):
+    rows = pltpu.VMEM((ROW_FIELDS, NR, LANES), jnp.float32)
     return pl.pallas_call(
         edge_kernel,
-        in_specs=[SCALARS] + [pl.BlockSpec(memory_space=pl.ANY)] * 2 + [WHOLE] * 3,
-        out_specs=[WHOLE] * 4,
-        out_shape=[
-            rows,
-            rows,
-            pltpu.VMEM((NR, LANES), jnp.float32),
-            pltpu.VMEM((4, NTH, NTH), jnp.bfloat16),
-        ],
-        scratch_shapes=[pltpu.SemaphoreType.DMA((4,))],
+        in_specs=[SCALARS] + [WHOLE] * 3,
+        out_specs=[WHOLE] * 3,
+        out_shape=[rows, rows, pltpu.VMEM((NR, LANES), jnp.float32)],
         compiler_params=PARAMS,
         cost_estimate=pl.CostEstimate(flops=320 * 1024 * 3, bytes_accessed=1_800_000, transcendentals=0),
         name="edges",
-    )(which, in_hbm(high), in_hbm(low), in_vmem(density), in_vmem(velocity), in_vmem(pressure))
-
-
-def axial_terms(before, after):
-    lane = lanes_of(before.shape)
-    both = jnp.where(lane % 2 == 1, before, spread(after, -2, 1))
+    )(which, in_vmem(density), in_vmem(velocity), in_vmem(pressure))
+
+
+def axial_terms(both):
+    lane = lanes_of(both.shape)
     fields = [both] + [spread(both, -16 * f, 1) for f in range(1, FIELDS)]
     q = conserved(fields)
     along = flux(fields, q, 2)
@@ -269,10 +269,10 @@
     return [SMOOTH * q[f] + push * along[f] for f in range(FIELDS)]
 
 
-def filter_kernel(r_ref, w_ref, columns_ref, out_ref, share_ref):
+def filter_kernel(r_ref, w_ref, columns_ref, out_ref, next_ref, last_ref, share):
     shape = (N_TH, SECTOR, LANES)
     row, lane = rows_of(shape), lanes_of(shape)
-    starts = [s * SEND_ROWS for s in range(N_TH)]
+    starts = [slot(s) * SEND_ROWS for s in range(N_TH)]
     main = jnp.stack([r_ref[a : a + 8, :] for a in starts])
     extra = jnp.stack([r_ref[a + 8 : a + 16, :] for a in starts])
     zero = jnp.zeros(shape, jnp.float32)
@@ -304,103 +304,168 @@
     half = product(w_ref[2], w_ref[3], half)
     packed = jnp.where(lane < 64, half, spread(spread(half, 64, 2), 4, 1))
     for s in range(N_TH):
-        base, start = s * BACK_ROWS, s * SEND_ROWS
+        base, start = slot(s) * BACK_ROWS, starts[s]
         out_ref[base : base + 8, :] = main[s]
         out_ref[base + 8 : base + 12, :] = packed[s, :4]
-        share_ref[5 * s : 5 * s + 1, :] = r_ref[start + 14 : start + 15, :]
-        share_ref[5 * s + 1 : 5 * s + 5, :] = r_ref[start + 16 : start + 20, :]
-    share_ref[SHARE:, :] = columns_ref[...]
+        share[5 * s : 5 * s + 1, :] = r_ref[start + 14 : start + 15, :]
+        share[5 * s + 1 : 5 * s + 5, :] = r_ref[start + 16 : start + 20, :]
+    values = share[...]
+    columns = columns_ref[...]
+    for place, upper, lower in (
+        (slice(0, HALF_SHARE), values[:HALF_SHARE], values[HALF_SHARE:]),
+        (slice(HALF_SHARE, None), columns[: NR // 2], columns[NR // 2 :]),
+    ):
+        next_ref[place, :], last_ref[place, :] = two_halves(upper, lower)
+
+
+def two_halves(upper, lower):
+    odd = lanes_of(upper.shape) % 2 == 1
+    return jnp.where(odd, upper, spread(lower, -1, 1)), jnp.where(odd, spread(upper, 1, 1), lower)
+
+
+def from_halves(odd_lanes, even_lanes):
+    odd = lanes_of(odd_lanes.shape) % 2 == 1
+    upper = jnp.where(odd, odd_lanes, spread(even_lanes, -1, 1))
+    lower = jnp.where(odd, spread(odd_lanes, 1, 1), even_lanes)
+    return upper, lower
 
 
 def filtered(received, matrices, columns):
+    pack = pltpu.VMEM((HALF_SHARE + NR // 2, LANES), jnp.float32)
     return pl.pallas_call(
         filter_kernel,
         in_specs=[WHOLE] * 3,
-        out_specs=[WHOLE] * 2,
-        out_shape=[
-            pltpu.VMEM((N_TH * BACK_ROWS, LANES), jnp.float32),
-            pltpu.VMEM((SHARE + NR, LANES), jnp.float32),
-        ],
+        out_specs=[WHOLE] * 3,
+        out_shape=[pltpu.VMEM((N_TH * BACK_ROWS, LANES), jnp.float32), pack, pack],
+        scratch_shapes=[pltpu.VMEM((SHARE, LANES), jnp.float32)],
         compiler_params=PARAMS,
         cost_estimate=pl.CostEstimate(flops=6 * 256 * 256 * 256, bytes_accessed=1_200_000, transcendentals=0),
         name="filtered",
     )(in_vmem(received), in_vmem(matrices), in_vmem(columns))
 
 
-def outer_kernel(odd_ref, d_ref, v_ref, p_ref, side_ref, back_ref, token_ref, out_ref):
-    del token_ref
-    th_odd = odd_ref[0] == 1
+def theta_terms(fields, q, c):
+    around = flux(fields, q, 1)
+    smooth = [(0.4 * c) * part for part in q]
+    push = [c * part for part in around]
+    return [a + b for a, b in zip(smooth, push)], [a - b for a, b in zip(smooth, push)]
+
+
+def outer_kernel(
+    which_ref, high_ref, low_ref, table_ref, d_ref, v_ref, p_ref, out_ref, w_ref, rising_ref, done
+):
+    copies = [
+        pltpu.make_async_copy(table.at[which_ref[1 + k]], w_ref.at[2 * k + n], done.at[2 * k + n])
+        for k in range(2)
+        for n, table in enumerate((high_ref, low_ref))
+    ]
+    first = pl.multiple_of(which_ref[3] * SECTOR, SECTOR)
+    size = N_TH * SECTOR
+    copies.append(
+        pltpu.make_async_copy(
+            table_ref.at[pl.ds(first, size), :], out_ref.at[pl.ds(BLOCK_ROWS, size), :], done.at[4]
+        )
+    )
+    for copy in copies:
+        copy.start()
+    out_ref[PARITY_ROW:, :] = jnp.full((SECTOR, LANES), which_ref[0].astype(jnp.float32))
     shape = (NR, LANES)
-    lane, row = lanes_of(shape), rows_of(shape)
+    lane, row = lanes_of(shape)[NF:], rows_of(shape)
     radius = row.astype(jnp.float32) + 0.5
-    inverse = 1.0 / radius
+    inverse = (1.0 / radius)[NF:]
     c = (theta_factor(0) * 0.5) * inverse
-
-    def load(j):
-        return (d_ref[j], v_ref[0, j], v_ref[1, j], v_ref[2, j], p_ref[j])
+    first_lane, last_lane = lane == 0, lane == LANES - 1
+    last_row = row == NR - 1
+    own_scale, source_scale = 0.8 - 0.8 * c, 0.25 * inverse
+    push_scale = HALF_STEP * radius
+    for f in range(FIELDS):
+        rising_ref[f] = jnp.zeros((NR - NF, LANES), jnp.float32)
+
+    def rows_at(f, j):
+        return pl.ds(pl.multiple_of((f * SECTOR + j) * OUTER, NF), OUTER)
 
     def step(j, carry):
-        fields = load(j)
-        below = load(jnp.maximum(j - 1, 0))
-        above = load(jnp.minimum(j + 1, SECTOR - 1))
-        use_low, use_high = j == 0, j == SECTOR - 1
-        below = [
-            jnp.where(use_low, jnp.where(th_odd, side_ref[f], back_ref[f]), below[f]) for f in range(FIELDS)
-        ]
-        above = [
-            jnp.where(use_high, jnp.where(th_odd, back_ref[f], side_ref[f]), above[f]) for f in range(FIELDS)
-        ]
-        q = conserved(fields)
-        radial = flux(fields, q, 0)
+        every = (d_ref[j], v_ref[0, j], v_ref[1, j], v_ref[2, j], p_ref[j])
+        every_q = conserved(every)
+        radial = flux(every, every_q, 0)
+        fields, q = [part[NF:] for part in every], [part[NF:] for part in every_q]
         along = flux(fields, q, 2)
-        q_low, q_high = conserved(below), conserved(above)
-        f_low, f_high = flux(below, q_low, 1), flux(above, q_high, 1)
-        scale = 0.25 * inverse
+        rising, falling = theta_terms(fields, q, c)
         sources = (
             None,
-            scale * (q[2] * fields[2] + fields[4]),
-            -scale * (q[1] * fields[2]),
+            source_scale * (q[2] * fields[2] + fields[4]),
+            -source_scale * (q[1] * fields[2]),
             None,
             None,
         )
         for f in range(FIELDS):
-            own = q[f] * (0.8 - 0.8 * c)
+            own = q[f] * own_scale
             if sources[f] is not None:
                 own = own + sources[f]
-            smooth, push = SMOOTH * q[f], HALF_STEP * along[f]
-            own = own + jnp.where(lane == 0, 0.0, spread(smooth + push, 1, 1))
-            own = own + jnp.where(lane == LANES - 1, 0.0, spread(smooth - push, LANES - 1, 1))
-            own = own + c * (0.4 * (q_low[f] + q_high[f]) + (f_low[f] - f_high[f]))
-            push = (HALF_STEP * radius) * radial[f]
-            smooth_ahead = jnp.where(row == NR - 1, smooth, spread(smooth, NR - 1, 0))
-            push_ahead = jnp.where(row == NR - 1, push + HALF_STEP * radial[f], spread(push, NR - 1, 0))
-            own = own + (smooth_ahead + spread(smooth, 1, 0))
-            own = own + inverse * (spread(push, 1, 0) - push_ahead)
-            out_ref[f, j] = own
+            smooth, push = SMOOTH * every_q[f], HALF_STEP * along[f]
+            near = smooth[NF:]
+            own = own + jnp.where(first_lane, 0.0, spread(near + push, 1, 1))
+            own = own + jnp.where(last_lane, 0.0, spread(near - push, LANES - 1, 1))
+            push = push_scale * radial[f]
+            ghost = push + HALF_STEP * radial[f]
+            smooth_ahead = jnp.where(last_row, smooth, spread(smooth, NR - 1, 0))
+            push_ahead = jnp.where(last_row, ghost, spread(push, NR - 1, 0))
+            own = own + (smooth_ahead + spread(smooth, 1, 0))[NF:]
+            own = own + inverse * (spread(push, 1, 0) - push_ahead)[NF:]
+            out_ref[rows_at(f, j), :] = own + rising_ref[f]
+            rising_ref[f] = rising[f]
+
+        @pl.when(j > 0)
+        def _():
+            for f in range(FIELDS):
+                out_ref[rows_at(f, j - 1), :] = out_ref[rows_at(f, j - 1), :] + falling[f]
+
         return carry
 
     lax.fori_loop(0, SECTOR, step, 0)
-
-
-def outer_part(odd, density, velocity, pressure, side, back, token):
+    for copy in copies:
+        copy.wait()
+
+
+def outer_part(which, high, low, table, density, velocity, pressure):
     return pl.pallas_call(
         outer_kernel,
-        in_specs=[SCALARS] + [WHOLE] * 5 + [pl.BlockSpec(memory_space=pl.ANY)],
-        out_specs=WHOLE,
-        out_shape=pltpu.VMEM((FIELDS, SECTOR, NR, LANES), jnp.float32),
+        in_specs=[SCALARS] + [pl.BlockSpec(memory_space=pl.ANY)] * 3 + [WHOLE] * 3,
+        out_specs=[WHOLE] * 2,
+        out_shape=[
+            pltpu.VMEM((REST_ROWS, LANES), jnp.float32),
+            pltpu.VMEM((4, NTH, NTH), jnp.bfloat16),
+        ],
+        scratch_shapes=[
+            pltpu.VMEM((FIELDS, NR - NF, LANES), jnp.float32),
+            pltpu.SemaphoreType.DMA((5,)),
+        ],
         compiler_params=PARAMS,
         cost_estimate=pl.CostEstimate(flops=64 * 1024 * 250, bytes_accessed=3_000_000, transcendentals=0),
         name="outer_part",
-    )(odd, density, velocity, pressure, in_vmem(side), in_vmem(back), token)
-
-
-def finish_kernel(place_ref, r_ref, w_ref, near_ref, far_ref, rest_ref, out_ref, buffer, border, done):
-    start = N_TH - 1 - place_ref[0]
-    odd = place_ref[1] == 1
-    near, far = near_ref[...], far_ref[...]
-    before, after = jnp.where(odd, near, far), jnp.where(odd, far, near)
-    border[...] = jnp.where(lanes_of((SHARE, LANES)) % 2 == 1, before[:SHARE], after[:SHARE])
-    terms = axial_terms(before[SHARE + NF :], after[SHARE + NF :])
+    )(
+        which,
+        *[in_hbm(value) for value in (high, low, table)],
+        *[in_vmem(value) for value in (density, velocity, pressure)],
+    )
+
+
+def finish_kernel(
+    r_ref, before_ref, after_ref, rest_ref, side_ref, back_ref, out_ref, buffer, border, rows_ref, done
+):
+    arrivals = [
+        pltpu.make_async_copy(
+            value.at[pl.ds(0, FIELDS), pl.ds(NF, NR - NF), :], rows_ref.at[n], done.at[SECTOR + 1 + n]
+        )
+        for n, value in enumerate((side_ref, back_ref))
+    ]
+    for copy in arrivals:
+        copy.start()
+    before, after = before_ref[...], after_ref[...]
+    upper, lower = from_halves(before, after)
+    border[:HALF_SHARE, :] = upper[:HALF_SHARE]
+    border[HALF_SHARE:, :] = lower[:HALF_SHARE]
+    terms = axial_terms(jnp.concatenate([upper[HALF_SHARE:], lower[HALF_SHARE:]], axis=0)[NF:])
     shape = (SECTOR, LANES)
     lane = lanes_of(shape)
     ends = (lane == 0) | (lane == LANES - 1)
@@ -412,24 +477,32 @@
         rows = pl.ds(NF, NR - NF)
         return pltpu.make_async_copy(buffer.at[:, j, rows, :], out_ref.at[:, j, rows, :], done.at[j])
 
-    for j in range(SECTOR):
+    def write_outer(j, more):
         for f in range(FIELDS):
-            side = spread(terms[f], LANES - 1 - 2 * j, 1)
-            buffer[f, j, NF:, :] = rest_ref[f, j, NF:, :] + jnp.where(far_ends, side, 0.0)
+            beyond = jnp.where(far_ends, spread(terms[f], LANES - 1 - 2 * j, 1), 0.0)
+            if more is not None:
+                beyond = beyond + more[f]
+            first = (f * SECTOR + j) * OUTER
+            buffer[f, j, NF:, :] = rest_ref[first : first + OUTER, :] + beyond
         outer(j).start()
+
+    for j in range(1, SECTOR - 1):
+        write_outer(j, None)
 
     sums = [jnp.zeros(shape, jnp.float32) for _ in range(FIELDS)]
     for t in range(N_TH):
-        weights = w_ref[start + t]
+        weights = rest_ref[BLOCK_ROWS + SECTOR * t : BLOCK_ROWS + SECTOR * (t + 1), :]
         for f in range(FIELDS):
             sums[f] = sums[f] + weights * border[5 * t + f : 5 * t + f + 1, :]
     for f in range(FIELDS):
         for shift in (2, 4, 8):
             sums[f] = sums[f] + spread(sums[f], -shift, 1)
 
+    tiles = buffer.reshape(FIELDS * SECTOR * NR, LANES)
+
     def joined(unit_a, unit_b):
-        a = r_ref[unit_a * BACK_ROWS + 8 : unit_a * BACK_ROWS + 12, :]
-        b = r_ref[unit_b * BACK_ROWS + 8 : unit_b * BACK_ROWS + 12, :]
+        start_a, start_b = slot(unit_a) * BACK_ROWS + 8, slot(unit_b) * BACK_ROWS + 8
+        a, b = r_ref[start_a : start_a + 4, :], r_ref[start_b : start_b + 4, :]
         top = jnp.where(low_half, a, spread(b, 64, 1))
         bottom = jnp.where(low_half, spread(a, 64, 1), b)
         return jnp.concatenate([top, bottom], axis=0)
@@ -437,38 +510,53 @@
     for f in range(FIELDS):
         for cycle in range(NF):
             if f < 4:
-                unit = (f * NF + cycle) * BACK_ROWS
-                tile = r_ref[unit : unit + 8, :]
+                start = slot(f * NF + cycle) * BACK_ROWS
+                tile = r_ref[start : start + 8, :]
             else:
                 tile = joined(cycle, NF + cycle)
             if cycle == 0:
                 tile = tile + joined(16 + 2 * f, 17 + 2 * f)
             tile = tile + jnp.where(ends, spread(sums[f], -(16 * cycle + 1), 1), 0.0)
-            buffer[f, :, cycle, :] = tile
+            tiles[pl.ds(f * SECTOR * NR + cycle, SECTOR, stride=NR), :] = tile
     rows = pl.ds(0, NF)
     inner = pltpu.make_async_copy(buffer.at[:, :, rows, :], out_ref.at[:, :, rows, :], done.at[SECTOR])
     inner.start()
+    for copy in arrivals:
+        copy.wait()
+    c = (theta_factor(0) * 0.5) / (rows_of((NR, LANES))[NF:].astype(jnp.float32) + 0.5)
+    odd = jnp.concatenate([rest_ref[PARITY_ROW:, :]] * (NR // NF - 1), axis=0) > 0.5
+    side = [rows_ref[0, f] for f in range(FIELDS)]
+    back = [rows_ref[1, f] for f in range(FIELDS)]
+    below = [jnp.where(odd, a, b) for a, b in zip(side, back)]
+    above = [jnp.where(odd, b, a) for a, b in zip(side, back)]
+    write_outer(0, theta_terms(below, conserved(below), c)[0])
+    write_outer(SECTOR - 1, theta_terms(above, conserved(above), c)[1])
     for j in range(SECTOR):
         outer(j).wait()
     inner.wait()
 
 
-def finish(place, received, weights, near, far, rest):
+def finish(received, before, after, rest, side, back):
     block = (FIELDS, SECTOR, NR, LANES)
     return pl.pallas_call(
         finish_kernel,
-        in_specs=[SCALARS] + [WHOLE] * 5,
+        in_specs=[WHOLE] * 4 + [pl.BlockSpec(memory_space=pl.ANY)] * 2,
         out_specs=pl.BlockSpec(memory_space=pl.ANY),
         out_shape=jax.ShapeDtypeStruct(block, jnp.float32),
         scratch_shapes=[
             pltpu.VMEM(block, jnp.float32),
             pltpu.VMEM((SHARE, LANES), jnp.float32),
-            pltpu.SemaphoreType.DMA((SECTOR + 1,)),
+            pltpu.VMEM((2, FIELDS, NR - NF, LANES), jnp.float32),
+            pltpu.SemaphoreType.DMA((SECTOR + 3,)),
         ],
         compiler_params=PARAMS,
         cost_estimate=pl.CostEstimate(flops=400 * 1024, bytes_accessed=3_000_000, transcendentals=0),
         name="finish",
-    )(place, in_vmem(received), in_vmem(weights), in_vmem(near), in_vmem(far), in_vmem(rest))
+    )(
+        *[in_vmem(value) for value in (received, before, after, rest)],
+        in_hbm(side),
+        in_hbm(back),
+    )
 
 
 def pairs(size, offset):
@@ -477,34 +565,35 @@
 
 def transposed(value, rows):
     value = value.reshape(N_TH, rows // 4, 4, LANES)
-    return lax.all_to_all(value, "th", 0, 0, tiled=True).reshape(N_TH * rows, LANES)
+    group = [(FIRST + k) % N_TH for k in range(N_TH)]
+    value = lax.all_to_all(value, "th", 0, 0, tiled=True, axis_index_groups=[group])
+    return value.reshape(N_TH * rows, LANES)
 
 
 def per_device(density, velocity, pressure):
     high, low = filter_matrices()
     high, low = jnp.asarray(high), jnp.asarray(low)
-    weights = jnp.asarray(edge_weights())
-    th, gz = lax.axis_index("th"), lax.axis_index("gz")
+    table = jnp.asarray(edge_weights())
+    th = lax.axis_index("th")
     main = th % NF
     half = jnp.where(th < 16, main, jnp.where(th < 26, NF, 0))
-    which = jnp.stack([th % 2, main, half]).astype(jnp.int32)
-    place = jnp.stack([th, gz % 2]).astype(jnp.int32)
+    which = jnp.stack([th % 2, main, half, N_TH - 1 - th]).astype(jnp.int32)
 
     sent = inner_part(density, velocity, pressure)
     received = transposed(sent, SEND_ROWS)
 
-    near_row, far_row, columns, matrices = edges(which, high, low, density, velocity, pressure)
+    near_row, far_row, columns = edges(which, density, velocity, pressure)
     th_far = lax.ppermute(far_row, "th", pairs(N_TH, 1))
     th_near = lax.ppermute(near_row, "th", pairs(N_TH, 0))
 
-    back, share = filtered(received, matrices, columns)
-    back, th_far, th_near = lax.optimization_barrier((back, th_far, th_near))
+    rest, matrices = outer_part(which, high, low, table, density, velocity, pressure)
+    back, to_next, to_last = filtered(received, matrices, columns)
+    to_next, to_last, th_far, th_near = lax.optimization_barrier((to_next, to_last, th_far, th_near))
     returned = transposed(back, BACK_ROWS)
-    gz_size = lax.axis_size("gz")
-    gz_far = lax.ppermute(share, "gz", pairs(gz_size, 1))
-    gz_near = lax.ppermute(share, "gz", pairs(gz_size, 0))
-    rest = outer_part(which, density, velocity, pressure, th_near, th_far, share)
-    return finish(place, returned, weights, gz_near, gz_far, rest)
+    size = lax.axis_size("gz")
+    before = lax.ppermute(to_next, "gz", [(i, (i + 1) % size) for i in range(size)])
+    after = lax.ppermute(to_last, "gz", [(i, (i - 1) % size) for i in range(size)])
+    return finish(returned, before, after, rest, th_near, th_far)
 
 
 def solution(mesh):

time: 64 us -> 56.5 us (0.88)
  waiting for transfers between devices: 7.42 us -> 1.24 us
  Pallas kernels: 12.1 us -> 9.39 us
  starting transfers between devices: 43.8 us -> 45.2 us
    all_to_all x2, starting transfers between devices: 23.9 us -> 31.5 us  [transposed(): lax.all_to_all(value, 'th', 0, 0, tiled=True, axis_index_groups=[group])]
    ppermute x1, starting transfers between devices: 8.16 us -> 2.03 us  [per_device(): th_near = lax.ppermute(near_row, 'th', pairs(N_TH, 0))]
    all_to_all x2, waiting for transfers between devices: 4.22 us -> 0.01 us  [transposed(): lax.all_to_all(value, 'th', 0, 0, tiled=True, axis_index_groups=[group])]
    ppermute x2, waiting for transfers between devices: 3.19 us -> 1.23 us  [the longest x1 1.18 us: per_device(): lax.ppermute(to_next, 'gz', [(i, (i + 1) % size) for i in range(size)])]
    pallas_call x1, Pallas kernels: 3.55 us -> 2.19 us  [inner_part(): pl.pallas_call(inner_kernel, grid=(1,), in_specs=[pl.BlockSpec((SECTOR, 1...]
    pallas_call x4, Pallas kernels: 8.56 us -> 7.21 us  [the longest x1 2.41 us: outer_part(): pl.pallas_call(outer_kernel, in_specs=[SCALARS] + [pl.BlockSpec(memory_sp...]
    ppermute x1, starting transfers between devices: 3.54 us -> 2.44 us  [per_device(): th_far = lax.ppermute(far_row, 'th', pairs(N_TH, 1))]
    ppermute x2, starting transfers between devices: 8.24 us -> 9.29 us  [the longest x1 6.28 us: per_device(): lax.ppermute(to_last, 'gz', [(i, (i - 1) % size) for i in range(size)])]
  transfers between devices with their start and end apart: 6 -> 6, of which waited for: 3 -> 2; matrix products, arithmetic and copies ran while one was open for 0% -> 0% of each run, Pallas kernels for 10% -> 9%
where the time goes in v3:
time: 56.5 us; the launch traced here: 56.1 us
  starting transfers between devices  45.2 us (80%)
  Pallas kernels  9.39 us (17%)
  waiting for transfers between devices  1.24 us (2%)
    all_to_all x2, starting transfers between devices, transposed(): lax.all_to_all(value, 'th', 0, 0, tiled=True, axis_index_groups=[group])  31.5 us
    ppermute x1, starting transfers between devices, per_device(): lax.ppermute(to_last, 'gz', [(i, (i - 1) % size) for i in range(size)])  6.28 us
    ppermute x1, starting transfers between devices, per_device(): lax.ppermute(to_next, 'gz', [(i, (i + 1) % size) for i in range(size)])  3.01 us
    ppermute x1, starting transfers between devices, per_device(): th_far = lax.ppermute(far_row, 'th', pairs(N_TH, 1))  2.44 us
    pallas_call x1, Pallas kernels, outer_part(): pl.pallas_call(outer_kernel, in_specs=[SCALARS] + [pl.BlockSpec(memory_sp...  2.41 us
    pallas_call x1, Pallas kernels, inner_part(): pl.pallas_call(inner_kernel, grid=(1,), in_specs=[pl.BlockSpec((SECTOR, 1...  2.19 us
    ppermute x1, starting transfers between devices, per_device(): th_near = lax.ppermute(near_row, 'th', pairs(N_TH, 0))  2.03 us
    pallas_call x1, Pallas kernels, finish(): pl.pallas_call(finish_kernel, in_specs=[WHOLE] * 4 + [pl.BlockSpec(memory...  1.94 us
  transfers between devices with their start and end apart: 6, of which 2 were waited for; matrix products, arithmetic and copies ran while one was open for 0% of the time, Pallas kernels for 9%

profile of v3, /device:TPU:1, one launch (start us, length us, event | category | flops | bytes accessed | tf_op | source)
XLA Modules:
  0.0 56.1 jit_solution(8569774224173654000)
XLA Ops:
  0.0 0.0 copy-start.2
  0.0 0.0 copy-start
  0.0 0.0 copy-start.1
  0.0 2.2 %inner_part.1 = f32[640,128]{1,0:T(8,128)} custom-call(f32[8,64,128]{2,1,0:T(8,128)} %d_ref.5, f32[3,8,64,128]{3,2,1,0:T(8,128)} %v_ref.5, f32[8,64,128]{2,1,0:T(8,128)} %p_ref.5), custom_call_target="tpu_custom_call" | custom-call | flops 1638400 | bytes 600000 | tf_op jit(solution)/shard_map/inner_part/pallas_call | solution.py:213
  2.2 19.0 %all-to-all-start = ((f32[32,5,4,128]{3,2,1,0:T(4,128)}), f32[32,5,4,128]{3,2,1,0:T(4,128)S(1)}, u32[]{:S(2)}, u32[]{:S(2)}) async-start(f32[32,5,4,128]{3,2,1,0:T(4,128)} %bitcast), calls=%async_computation | async-start | bytes 655360 | tf_op jit(solution)/shard_map/all_to_all | solution.py:569
  21.2 0.1 pad_add_fusion.which_ref
  21.3 0.0 copy-done.2
  21.3 0.0 copy-done
  21.3 0.0 copy-done.1
  21.3 1.7 %edges.1 = (f32[10,64,128]{2,1,0:T(8,128)}, f32[10,64,128]{2,1,0:T(8,128)}, f32[64,128]{1,0:T(8,128)S(1)}) custom-call(s32[4]{0:T(128)S(1)} %pad_add_fusion.which_ref, f32[8,64,128]{2,1,0:T(8,128)S(1)} %copy-done.1, f32[3,8,64,128]{3,2,1,0:T(8,128)S(1)} %copy-done, f32[8,64,128]{2,1,0:T(8,128)S(1)} %copy-done.2), custom_call_target="tpu_custom_call" | custom-call | flops 983040 | bytes 1800000 | tf_op jit(solution)/shard_map/edges/pallas_call | solution.py:252
  23.0 2.4 %collective-permute-start = (f32[10,64,128]{2,1,0:T(8,128)}, f32[10,64,128]{2,1,0:T(8,128)}, u32[]{:S(2)}, u32[]{:S(2)}) collective-permute-start(f32[10,64,128]{2,1,0:T(8,128)} %get-tuple-element.22), channel_id=1, source_target_pairs={{0,31},{1,2},{2,1},{3,4},{4,3},{5,6},{6,5},{7,8},{8,7},{9,10},{10,... | collective-permute-start | bytes 983048 | tf_op jit(solution)/shard_map/ppermute | solution.py:586
  25.5 2.0 %collective-permute-start.1 = (f32[10,64,128]{2,1,0:T(8,128)}, f32[10,64,128]{2,1,0:T(8,128)}, u32[]{:S(2)}, u32[]{:S(2)}) collective-permute-start(f32[10,64,128]{2,1,0:T(8,128)} %get-tuple-element.23), channel_id=1, source_target_pairs={{0,1},{1,0},{2,3},{3,2},{4,5},{5,4},{6,7},{7,6},{8,9},{9,8},{10,11... | collective-permute-start | bytes 983048 | tf_op jit(solution)/shard_map/ppermute | solution.py:587
  27.5 2.4 %outer_part.1 = (f32[2504,128]{1,0:T(8,128)S(1)}, bf16[4,256,256]{2,1,0:T(8,128)(2,1)S(1)}) custom-call(s32[4]{0:T(128)S(1)} %pad_add_fusion.which_ref, bf16[9,256,256]{2,1,0:T(8,128)(2,1)} %constant.40.clone.high_ref, bf16[9,256,256]{2,1,0:T(8,128)(2,1)} %constant.41.clone.low_ref, f32[512,128]{1,0:T(8,128)} %constant.42.clone.table_ref, ...), custom_call_target="tpu_custom_call" | custom-call | flops 16384000 | bytes 3000000 | tf_op jit(solution)/shard_map/outer_part/pallas_call | solution.py:431
  29.9 0.0 all-to-all-done
  29.9 1.1 %filtered.1 = (f32[384,128]{1,0:T(8,128)}, f32[112,128]{1,0:T(8,128)S(1)}, f32[112,128]{1,0:T(8,128)S(1)}) custom-call(f32[640,128]{1,0:T(8,128)S(1)} %bitcast.8, bf16[4,256,256]{2,1,0:T(8,128)(2,1)S(1)} %get-tuple-element.17.w_ref, f32[64,128]{1,0:T(8,128)S(1)} %get-tuple-element.18.columns_ref), custom_call_target="tpu_custom_call" | custom-call | flops 100663296 | bytes 1200000 | tf_op jit(solution)/shard_map/filtered/pallas_call | solution.py:335
  31.1 12.5 %all-to-all-start.1 = ((f32[32,3,4,128]{3,2,1,0:T(4,128)}), f32[32,3,4,128]{3,2,1,0:T(4,128)S(1)}, u32[]{:S(2)}, u32[]{:S(2)}) async-start(f32[32,3,4,128]{3,2,1,0:T(4,128)} %bitcast.6), calls=%async_computation.1 | async-start | bytes 393216 | tf_op jit(solution)/shard_map/all_to_all | solution.py:569
  43.6 0.0 collective-permute-done.back_ref
  43.6 0.0 collective-permute-done.1.side_ref
  43.6 3.0 %collective-permute-start.2 = (f32[112,128]{1,0:T(8,128)S(1)}, f32[112,128]{1,0:T(8,128)S(1)}, u32[]{:S(2)}, u32[]{:S(2)}) collective-permute-start(f32[112,128]{1,0:T(8,128)S(1)} %get-tuple-element.24), channel_id=1, source_target_pairs={{0,32},{32,64},{64,96},{96,128},{128,160},{160,192},{192,224},{224... | collective-permute-start | bytes 172040 | tf_op jit(solution)/shard_map/ppermute | solution.py:594
  46.6 6.3 %collective-permute-start.3 = (f32[112,128]{1,0:T(8,128)S(1)}, f32[112,128]{1,0:T(8,128)S(1)}, u32[]{:S(2)}, u32[]{:S(2)}) collective-permute-start(f32[112,128]{1,0:T(8,128)S(1)} %get-tuple-element.25), channel_id=1, source_target_pairs={{0,480},{32,0},{64,32},{96,64},{128,96},{160,128},{192,160},{224,1... | collective-permute-start | bytes 172040 | tf_op jit(solution)/shard_map/ppermute | solution.py:595
  52.9 1.2 %collective-permute-done.2.before_ref = f32[112,128]{1,0:T(8,128)S(1)} collective-permute-done((f32[112,128]{1,0:T(8,128)S(1)}, f32[112,128]{1,0:T(8,128)S(1)}, u32[]{:S(2)}, u32[]{:S(2)}) %collective-permute-start.2) | collective-permute-done | bytes 57376 | tf_op jit(solution)/shard_map/ppermute | solution.py:594
  54.1 0.1 collective-permute-done.3.after_ref
  54.1 0.0 all-to-all-done.1
  54.1 1.9 %finish.1 = f32[5,8,64,128]{3,2,1,0:T(8,128)} custom-call(f32[384,128]{1,0:T(8,128)S(1)} %bitcast.9, f32[112,128]{1,0:T(8,128)S(1)} %collective-permute-done.2.before_ref, f32[112,128]{1,0:T(8,128)S(1)} %collective-permute-done.3.after_ref, f32[2504,128]{1,0:T(8,128)S(1)} %get-tuple-element.26.rest_ref, f32[10,64,128]{2,1,0:T(8,128)} %collective-permute-done.1.side_ref, ...), custom_call_target="tpu_custom_call" | custom-call | flops 409600 | bytes 3000000 | tf_op jit(solution)/shard_map/finish/pallas_call | solution.py:541
Async XLA Ops:
  0.0 21.3 %copy-start.2 = (f32[8,64,128]{2,1,0:T(8,128)S(1)}, f32[8,64,128]{2,1,0:T(8,128)}, u32[]{:S(2)}) copy-start(f32[8,64,128]{2,1,0:T(8,128)} %p_ref.5) | copy-start | bytes 786436
  0.0 21.3 %copy-start = (f32[3,8,64,128]{3,2,1,0:T(8,128)S(1)}, f32[3,8,64,128]{3,2,1,0:T(8,128)}, u32[]{:S(2)}) copy-start(f32[3,8,64,128]{3,2,1,0:T(8,128)} %v_ref.5) | copy-start | bytes 2359300
  0.0 21.3 %copy-start.1 = (f32[8,64,128]{2,1,0:T(8,128)S(1)}, f32[8,64,128]{2,1,0:T(8,128)}, u32[]{:S(2)}) copy-start(f32[8,64,128]{2,1,0:T(8,128)} %d_ref.5) | copy-start | bytes 786436
  2.2 27.7 %all-to-all-start = ((f32[32,5,4,128]{3,2,1,0:T(4,128)}), f32[32,5,4,128]{3,2,1,0:T(4,128)S(1)}, u32[]{:S(2)}, u32[]{:S(2)}) async-start(f32[32,5,4,128]{3,2,1,0:T(4,128)} %bitcast), calls=%async_computation | async-start | bytes 655360 | tf_op jit(solution)/shard_map/all_to_all | solution.py:569
  23.0 20.6 %collective-permute-start = (f32[10,64,128]{2,1,0:T(8,128)}, f32[10,64,128]{2,1,0:T(8,128)}, u32[]{:S(2)}, u32[]{:S(2)}) collective-permute-start(f32[10,64,128]{2,1,0:T(8,128)} %get-tuple-element.22), channel_id=1, source_target_pairs={{0,31},{1,2},{2,1},{3,4},{4,3},{5,6},{6,5},{7,8},{8,7},{9,10},{10,... | collective-permute-start | bytes 983048 | tf_op jit(solution)/shard_map/ppermute | solution.py:586
  25.5 18.1 %collective-permute-start.1 = (f32[10,64,128]{2,1,0:T(8,128)}, f32[10,64,128]{2,1,0:T(8,128)}, u32[]{:S(2)}, u32[]{:S(2)}) collective-permute-start(f32[10,64,128]{2,1,0:T(8,128)} %get-tuple-element.23), channel_id=1, source_target_pairs={{0,1},{1,0},{2,3},{3,2},{4,5},{5,4},{6,7},{7,6},{8,9},{9,8},{10,11... | collective-permute-start | bytes 983048 | tf_op jit(solution)/shard_map/ppermute | solution.py:587
  31.1 23.1 %all-to-all-start.1 = ((f32[32,3,4,128]{3,2,1,0:T(4,128)}), f32[32,3,4,128]{3,2,1,0:T(4,128)S(1)}, u32[]{:S(2)}, u32[]{:S(2)}) async-start(f32[32,3,4,128]{3,2,1,0:T(4,128)} %bitcast.6), calls=%async_computation.1 | async-start | bytes 393216 | tf_op jit(solution)/shard_map/all_to_all | solution.py:569
  43.6 10.5 %collective-permute-start.2 = (f32[112,128]{1,0:T(8,128)S(1)}, f32[112,128]{1,0:T(8,128)S(1)}, u32[]{:S(2)}, u32[]{:S(2)}) collective-permute-start(f32[112,128]{1,0:T(8,128)S(1)} %get-tuple-element.24), channel_id=1, source_target_pairs={{0,32},{32,64},{64,96},{96,128},{128,160},{160,192},{192,224},{224... | collective-permute-start | bytes 172040 | tf_op jit(solution)/shard_map/ppermute | solution.py:594
  46.6 7.5 %collective-permute-start.3 = (f32[112,128]{1,0:T(8,128)S(1)}, f32[112,128]{1,0:T(8,128)S(1)}, u32[]{:S(2)}, u32[]{:S(2)}) collective-permute-start(f32[112,128]{1,0:T(8,128)S(1)} %get-tuple-element.25), channel_id=1, source_target_pairs={{0,480},{32,0},{64,32},{96,64},{128,96},{160,128},{192,160},{224,1... | collective-permute-start | bytes 172040 | tf_op jit(solution)/shard_map/ppermute | solution.py:595

commit v4 on v3

--- a/solution.py
+++ b/solution.py
@@ -18,14 +18,12 @@
 FIELDS = 5
 SEND_ROWS = 20
 BACK_ROWS = 12
-SHARE = N_TH * FIELDS
-HALF_SHARE = SHARE // 2
 OUTER = NR - NF
 BLOCK_ROWS = FIELDS * SECTOR * OUTER
-PARITY_ROW = BLOCK_ROWS + N_TH * SECTOR
-REST_ROWS = PARITY_ROW + SECTOR
+PACK_ROWS = SECTOR + NR // 2
+UP_ROWS, DOWN_ROWS = 0, 0
 FIRST = 24
-ROW_FIELDS = 10
+ROW_FIELDS = 11
 
 HALF_STEP = 0.125
 SMOOTH = 0.05
@@ -206,7 +204,6 @@
 
 PARAMS = pltpu.CompilerParams(vmem_limit_bytes=24 << 20)
 WHOLE = pl.BlockSpec(memory_space=pltpu.VMEM)
-SCALARS = pl.BlockSpec(memory_space=pltpu.SMEM)
 
 
 def inner_part(density, velocity, pressure):
@@ -226,9 +223,9 @@
     )(in_hbm(density), in_hbm(velocity), in_hbm(pressure))
 
 
-def edge_kernel(which_ref, d_ref, v_ref, p_ref, near_ref, far_ref, columns_ref):
+def edge_kernel(d_ref, v_ref, p_ref, near_ref, far_ref, columns_ref):
     lane = lanes_of((NR, LANES))
-    odd = which_ref[0] == 1
+    odd = lax.axis_index("th") % 2 == 1
 
     def load(f, j):
         return d_ref[j] if f == 0 else (p_ref[j] if f == 4 else v_ref[f - 1, j])
@@ -247,17 +244,17 @@
     columns_ref[...] = spread(firsts, -1, 1) + spread(lasts, 1, 1)
 
 
-def edges(which, density, velocity, pressure):
+def edges(density, velocity, pressure):
     rows = pltpu.VMEM((ROW_FIELDS, NR, LANES), jnp.float32)
     return pl.pallas_call(
         edge_kernel,
-        in_specs=[SCALARS] + [WHOLE] * 3,
+        in_specs=[WHOLE] * 3,
         out_specs=[WHOLE] * 3,
         out_shape=[rows, rows, pltpu.VMEM((NR, LANES), jnp.float32)],
         compiler_params=PARAMS,
         cost_estimate=pl.CostEstimate(flops=320 * 1024 * 3, bytes_accessed=1_800_000, transcendentals=0),
         name="edges",
-    )(which, in_vmem(density), in_vmem(velocity), in_vmem(pressure))
+    )(in_vmem(density), in_vmem(velocity), in_vmem(pressure))
 
 
 def axial_terms(both):
@@ -269,7 +266,7 @@
     return [SMOOTH * q[f] + push * along[f] for f in range(FIELDS)]
 
 
-def filter_kernel(r_ref, w_ref, columns_ref, out_ref, next_ref, last_ref, share):
+def filter_kernel(r_ref, w_ref, weights_ref, columns_ref, out_ref, up_ref, down_ref):
     shape = (N_TH, SECTOR, LANES)
     row, lane = rows_of(shape), lanes_of(shape)
     starts = [slot(s) * SEND_ROWS for s in range(N_TH)]
@@ -303,19 +300,25 @@
     main = product(w_ref[0], w_ref[1], main)
     half = product(w_ref[2], w_ref[3], half)
     packed = jnp.where(lane < 64, half, spread(spread(half, 64, 2), 4, 1))
+    sums = [jnp.zeros((SECTOR, LANES), jnp.float32) for _ in range(FIELDS)]
     for s in range(N_TH):
         base, start = slot(s) * BACK_ROWS, starts[s]
         out_ref[base : base + 8, :] = main[s]
         out_ref[base + 8 : base + 12, :] = packed[s, :4]
-        share[5 * s : 5 * s + 1, :] = r_ref[start + 14 : start + 15, :]
-        share[5 * s + 1 : 5 * s + 5, :] = r_ref[start + 16 : start + 20, :]
-    values = share[...]
+        weights = weights_ref[SECTOR * s : SECTOR * (s + 1), :]
+        for f, place in enumerate((14, 16, 17, 18, 19)):
+            sums[f] = sums[f] + weights * r_ref[start + place : start + place + 1, :]
+    first = lanes_of((SECTOR, LANES)) % 16 < 2
+    terms = jnp.zeros((SECTOR, LANES), jnp.float32)
+    for f in range(FIELDS):
+        for shift in (2, 4, 8):
+            sums[f] = sums[f] + spread(sums[f], -shift, 1)
+        terms = terms + spread(jnp.where(first, sums[f], 0.0), 2 * f, 1)
     columns = columns_ref[...]
-    for place, upper, lower in (
-        (slice(0, HALF_SHARE), values[:HALF_SHARE], values[HALF_SHARE:]),
-        (slice(HALF_SHARE, None), columns[: NR // 2], columns[NR // 2 :]),
-    ):
-        next_ref[place, :], last_ref[place, :] = two_halves(upper, lower)
+    up, down = two_halves(columns[: NR // 2], columns[NR // 2 :])
+    for target, value in ((up_ref, up), (down_ref, down)):
+        target[:SECTOR, :] = terms
+        target[SECTOR:PACK_ROWS, :] = value
 
 
 def two_halves(upper, lower):
@@ -330,18 +333,18 @@
     return upper, lower
 
 
-def filtered(received, matrices, columns):
-    pack = pltpu.VMEM((HALF_SHARE + NR // 2, LANES), jnp.float32)
+def filtered(received, matrices, weights, columns):
+    up = pltpu.VMEM((PACK_ROWS + UP_ROWS, LANES), jnp.float32)
+    down = pltpu.VMEM((PACK_ROWS + DOWN_ROWS, LANES), jnp.float32)
     return pl.pallas_call(
         filter_kernel,
-        in_specs=[WHOLE] * 3,
+        in_specs=[WHOLE] * 4,
         out_specs=[WHOLE] * 3,
-        out_shape=[pltpu.VMEM((N_TH * BACK_ROWS, LANES), jnp.float32), pack, pack],
-        scratch_shapes=[pltpu.VMEM((SHARE, LANES), jnp.float32)],
+        out_shape=[pltpu.VMEM((N_TH * BACK_ROWS, LANES), jnp.float32), up, down],
         compiler_params=PARAMS,
         cost_estimate=pl.CostEstimate(flops=6 * 256 * 256 * 256, bytes_accessed=1_200_000, transcendentals=0),
         name="filtered",
-    )(in_vmem(received), in_vmem(matrices), in_vmem(columns))
+    )(*[in_vmem(value) for value in (received, matrices, weights, columns)])
 
 
 def theta_terms(fields, q, c):
@@ -352,23 +355,22 @@
 
 
 def outer_kernel(
-    which_ref, high_ref, low_ref, table_ref, d_ref, v_ref, p_ref, out_ref, w_ref, rising_ref, done
+    high_ref, low_ref, table_ref, d_ref, v_ref, p_ref, out_ref, w_ref, weights_ref, rising_ref, done
 ):
+    th = lax.axis_index("th")
+    cycle = th % NF
+    half = jnp.where(th < 2 * NF, cycle, jnp.where(th < 2 * NF + 2 * FIELDS, NF, 0))
     copies = [
-        pltpu.make_async_copy(table.at[which_ref[1 + k]], w_ref.at[2 * k + n], done.at[2 * k + n])
-        for k in range(2)
+        pltpu.make_async_copy(table.at[place], w_ref.at[2 * k + n], done.at[2 * k + n])
+        for k, place in enumerate((cycle, half))
         for n, table in enumerate((high_ref, low_ref))
     ]
-    first = pl.multiple_of(which_ref[3] * SECTOR, SECTOR)
-    size = N_TH * SECTOR
+    first = pl.multiple_of((N_TH - 1 - th) * SECTOR, SECTOR)
     copies.append(
-        pltpu.make_async_copy(
-            table_ref.at[pl.ds(first, size), :], out_ref.at[pl.ds(BLOCK_ROWS, size), :], done.at[4]
-        )
+        pltpu.make_async_copy(table_ref.at[pl.ds(first, N_TH * SECTOR), :], weights_ref, done.at[4])
     )
     for copy in copies:
         copy.start()
-    out_ref[PARITY_ROW:, :] = jnp.full((SECTOR, LANES), which_ref[0].astype(jnp.float32))
     shape = (NR, LANES)
     lane, row = lanes_of(shape)[NF:], rows_of(shape)
     radius = row.astype(jnp.float32) + 0.5
@@ -427,14 +429,15 @@
         copy.wait()
 
 
-def outer_part(which, high, low, table, density, velocity, pressure):
+def outer_part(high, low, table, density, velocity, pressure):
     return pl.pallas_call(
         outer_kernel,
-        in_specs=[SCALARS] + [pl.BlockSpec(memory_space=pl.ANY)] * 3 + [WHOLE] * 3,
-        out_specs=[WHOLE] * 2,
+        in_specs=[pl.BlockSpec(memory_space=pl.ANY)] * 3 + [WHOLE] * 3,
+        out_specs=[WHOLE] * 3,
         out_shape=[
-            pltpu.VMEM((REST_ROWS, LANES), jnp.float32),
+            pltpu.VMEM((BLOCK_ROWS, LANES), jnp.float32),
             pltpu.VMEM((4, NTH, NTH), jnp.bfloat16),
+            pltpu.VMEM((N_TH * SECTOR, LANES), jnp.float32),
         ],
         scratch_shapes=[
             pltpu.VMEM((FIELDS, NR - NF, LANES), jnp.float32),
@@ -444,14 +447,13 @@
         cost_estimate=pl.CostEstimate(flops=64 * 1024 * 250, bytes_accessed=3_000_000, transcendentals=0),
         name="outer_part",
     )(
-        which,
         *[in_hbm(value) for value in (high, low, table)],
         *[in_vmem(value) for value in (density, velocity, pressure)],
     )
 
 
 def finish_kernel(
-    r_ref, before_ref, after_ref, rest_ref, side_ref, back_ref, out_ref, buffer, border, rows_ref, done
+    r_ref, before_ref, after_ref, rest_ref, side_ref, back_ref, out_ref, buffer, rows_ref, done
 ):
     arrivals = [
         pltpu.make_async_copy(
@@ -461,14 +463,13 @@
     ]
     for copy in arrivals:
         copy.start()
-    before, after = before_ref[...], after_ref[...]
-    upper, lower = from_halves(before, after)
-    border[:HALF_SHARE, :] = upper[:HALF_SHARE]
-    border[HALF_SHARE:, :] = lower[:HALF_SHARE]
-    terms = axial_terms(jnp.concatenate([upper[HALF_SHARE:], lower[HALF_SHARE:]], axis=0)[NF:])
+    before, after = before_ref[:PACK_ROWS, :], after_ref[:PACK_ROWS, :]
+    upper, lower = from_halves(before[SECTOR:], after[SECTOR:])
+    terms = axial_terms(jnp.concatenate([upper, lower], axis=0)[NF:])
     shape = (SECTOR, LANES)
     lane = lanes_of(shape)
     ends = (lane == 0) | (lane == LANES - 1)
+    border = jnp.where(lane % 2 == 1, before[:SECTOR], after[:SECTOR])
     low_half = lanes_of((4, LANES)) < 64
     far_lane = lanes_of((NR - NF, LANES))
     far_ends = (far_lane == 0) | (far_lane == LANES - 1)
@@ -488,15 +489,6 @@
 
     for j in range(1, SECTOR - 1):
         write_outer(j, None)
-
-    sums = [jnp.zeros(shape, jnp.float32) for _ in range(FIELDS)]
-    for t in range(N_TH):
-        weights = rest_ref[BLOCK_ROWS + SECTOR * t : BLOCK_ROWS + SECTOR * (t + 1), :]
-        for f in range(FIELDS):
-            sums[f] = sums[f] + weights * border[5 * t + f : 5 * t + f + 1, :]
-    for f in range(FIELDS):
-        for shift in (2, 4, 8):
-            sums[f] = sums[f] + spread(sums[f], -shift, 1)
 
     tiles = buffer.reshape(FIELDS * SECTOR * NR, LANES)
 
@@ -516,7 +508,7 @@
                 tile = joined(cycle, NF + cycle)
             if cycle == 0:
                 tile = tile + joined(16 + 2 * f, 17 + 2 * f)
-            tile = tile + jnp.where(ends, spread(sums[f], -(16 * cycle + 1), 1), 0.0)
+            tile = tile + jnp.where(ends, spread(border, -(16 * cycle + 2 * f + 1), 1), 0.0)
             tiles[pl.ds(f * SECTOR * NR + cycle, SECTOR, stride=NR), :] = tile
     rows = pl.ds(0, NF)
     inner = pltpu.make_async_copy(buffer.at[:, :, rows, :], out_ref.at[:, :, rows, :], done.at[SECTOR])
@@ -524,7 +516,7 @@
     for copy in arrivals:
         copy.wait()
     c = (theta_factor(0) * 0.5) / (rows_of((NR, LANES))[NF:].astype(jnp.float32) + 0.5)
-    odd = jnp.concatenate([rest_ref[PARITY_ROW:, :]] * (NR // NF - 1), axis=0) > 0.5
+    odd = lax.axis_index("th") % 2 == 1
     side = [rows_ref[0, f] for f in range(FIELDS)]
     back = [rows_ref[1, f] for f in range(FIELDS)]
     below = [jnp.where(odd, a, b) for a, b in zip(side, back)]
@@ -545,7 +537,6 @@
         out_shape=jax.ShapeDtypeStruct(block, jnp.float32),
         scratch_shapes=[
             pltpu.VMEM(block, jnp.float32),
-            pltpu.VMEM((SHARE, LANES), jnp.float32),
             pltpu.VMEM((2, FIELDS, NR - NF, LANES), jnp.float32),
             pltpu.SemaphoreType.DMA((SECTOR + 3,)),
         ],
@@ -574,25 +565,20 @@
     high, low = filter_matrices()
     high, low = jnp.asarray(high), jnp.asarray(low)
     table = jnp.asarray(edge_weights())
-    th = lax.axis_index("th")
-    main = th % NF
-    half = jnp.where(th < 16, main, jnp.where(th < 26, NF, 0))
-    which = jnp.stack([th % 2, main, half, N_TH - 1 - th]).astype(jnp.int32)
-
     sent = inner_part(density, velocity, pressure)
     received = transposed(sent, SEND_ROWS)
 
-    near_row, far_row, columns = edges(which, density, velocity, pressure)
+    near_row, far_row, columns = edges(density, velocity, pressure)
     th_far = lax.ppermute(far_row, "th", pairs(N_TH, 1))
     th_near = lax.ppermute(near_row, "th", pairs(N_TH, 0))
 
-    rest, matrices = outer_part(which, high, low, table, density, velocity, pressure)
-    back, to_next, to_last = filtered(received, matrices, columns)
-    to_next, to_last, th_far, th_near = lax.optimization_barrier((to_next, to_last, th_far, th_near))
+    rest, matrices, weights = outer_part(high, low, table, density, velocity, pressure)
+    back, up, down = filtered(received, matrices, weights, columns)
+    up, down, th_far, th_near = lax.optimization_barrier((up, down, th_far, th_near))
     returned = transposed(back, BACK_ROWS)
     size = lax.axis_size("gz")
-    before = lax.ppermute(to_next, "gz", [(i, (i + 1) % size) for i in range(size)])
-    after = lax.ppermute(to_last, "gz", [(i, (i - 1) % size) for i in range(size)])
+    before = lax.ppermute(up, "gz", [(i, (i + 1) % size) for i in range(size)])
+    after = lax.ppermute(down, "gz", [(i, (i - 1) % size) for i in range(size)])
     return finish(returned, before, after, rest, th_near, th_far)
 
 

time: 56.5 us -> 56.3 us (level)
  Pallas kernels: 9.39 us -> 8.42 us
  waiting for transfers between devices: 1.24 us -> 1.84 us
    pallas_call x3, Pallas kernels: 5.27 us -> 4.24 us  [the longest x1 1.87 us: outer_part(): pl.pallas_call(outer_kernel, in_specs=[pl.BlockSpec(memory_space=pl.ANY)]...]
    all_to_all x2, waiting for transfers between devices: 0.01 us -> 0.95 us  [transposed(): lax.all_to_all(value, 'th', 0, 0, tiled=True, axis_index_groups=[group])]
  transfers between devices with their start and end apart: 6 -> 6, of which waited for: 2 -> 2; matrix products, arithmetic and copies ran while one was open for 0% -> 0% of each run, Pallas kernels for 9% -> 8%
where the time goes in v4:
time: 56.3 us; the launch traced here: 55.9 us
  starting transfers between devices  45.5 us (81%)
  Pallas kernels  8.42 us (15%)
  waiting for transfers between devices  1.84 us (3%)
    all_to_all x2, starting transfers between devices, transposed(): lax.all_to_all(value, 'th', 0, 0, tiled=True, axis_index_groups=[group])  31.7 us
    ppermute x1, starting transfers between devices, per_device(): after = lax.ppermute(down, 'gz', [(i, (i - 1) % size) for i in range(size)])  6.34 us
    ppermute x1, starting transfers between devices, per_device(): before = lax.ppermute(up, 'gz', [(i, (i + 1) % size) for i in range(size)])  3 us
    ppermute x1, starting transfers between devices, per_device(): th_far = lax.ppermute(far_row, 'th', pairs(N_TH, 1))  2.44 us
    pallas_call x1, Pallas kernels, inner_part(): pl.pallas_call(inner_kernel, grid=(1,), in_specs=[pl.BlockSpec((SECTOR, 1...  2.21 us
    ppermute x1, starting transfers between devices, per_device(): th_near = lax.ppermute(near_row, 'th', pairs(N_TH, 0))  2.03 us
    pallas_call x1, Pallas kernels, finish(): pl.pallas_call(finish_kernel, in_specs=[WHOLE] * 4 + [pl.BlockSpec(memory...  1.97 us
    pallas_call x1, Pallas kernels, outer_part(): pl.pallas_call(outer_kernel, in_specs=[pl.BlockSpec(memory_space=pl.ANY)]...  1.87 us
  transfers between devices with their start and end apart: 6, of which 2 were waited for; matrix products, arithmetic and copies ran while one was open for 0% of the time, Pallas kernels for 8%

profile of v4, /device:TPU:1, one launch (start us, length us, event | category | flops | bytes accessed | tf_op | source)
XLA Modules:
  0.0 55.9 jit_solution(2820451372349885748)
XLA Ops:
  0.0 0.0 copy-start.2
  0.0 0.0 copy-start
  0.0 0.0 copy-start.1
  0.0 2.2 %inner_part.1 = f32[640,128]{1,0:T(8,128)} custom-call(f32[8,64,128]{2,1,0:T(8,128)} %d_ref.5, f32[3,8,64,128]{3,2,1,0:T(8,128)} %v_ref.5, f32[8,64,128]{2,1,0:T(8,128)} %p_ref.5), custom_call_target="tpu_custom_call" | custom-call | flops 1638400 | bytes 600000 | tf_op jit(solution)/shard_map/inner_part/pallas_call | solution.py:210
  2.2 19.0 %all-to-all-start = ((f32[32,5,4,128]{3,2,1,0:T(4,128)}), f32[32,5,4,128]{3,2,1,0:T(4,128)S(1)}, u32[]{:S(2)}, u32[]{:S(2)}) async-start(f32[32,5,4,128]{3,2,1,0:T(4,128)} %bitcast), calls=%async_computation | async-start | bytes 655360 | tf_op jit(solution)/shard_map/all_to_all | solution.py:560
  21.2 0.0 copy-done.2
  21.2 0.0 copy-done
  21.2 0.0 copy-done.1
  21.2 1.2 %edges.1 = (f32[11,64,128]{2,1,0:T(8,128)}, f32[11,64,128]{2,1,0:T(8,128)}, f32[64,128]{1,0:T(8,128)S(1)}) custom-call(f32[8,64,128]{2,1,0:T(8,128)S(1)} %copy-done.1, f32[3,8,64,128]{3,2,1,0:T(8,128)S(1)} %copy-done, f32[8,64,128]{2,1,0:T(8,128)S(1)} %copy-done.2), custom_call_target="tpu_custom_call" | custom-call | flops 983040 | bytes 1800000 | tf_op jit(solution)/shard_map/edges/pallas_call | solution.py:249
  22.4 2.4 %collective-permute-start = (f32[11,64,128]{2,1,0:T(8,128)}, f32[11,64,128]{2,1,0:T(8,128)}, u32[]{:S(2)}, u32[]{:S(2)}) collective-permute-start(f32[11,64,128]{2,1,0:T(8,128)} %get-tuple-element.24), channel_id=1, source_target_pairs={{0,31},{1,2},{2,1},{3,4},{4,3},{5,6},{6,5},{7,8},{8,7},{9,10},{10,... | collective-permute-start | bytes 1081352 | tf_op jit(solution)/shard_map/ppermute | solution.py:572
  24.9 2.0 %collective-permute-start.1 = (f32[11,64,128]{2,1,0:T(8,128)}, f32[11,64,128]{2,1,0:T(8,128)}, u32[]{:S(2)}, u32[]{:S(2)}) collective-permute-start(f32[11,64,128]{2,1,0:T(8,128)} %get-tuple-element.25), channel_id=1, source_target_pairs={{0,1},{1,0},{2,3},{3,2},{4,5},{5,4},{6,7},{7,6},{8,9},{9,8},{10,11... | collective-permute-start | bytes 1081352 | tf_op jit(solution)/shard_map/ppermute | solution.py:573
  26.9 1.9 %outer_part.1 = (f32[2240,128]{1,0:T(8,128)S(1)}, bf16[4,256,256]{2,1,0:T(8,128)(2,1)S(1)}, f32[256,128]{1,0:T(8,128)S(1)}) custom-call(bf16[9,256,256]{2,1,0:T(8,128)(2,1)} %constant.6.clone.high_ref, bf16[9,256,256]{2,1,0:T(8,128)(2,1)} %constant.7.clone.low_ref, f32[512,128]{1,0:T(8,128)} %constant.8.clone.table_ref, f32[8,64,128]{2,1,0:T(8,128)S(1)} %copy-done.1, ...), custom_call_target="tpu_custom_call" | custom-call | flops 16384000 | bytes 3000000 | tf_op jit(solution)/shard_map/outer_part/pallas_call | solution.py:433
  28.8 0.9 %all-to-all-done = f32[32,5,4,128]{3,2,1,0:T(4,128)S(1)} async-done(((f32[32,5,4,128]{3,2,1,0:T(4,128)}), f32[32,5,4,128]{3,2,1,0:T(4,128)S(1)}, u32[]{:S(2)}, u32[]{:S(2)}) %all-to-all-start) | async-done | bytes 327712 | tf_op jit(solution)/shard_map/all_to_all | solution.py:560
  29.7 1.2 %filtered.1 = (f32[384,128]{1,0:T(8,128)}, f32[40,128]{1,0:T(8,128)S(1)}, f32[40,128]{1,0:T(8,128)S(1)}) custom-call(f32[640,128]{1,0:T(8,128)S(1)} %bitcast.4, bf16[4,256,256]{2,1,0:T(8,128)(2,1)S(1)} %get-tuple-element.18.w_ref, f32[256,128]{1,0:T(8,128)S(1)} %get-tuple-element.19.weights_ref, f32[64,128]{1,0:T(8,128)S(1)} %get-tuple-element.20.columns_ref), custom_call_target="tpu_custom_call" | custom-call | flops 100663296 | bytes 1200000 | tf_op jit(solution)/shard_map/filtered/pallas_call | solution.py:339
  30.9 12.7 %all-to-all-start.1 = ((f32[32,3,4,128]{3,2,1,0:T(4,128)}), f32[32,3,4,128]{3,2,1,0:T(4,128)S(1)}, u32[]{:S(2)}, u32[]{:S(2)}) async-start(f32[32,3,4,128]{3,2,1,0:T(4,128)} %bitcast.2), calls=%async_computation.1 | async-start | bytes 393216 | tf_op jit(solution)/shard_map/all_to_all | solution.py:560
  43.6 0.0 collective-permute-done.back_ref
  43.6 0.0 collective-permute-done.1.side_ref
  43.7 3.0 %collective-permute-start.2 = (f32[40,128]{1,0:T(8,128)S(1)}, f32[40,128]{1,0:T(8,128)S(1)}, u32[]{:S(2)}, u32[]{:S(2)}) collective-permute-start(f32[40,128]{1,0:T(8,128)S(1)} %get-tuple-element.26), channel_id=1, source_target_pairs={{0,32},{32,64},{64,96},{96,128},{128,160},{160,192},{192,224},{224... | collective-permute-start | bytes 61448 | tf_op jit(solution)/shard_map/ppermute | solution.py:580
  46.7 6.3 %collective-permute-start.3 = (f32[40,128]{1,0:T(8,128)S(1)}, f32[40,128]{1,0:T(8,128)S(1)}, u32[]{:S(2)}, u32[]{:S(2)}) collective-permute-start(f32[40,128]{1,0:T(8,128)S(1)} %get-tuple-element.27), channel_id=1, source_target_pairs={{0,480},{32,0},{64,32},{96,64},{128,96},{160,128},{192,160},{224,1... | collective-permute-start | bytes 61448 | tf_op jit(solution)/shard_map/ppermute | solution.py:581
  53.0 0.0 collective-permute-done.2.before_ref
  53.0 0.9 %collective-permute-done.3.after_ref = f32[40,128]{1,0:T(8,128)S(1)} collective-permute-done((f32[40,128]{1,0:T(8,128)S(1)}, f32[40,128]{1,0:T(8,128)S(1)}, u32[]{:S(2)}, u32[]{:S(2)}) %collective-permute-start.3) | collective-permute-done | bytes 20512 | tf_op jit(solution)/shard_map/ppermute | solution.py:581
  53.9 0.0 all-to-all-done.1
  53.9 2.0 %finish.1 = f32[5,8,64,128]{3,2,1,0:T(8,128)} custom-call(f32[384,128]{1,0:T(8,128)S(1)} %bitcast.5, f32[40,128]{1,0:T(8,128)S(1)} %collective-permute-done.2.before_ref, f32[40,128]{1,0:T(8,128)S(1)} %collective-permute-done.3.after_ref, f32[2240,128]{1,0:T(8,128)S(1)} %get-tuple-element.28.rest_ref, f32[11,64,128]{2,1,0:T(8,128)} %collective-permute-done.1.side_ref, ...), custom_call_target="tpu_custom_call" | custom-call | flops 409600 | bytes 3000000 | tf_op jit(solution)/shard_map/finish/pallas_call | solution.py:533
Async XLA Ops:
  0.0 21.2 %copy-start.2 = (f32[8,64,128]{2,1,0:T(8,128)S(1)}, f32[8,64,128]{2,1,0:T(8,128)}, u32[]{:S(2)}) copy-start(f32[8,64,128]{2,1,0:T(8,128)} %p_ref.5) | copy-start | bytes 786436
  0.0 21.2 %copy-start = (f32[3,8,64,128]{3,2,1,0:T(8,128)S(1)}, f32[3,8,64,128]{3,2,1,0:T(8,128)}, u32[]{:S(2)}) copy-start(f32[3,8,64,128]{3,2,1,0:T(8,128)} %v_ref.5) | copy-start | bytes 2359300
  0.0 21.2 %copy-start.1 = (f32[8,64,128]{2,1,0:T(8,128)S(1)}, f32[8,64,128]{2,1,0:T(8,128)}, u32[]{:S(2)}) copy-start(f32[8,64,128]{2,1,0:T(8,128)} %d_ref.5) | copy-start | bytes 786436
  2.2 27.5 %all-to-all-start = ((f32[32,5,4,128]{3,2,1,0:T(4,128)}), f32[32,5,4,128]{3,2,1,0:T(4,128)S(1)}, u32[]{:S(2)}, u32[]{:S(2)}) async-start(f32[32,5,4,128]{3,2,1,0:T(4,128)} %bitcast), calls=%async_computation | async-start | bytes 655360 | tf_op jit(solution)/shard_map/all_to_all | solution.py:560
  22.4 21.2 %collective-permute-start = (f32[11,64,128]{2,1,0:T(8,128)}, f32[11,64,128]{2,1,0:T(8,128)}, u32[]{:S(2)}, u32[]{:S(2)}) collective-permute-start(f32[11,64,128]{2,1,0:T(8,128)} %get-tuple-element.24), channel_id=1, source_target_pairs={{0,31},{1,2},{2,1},{3,4},{4,3},{5,6},{6,5},{7,8},{8,7},{9,10},{10,... | collective-permute-start | bytes 1081352 | tf_op jit(solution)/shard_map/ppermute | solution.py:572
  24.9 18.8 %collective-permute-start.1 = (f32[11,64,128]{2,1,0:T(8,128)}, f32[11,64,128]{2,1,0:T(8,128)}, u32[]{:S(2)}, u32[]{:S(2)}) collective-permute-start(f32[11,64,128]{2,1,0:T(8,128)} %get-tuple-element.25), channel_id=1, source_target_pairs={{0,1},{1,0},{2,3},{3,2},{4,5},{5,4},{6,7},{7,6},{8,9},{9,8},{10,11... | collective-permute-start | bytes 1081352 | tf_op jit(solution)/shard_map/ppermute | solution.py:573
  30.9 23.0 %all-to-all-start.1 = ((f32[32,3,4,128]{3,2,1,0:T(4,128)}), f32[32,3,4,128]{3,2,1,0:T(4,128)S(1)}, u32[]{:S(2)}, u32[]{:S(2)}) async-start(f32[32,3,4,128]{3,2,1,0:T(4,128)} %bitcast.2), calls=%async_computation.1 | async-start | bytes 393216 | tf_op jit(solution)/shard_map/all_to_all | solution.py:560
  43.7 9.4 %collective-permute-start.2 = (f32[40,128]{1,0:T(8,128)S(1)}, f32[40,128]{1,0:T(8,128)S(1)}, u32[]{:S(2)}, u32[]{:S(2)}) collective-permute-start(f32[40,128]{1,0:T(8,128)S(1)} %get-tuple-element.26), channel_id=1, source_target_pairs={{0,32},{32,64},{64,96},{96,128},{128,160},{160,192},{192,224},{224... | collective-permute-start | bytes 61448 | tf_op jit(solution)/shard_map/ppermute | solution.py:580
  46.7 7.2 %collective-permute-start.3 = (f32[40,128]{1,0:T(8,128)S(1)}, f32[40,128]{1,0:T(8,128)S(1)}, u32[]{:S(2)}, u32[]{:S(2)}) collective-permute-start(f32[40,128]{1,0:T(8,128)S(1)} %get-tuple-element.27), channel_id=1, source_target_pairs={{0,480},{32,0},{64,32},{96,64},{128,96},{160,128},{192,160},{224,1... | collective-permute-start | bytes 61448 | tf_op jit(solution)/shard_map/ppermute | solution.py:581

commit v5 on v4

--- a/solution.py
+++ b/solution.py
@@ -22,7 +22,8 @@
 BLOCK_ROWS = FIELDS * SECTOR * OUTER
 PACK_ROWS = SECTOR + NR // 2
 UP_ROWS, DOWN_ROWS = 0, 0
-FIRST = 24
+ORDER = [(23 + n) % N_TH for n in range(N_TH)]
+BACK_ORDER = [(16 + n) % N_TH for n in range(N_TH)]
 ROW_FIELDS = 11
 
 HALF_STEP = 0.125
@@ -80,8 +81,8 @@
     return parts
 
 
-def slot(sector):
-    return (sector - FIRST) % N_TH
+def slot(sector, order):
+    return order.index(sector)
 
 
 def lanes_of(shape):
@@ -118,7 +119,7 @@
         return (rows(d_rows, 0), *[rows(v_rows, n * size) for n in range(3)], rows(p_rows, 0))
 
     def store(unit, row, value):
-        start = slot(unit) * SEND_ROWS + row
+        start = slot(unit, ORDER) * SEND_ROWS + row
         out_ref[start : start + value.shape[0], :] = value
 
     shape = (SECTOR, LANES)
@@ -269,7 +270,7 @@
 def filter_kernel(r_ref, w_ref, weights_ref, columns_ref, out_ref, up_ref, down_ref):
     shape = (N_TH, SECTOR, LANES)
     row, lane = rows_of(shape), lanes_of(shape)
-    starts = [slot(s) * SEND_ROWS for s in range(N_TH)]
+    starts = [slot(s, ORDER) * SEND_ROWS for s in range(N_TH)]
     main = jnp.stack([r_ref[a : a + 8, :] for a in starts])
     extra = jnp.stack([r_ref[a + 8 : a + 16, :] for a in starts])
     zero = jnp.zeros(shape, jnp.float32)
@@ -302,7 +303,7 @@
     packed = jnp.where(lane < 64, half, spread(spread(half, 64, 2), 4, 1))
     sums = [jnp.zeros((SECTOR, LANES), jnp.float32) for _ in range(FIELDS)]
     for s in range(N_TH):
-        base, start = slot(s) * BACK_ROWS, starts[s]
+        base, start = slot(s, BACK_ORDER) * BACK_ROWS, starts[s]
         out_ref[base : base + 8, :] = main[s]
         out_ref[base + 8 : base + 12, :] = packed[s, :4]
         weights = weights_ref[SECTOR * s : SECTOR * (s + 1), :]
@@ -493,7 +494,7 @@
     tiles = buffer.reshape(FIELDS * SECTOR * NR, LANES)
 
     def joined(unit_a, unit_b):
-        start_a, start_b = slot(unit_a) * BACK_ROWS + 8, slot(unit_b) * BACK_ROWS + 8
+        start_a, start_b = (slot(unit, BACK_ORDER) * BACK_ROWS + 8 for unit in (unit_a, unit_b))
         a, b = r_ref[start_a : start_a + 4, :], r_ref[start_b : start_b + 4, :]
         top = jnp.where(low_half, a, spread(b, 64, 1))
         bottom = jnp.where(low_half, spread(a, 64, 1), b)
@@ -502,7 +503,7 @@
     for f in range(FIELDS):
         for cycle in range(NF):
             if f < 4:
-                start = slot(f * NF + cycle) * BACK_ROWS
+                start = slot(f * NF + cycle, BACK_ORDER) * BACK_ROWS
                 tile = r_ref[start : start + 8, :]
             else:
                 tile = joined(cycle, NF + cycle)
@@ -554,10 +555,9 @@
     return [(i, (((i - offset) ^ 1) + offset) % size) for i in range(size)]
 
 
-def transposed(value, rows):
+def transposed(value, rows, order):
     value = value.reshape(N_TH, rows // 4, 4, LANES)
-    group = [(FIRST + k) % N_TH for k in range(N_TH)]
-    value = lax.all_to_all(value, "th", 0, 0, tiled=True, axis_index_groups=[group])
+    value = lax.all_to_all(value, "th", 0, 0, tiled=True, axis_index_groups=[order])
     return value.reshape(N_TH * rows, LANES)
 
 
@@ -566,7 +566,7 @@
     high, low = jnp.asarray(high), jnp.asarray(low)
     table = jnp.asarray(edge_weights())
     sent = inner_part(density, velocity, pressure)
-    received = transposed(sent, SEND_ROWS)
+    received = transposed(sent, SEND_ROWS, ORDER)
 
     near_row, far_row, columns = edges(density, velocity, pressure)
     th_far = lax.ppermute(far_row, "th", pairs(N_TH, 1))
@@ -575,7 +575,7 @@
     rest, matrices, weights = outer_part(high, low, table, density, velocity, pressure)
     back, up, down = filtered(received, matrices, weights, columns)
     up, down, th_far, th_near = lax.optimization_barrier((up, down, th_far, th_near))
-    returned = transposed(back, BACK_ROWS)
+    returned = transposed(back, BACK_ROWS, BACK_ORDER)
     size = lax.axis_size("gz")
     before = lax.ppermute(up, "gz", [(i, (i + 1) % size) for i in range(size)])
     after = lax.ppermute(down, "gz", [(i, (i - 1) % size) for i in range(size)])

time: 56.3 us -> 54.3 us (0.964)
  starting transfers between devices: 45.5 us -> 43.6 us
    all_to_all x2, starting transfers between devices: 31.7 us -> 27.8 us  [transposed(): lax.all_to_all(value, 'th', 0, 0, tiled=True, axis_index_groups=[order])]
    ppermute x1, starting transfers between devices: 2.03 us -> 4.17 us  [per_device(): th_near = lax.ppermute(near_row, 'th', pairs(N_TH, 0))]
where the time goes in v5:
time: 54.3 us; the launch traced here: 53.9 us
  starting transfers between devices  43.6 us (80%)
  Pallas kernels  8.42 us (16%)
  waiting for transfers between devices  1.76 us (3%)
    all_to_all x2, starting transfers between devices, transposed(): lax.all_to_all(value, 'th', 0, 0, tiled=True, axis_index_groups=[order])  27.8 us
    ppermute x1, starting transfers between devices, per_device(): after = lax.ppermute(down, 'gz', [(i, (i - 1) % size) for i in range(size)])  6.09 us
    ppermute x1, starting transfers between devices, per_device(): th_near = lax.ppermute(near_row, 'th', pairs(N_TH, 0))  4.17 us
    ppermute x1, starting transfers between devices, per_device(): before = lax.ppermute(up, 'gz', [(i, (i + 1) % size) for i in range(size)])  3.1 us
    ppermute x1, starting transfers between devices, per_device(): th_far = lax.ppermute(far_row, 'th', pairs(N_TH, 1))  2.43 us
    pallas_call x1, Pallas kernels, inner_part(): pl.pallas_call(inner_kernel, grid=(1,), in_specs=[pl.BlockSpec((SECTOR, 1...  2.21 us
    pallas_call x1, Pallas kernels, finish(): pl.pallas_call(finish_kernel, in_specs=[WHOLE] * 4 + [pl.BlockSpec(memory...  1.97 us
    pallas_call x1, Pallas kernels, outer_part(): pl.pallas_call(outer_kernel, in_specs=[pl.BlockSpec(memory_space=pl.ANY)]...  1.87 us
  transfers between devices with their start and end apart: 6, of which 2 were waited for; matrix products, arithmetic and copies ran while one was open for 0% of the time, Pallas kernels for 8%

profile of v5, /device:TPU:1, one launch (start us, length us, event | category | flops | bytes accessed | tf_op | source)
XLA Modules:
  0.0 53.9 jit_solution(3328683411887416728)
XLA Ops:
  0.0 0.0 copy-start.2
  0.0 0.0 copy-start
  0.0 0.0 copy-start.1
  0.0 2.2 %inner_part.1 = f32[640,128]{1,0:T(8,128)} custom-call(f32[8,64,128]{2,1,0:T(8,128)} %d_ref.5, f32[3,8,64,128]{3,2,1,0:T(8,128)} %v_ref.5, f32[8,64,128]{2,1,0:T(8,128)} %p_ref.5), custom_call_target="tpu_custom_call" | custom-call | flops 1638400 | bytes 600000 | tf_op jit(solution)/shard_map/inner_part/pallas_call | solution.py:211
  2.2 17.5 %all-to-all-start = ((f32[32,5,4,128]{3,2,1,0:T(4,128)}), f32[32,5,4,128]{3,2,1,0:T(4,128)S(1)}, u32[]{:S(2)}, u32[]{:S(2)}) async-start(f32[32,5,4,128]{3,2,1,0:T(4,128)} %bitcast), calls=%async_computation | async-start | bytes 655360 | tf_op jit(solution)/shard_map/all_to_all | solution.py:560
  19.7 0.0 copy-done.2
  19.7 0.0 copy-done
  19.7 0.0 copy-done.1
  19.7 1.2 %edges.1 = (f32[11,64,128]{2,1,0:T(8,128)}, f32[11,64,128]{2,1,0:T(8,128)}, f32[64,128]{1,0:T(8,128)S(1)}) custom-call(f32[8,64,128]{2,1,0:T(8,128)S(1)} %copy-done.1, f32[3,8,64,128]{3,2,1,0:T(8,128)S(1)} %copy-done, f32[8,64,128]{2,1,0:T(8,128)S(1)} %copy-done.2), custom_call_target="tpu_custom_call" | custom-call | flops 983040 | bytes 1800000 | tf_op jit(solution)/shard_map/edges/pallas_call | solution.py:250
  20.9 2.4 %collective-permute-start = (f32[11,64,128]{2,1,0:T(8,128)}, f32[11,64,128]{2,1,0:T(8,128)}, u32[]{:S(2)}, u32[]{:S(2)}) collective-permute-start(f32[11,64,128]{2,1,0:T(8,128)} %get-tuple-element.24), channel_id=1, source_target_pairs={{0,31},{1,2},{2,1},{3,4},{4,3},{5,6},{6,5},{7,8},{8,7},{9,10},{10,... | collective-permute-start | bytes 1081352 | tf_op jit(solution)/shard_map/ppermute | solution.py:572
  23.4 4.2 %collective-permute-start.1 = (f32[11,64,128]{2,1,0:T(8,128)}, f32[11,64,128]{2,1,0:T(8,128)}, u32[]{:S(2)}, u32[]{:S(2)}) collective-permute-start(f32[11,64,128]{2,1,0:T(8,128)} %get-tuple-element.25), channel_id=1, source_target_pairs={{0,1},{1,0},{2,3},{3,2},{4,5},{5,4},{6,7},{7,6},{8,9},{9,8},{10,11... | collective-permute-start | bytes 1081352 | tf_op jit(solution)/shard_map/ppermute | solution.py:573
  27.5 1.9 %outer_part.1 = (f32[2240,128]{1,0:T(8,128)S(1)}, bf16[4,256,256]{2,1,0:T(8,128)(2,1)S(1)}, f32[256,128]{1,0:T(8,128)S(1)}) custom-call(bf16[9,256,256]{2,1,0:T(8,128)(2,1)} %constant.6.clone.high_ref, bf16[9,256,256]{2,1,0:T(8,128)(2,1)} %constant.7.clone.low_ref, f32[512,128]{1,0:T(8,128)} %constant.8.clone.table_ref, f32[8,64,128]{2,1,0:T(8,128)S(1)} %copy-done.1, ...), custom_call_target="tpu_custom_call" | custom-call | flops 16384000 | bytes 3000000 | tf_op jit(solution)/shard_map/outer_part/pallas_call | solution.py:434
  29.4 0.9 %all-to-all-done = f32[32,5,4,128]{3,2,1,0:T(4,128)S(1)} async-done(((f32[32,5,4,128]{3,2,1,0:T(4,128)}), f32[32,5,4,128]{3,2,1,0:T(4,128)S(1)}, u32[]{:S(2)}, u32[]{:S(2)}) %all-to-all-start) | async-done | bytes 327712 | tf_op jit(solution)/shard_map/all_to_all | solution.py:560
  30.3 1.2 %filtered.1 = (f32[384,128]{1,0:T(8,128)}, f32[40,128]{1,0:T(8,128)S(1)}, f32[40,128]{1,0:T(8,128)S(1)}) custom-call(f32[640,128]{1,0:T(8,128)S(1)} %bitcast.4, bf16[4,256,256]{2,1,0:T(8,128)(2,1)S(1)} %get-tuple-element.18.w_ref, f32[256,128]{1,0:T(8,128)S(1)} %get-tuple-element.19.weights_ref, f32[64,128]{1,0:T(8,128)S(1)} %get-tuple-element.20.columns_ref), custom_call_target="tpu_custom_call" | custom-call | flops 100663296 | bytes 1200000 | tf_op jit(solution)/shard_map/filtered/pallas_call | solution.py:340
  31.5 10.3 %all-to-all-start.1 = ((f32[32,3,4,128]{3,2,1,0:T(4,128)}), f32[32,3,4,128]{3,2,1,0:T(4,128)S(1)}, u32[]{:S(2)}, u32[]{:S(2)}) async-start(f32[32,3,4,128]{3,2,1,0:T(4,128)} %bitcast.2), calls=%async_computation.1 | async-start | bytes 393216 | tf_op jit(solution)/shard_map/all_to_all | solution.py:560
  41.8 0.0 collective-permute-done.back_ref
  41.8 0.0 collective-permute-done.1.side_ref
  41.8 3.1 %collective-permute-start.2 = (f32[40,128]{1,0:T(8,128)S(1)}, f32[40,128]{1,0:T(8,128)S(1)}, u32[]{:S(2)}, u32[]{:S(2)}) collective-permute-start(f32[40,128]{1,0:T(8,128)S(1)} %get-tuple-element.26), channel_id=1, source_target_pairs={{0,32},{32,64},{64,96},{96,128},{128,160},{160,192},{192,224},{224... | collective-permute-start | bytes 61448 | tf_op jit(solution)/shard_map/ppermute | solution.py:580
  44.9 6.1 %collective-permute-start.3 = (f32[40,128]{1,0:T(8,128)S(1)}, f32[40,128]{1,0:T(8,128)S(1)}, u32[]{:S(2)}, u32[]{:S(2)}) collective-permute-start(f32[40,128]{1,0:T(8,128)S(1)} %get-tuple-element.27), channel_id=1, source_target_pairs={{0,480},{32,0},{64,32},{96,64},{128,96},{160,128},{192,160},{224,1... | collective-permute-start | bytes 61448 | tf_op jit(solution)/shard_map/ppermute | solution.py:581
  51.0 0.0 collective-permute-done.2.before_ref
  51.0 0.9 %collective-permute-done.3.after_ref = f32[40,128]{1,0:T(8,128)S(1)} collective-permute-done((f32[40,128]{1,0:T(8,128)S(1)}, f32[40,128]{1,0:T(8,128)S(1)}, u32[]{:S(2)}, u32[]{:S(2)}) %collective-permute-start.3) | collective-permute-done | bytes 20512 | tf_op jit(solution)/shard_map/ppermute | solution.py:581
  51.9 0.0 all-to-all-done.1
  51.9 2.0 %finish.1 = f32[5,8,64,128]{3,2,1,0:T(8,128)} custom-call(f32[384,128]{1,0:T(8,128)S(1)} %bitcast.5, f32[40,128]{1,0:T(8,128)S(1)} %collective-permute-done.2.before_ref, f32[40,128]{1,0:T(8,128)S(1)} %collective-permute-done.3.after_ref, f32[2240,128]{1,0:T(8,128)S(1)} %get-tuple-element.28.rest_ref, f32[11,64,128]{2,1,0:T(8,128)} %collective-permute-done.1.side_ref, ...), custom_call_target="tpu_custom_call" | custom-call | flops 409600 | bytes 3000000 | tf_op jit(solution)/shard_map/finish/pallas_call | solution.py:534
Async XLA Ops:
  0.0 19.7 %copy-start.2 = (f32[8,64,128]{2,1,0:T(8,128)S(1)}, f32[8,64,128]{2,1,0:T(8,128)}, u32[]{:S(2)}) copy-start(f32[8,64,128]{2,1,0:T(8,128)} %p_ref.5) | copy-start | bytes 786436
  0.0 19.7 %copy-start = (f32[3,8,64,128]{3,2,1,0:T(8,128)S(1)}, f32[3,8,64,128]{3,2,1,0:T(8,128)}, u32[]{:S(2)}) copy-start(f32[3,8,64,128]{3,2,1,0:T(8,128)} %v_ref.5) | copy-start | bytes 2359300
  0.0 19.7 %copy-start.1 = (f32[8,64,128]{2,1,0:T(8,128)S(1)}, f32[8,64,128]{2,1,0:T(8,128)}, u32[]{:S(2)}) copy-start(f32[8,64,128]{2,1,0:T(8,128)} %d_ref.5) | copy-start | bytes 786436
  2.2 28.1 %all-to-all-start = ((f32[32,5,4,128]{3,2,1,0:T(4,128)}), f32[32,5,4,128]{3,2,1,0:T(4,128)S(1)}, u32[]{:S(2)}, u32[]{:S(2)}) async-start(f32[32,5,4,128]{3,2,1,0:T(4,128)} %bitcast), calls=%async_computation | async-start | bytes 655360 | tf_op jit(solution)/shard_map/all_to_all | solution.py:560
  20.9 20.9 %collective-permute-start = (f32[11,64,128]{2,1,0:T(8,128)}, f32[11,64,128]{2,1,0:T(8,128)}, u32[]{:S(2)}, u32[]{:S(2)}) collective-permute-start(f32[11,64,128]{2,1,0:T(8,128)} %get-tuple-element.24), channel_id=1, source_target_pairs={{0,31},{1,2},{2,1},{3,4},{4,3},{5,6},{6,5},{7,8},{8,7},{9,10},{10,... | collective-permute-start | bytes 1081352 | tf_op jit(solution)/shard_map/ppermute | solution.py:572
  23.4 18.5 %collective-permute-start.1 = (f32[11,64,128]{2,1,0:T(8,128)}, f32[11,64,128]{2,1,0:T(8,128)}, u32[]{:S(2)}, u32[]{:S(2)}) collective-permute-start(f32[11,64,128]{2,1,0:T(8,128)} %get-tuple-element.25), channel_id=1, source_target_pairs={{0,1},{1,0},{2,3},{3,2},{4,5},{5,4},{6,7},{7,6},{8,9},{9,8},{10,11... | collective-permute-start | bytes 1081352 | tf_op jit(solution)/shard_map/ppermute | solution.py:573
  31.5 20.5 %all-to-all-start.1 = ((f32[32,3,4,128]{3,2,1,0:T(4,128)}), f32[32,3,4,128]{3,2,1,0:T(4,128)S(1)}, u32[]{:S(2)}, u32[]{:S(2)}) async-start(f32[32,3,4,128]{3,2,1,0:T(4,128)} %bitcast.2), calls=%async_computation.1 | async-start | bytes 393216 | tf_op jit(solution)/shard_map/all_to_all | solution.py:560
  41.8 9.2 %collective-permute-start.2 = (f32[40,128]{1,0:T(8,128)S(1)}, f32[40,128]{1,0:T(8,128)S(1)}, u32[]{:S(2)}, u32[]{:S(2)}) collective-permute-start(f32[40,128]{1,0:T(8,128)S(1)} %get-tuple-element.26), channel_id=1, source_target_pairs={{0,32},{32,64},{64,96},{96,128},{128,160},{160,192},{192,224},{224... | collective-permute-start | bytes 61448 | tf_op jit(solution)/shard_map/ppermute | solution.py:580
  44.9 7.0 %collective-permute-start.3 = (f32[40,128]{1,0:T(8,128)S(1)}, f32[40,128]{1,0:T(8,128)S(1)}, u32[]{:S(2)}, u32[]{:S(2)}) collective-permute-start(f32[40,128]{1,0:T(8,128)S(1)} %get-tuple-element.27), channel_id=1, source_target_pairs={{0,480},{32,0},{64,32},{96,64},{128,96},{160,128},{192,160},{224,1... | collective-permute-start | bytes 61448 | tf_op jit(solution)/shard_map/ppermute | solution.py:581

commit v6 on v5

--- a/solution.py
+++ b/solution.py
@@ -106,17 +106,11 @@
     return first[:4], second[:4]
 
 
-def inner_kernel(d_ref, v_ref, p_ref, out_ref):
-    size = 16 * SECTOR
-    d_rows, v_rows, p_rows = (
-        d_ref.reshape(size, LANES), v_ref.reshape(3 * size, LANES), p_ref.reshape(size, LANES)
-    )
+def inner_kernel(d_ref, u_ref, w_ref, v_ref, p_ref, out_ref):
+    flat = [ref.reshape(16 * SECTOR, LANES) for ref in (d_ref, u_ref, w_ref, v_ref, p_ref)]
 
     def load(cycle):
-        def rows(ref, first):
-            return ref[pl.ds(first + cycle, SECTOR, stride=16), :]
-
-        return (rows(d_rows, 0), *[rows(v_rows, n * size) for n in range(3)], rows(p_rows, 0))
+        return [ref[pl.ds(cycle, SECTOR, stride=16), :] for ref in flat]
 
     def store(unit, row, value):
         start = slot(unit, ORDER) * SEND_ROWS + row
@@ -213,7 +207,7 @@
         grid=(1,),
         in_specs=[
             pl.BlockSpec((SECTOR, 16, LANES), lambda i: (0, 0, 0)),
-            pl.BlockSpec((3, SECTOR, 16, LANES), lambda i: (0, 0, 0, 0)),
+            *[pl.BlockSpec((None, SECTOR, 16, LANES), lambda i, n=n: (n, 0, 0, 0)) for n in range(3)],
             pl.BlockSpec((SECTOR, 16, LANES), lambda i: (0, 0, 0)),
         ],
         out_specs=WHOLE,
@@ -221,7 +215,7 @@
         compiler_params=PARAMS,
         cost_estimate=pl.CostEstimate(flops=8 * 1024 * 200, bytes_accessed=600_000, transcendentals=0),
         name="inner_part",
-    )(in_hbm(density), in_hbm(velocity), in_hbm(pressure))
+    )(in_hbm(density), *[in_hbm(velocity)] * 3, in_hbm(pressure))
 
 
 def edge_kernel(d_ref, v_ref, p_ref, near_ref, far_ref, columns_ref):

time: 54.3 us -> 54.3 us (level)
  no operation moved by 1% of the time
where the time goes in v6:
time: 54.3 us; the launch traced here: 53.9 us
  starting transfers between devices  43.6 us (80%)
  Pallas kernels  8.42 us (16%)
  waiting for transfers between devices  1.76 us (3%)
    all_to_all x2, starting transfers between devices, transposed(): lax.all_to_all(value, 'th', 0, 0, tiled=True, axis_index_groups=[order])  27.8 us
    ppermute x1, starting transfers between devices, per_device(): after = lax.ppermute(down, 'gz', [(i, (i - 1) % size) for i in range(size)])  6.09 us
    ppermute x1, starting transfers between devices, per_device(): th_near = lax.ppermute(near_row, 'th', pairs(N_TH, 0))  4.17 us
    ppermute x1, starting transfers between devices, per_device(): before = lax.ppermute(up, 'gz', [(i, (i + 1) % size) for i in range(size)])  3.1 us
    ppermute x1, starting transfers between devices, per_device(): th_far = lax.ppermute(far_row, 'th', pairs(N_TH, 1))  2.43 us
    pallas_call x1, Pallas kernels, inner_part(): pl.pallas_call(inner_kernel, grid=(1,), in_specs=[pl.BlockSpec((SECTOR, 1...  2.21 us
    pallas_call x1, Pallas kernels, finish(): pl.pallas_call(finish_kernel, in_specs=[WHOLE] * 4 + [pl.BlockSpec(memory...  1.97 us
    pallas_call x1, Pallas kernels, outer_part(): pl.pallas_call(outer_kernel, in_specs=[pl.BlockSpec(memory_space=pl.ANY)]...  1.87 us
  transfers between devices with their start and end apart: 6, of which 2 were waited for; matrix products, arithmetic and copies ran while one was open for 0% of the time, Pallas kernels for 8%

profile of v6, /device:TPU:1, one launch (start us, length us, event | category | flops | bytes accessed | tf_op | source)
XLA Modules:
  0.0 53.9 jit_solution(9405478539461582610)
XLA Ops:
  0.0 0.0 copy-start.2
  0.0 0.0 copy-start
  0.0 0.0 copy-start.1
  0.0 2.2 %inner_part.1 = f32[640,128]{1,0:T(8,128)} custom-call(f32[8,64,128]{2,1,0:T(8,128)} %d_ref.5, f32[3,8,64,128]{3,2,1,0:T(8,128)} %v_ref.5, f32[3,8,64,128]{3,2,1,0:T(8,128)} %v_ref.5, f32[3,8,64,128]{3,2,1,0:T(8,128)} %v_ref.5, f32[8,64,128]{2,1,0:T(8,128)} %p_ref.5), custom_call_target="tpu_custom_call" | custom-call | flops 1638400 | bytes 600000 | tf_op jit(solution)/shard_map/inner_part/pallas_call | solution.py:205
  2.2 17.5 %all-to-all-start = ((f32[32,5,4,128]{3,2,1,0:T(4,128)}), f32[32,5,4,128]{3,2,1,0:T(4,128)S(1)}, u32[]{:S(2)}, u32[]{:S(2)}) async-start(f32[32,5,4,128]{3,2,1,0:T(4,128)} %bitcast), calls=%async_computation | async-start | bytes 655360 | tf_op jit(solution)/shard_map/all_to_all | solution.py:554
  19.7 0.0 copy-done.2
  19.7 0.0 copy-done
  19.7 0.0 copy-done.1
  19.7 1.2 %edges.1 = (f32[11,64,128]{2,1,0:T(8,128)}, f32[11,64,128]{2,1,0:T(8,128)}, f32[64,128]{1,0:T(8,128)S(1)}) custom-call(f32[8,64,128]{2,1,0:T(8,128)S(1)} %copy-done.1, f32[3,8,64,128]{3,2,1,0:T(8,128)S(1)} %copy-done, f32[8,64,128]{2,1,0:T(8,128)S(1)} %copy-done.2), custom_call_target="tpu_custom_call" | custom-call | flops 983040 | bytes 1800000 | tf_op jit(solution)/shard_map/edges/pallas_call | solution.py:244
  20.9 2.4 %collective-permute-start = (f32[11,64,128]{2,1,0:T(8,128)}, f32[11,64,128]{2,1,0:T(8,128)}, u32[]{:S(2)}, u32[]{:S(2)}) collective-permute-start(f32[11,64,128]{2,1,0:T(8,128)} %get-tuple-element.24), channel_id=1, source_target_pairs={{0,31},{1,2},{2,1},{3,4},{4,3},{5,6},{6,5},{7,8},{8,7},{9,10},{10,... | collective-permute-start | bytes 1081352 | tf_op jit(solution)/shard_map/ppermute | solution.py:566
  23.4 4.2 %collective-permute-start.1 = (f32[11,64,128]{2,1,0:T(8,128)}, f32[11,64,128]{2,1,0:T(8,128)}, u32[]{:S(2)}, u32[]{:S(2)}) collective-permute-start(f32[11,64,128]{2,1,0:T(8,128)} %get-tuple-element.25), channel_id=1, source_target_pairs={{0,1},{1,0},{2,3},{3,2},{4,5},{5,4},{6,7},{7,6},{8,9},{9,8},{10,11... | collective-permute-start | bytes 1081352 | tf_op jit(solution)/shard_map/ppermute | solution.py:567
  27.5 1.9 %outer_part.1 = (f32[2240,128]{1,0:T(8,128)S(1)}, bf16[4,256,256]{2,1,0:T(8,128)(2,1)S(1)}, f32[256,128]{1,0:T(8,128)S(1)}) custom-call(bf16[9,256,256]{2,1,0:T(8,128)(2,1)} %constant.6.clone.high_ref, bf16[9,256,256]{2,1,0:T(8,128)(2,1)} %constant.7.clone.low_ref, f32[512,128]{1,0:T(8,128)} %constant.8.clone.table_ref, f32[8,64,128]{2,1,0:T(8,128)S(1)} %copy-done.1, ...), custom_call_target="tpu_custom_call" | custom-call | flops 16384000 | bytes 3000000 | tf_op jit(solution)/shard_map/outer_part/pallas_call | solution.py:428
  29.4 0.9 %all-to-all-done = f32[32,5,4,128]{3,2,1,0:T(4,128)S(1)} async-done(((f32[32,5,4,128]{3,2,1,0:T(4,128)}), f32[32,5,4,128]{3,2,1,0:T(4,128)S(1)}, u32[]{:S(2)}, u32[]{:S(2)}) %all-to-all-start) | async-done | bytes 327712 | tf_op jit(solution)/shard_map/all_to_all | solution.py:554
  30.3 1.2 %filtered.1 = (f32[384,128]{1,0:T(8,128)}, f32[40,128]{1,0:T(8,128)S(1)}, f32[40,128]{1,0:T(8,128)S(1)}) custom-call(f32[640,128]{1,0:T(8,128)S(1)} %bitcast.4, bf16[4,256,256]{2,1,0:T(8,128)(2,1)S(1)} %get-tuple-element.18.w_ref, f32[256,128]{1,0:T(8,128)S(1)} %get-tuple-element.19.weights_ref, f32[64,128]{1,0:T(8,128)S(1)} %get-tuple-element.20.columns_ref), custom_call_target="tpu_custom_call" | custom-call | flops 100663296 | bytes 1200000 | tf_op jit(solution)/shard_map/filtered/pallas_call | solution.py:334
  31.5 10.3 %all-to-all-start.1 = ((f32[32,3,4,128]{3,2,1,0:T(4,128)}), f32[32,3,4,128]{3,2,1,0:T(4,128)S(1)}, u32[]{:S(2)}, u32[]{:S(2)}) async-start(f32[32,3,4,128]{3,2,1,0:T(4,128)} %bitcast.2), calls=%async_computation.1 | async-start | bytes 393216 | tf_op jit(solution)/shard_map/all_to_all | solution.py:554
  41.8 0.0 collective-permute-done.back_ref
  41.8 0.0 collective-permute-done.1.side_ref
  41.8 3.1 %collective-permute-start.2 = (f32[40,128]{1,0:T(8,128)S(1)}, f32[40,128]{1,0:T(8,128)S(1)}, u32[]{:S(2)}, u32[]{:S(2)}) collective-permute-start(f32[40,128]{1,0:T(8,128)S(1)} %get-tuple-element.26), channel_id=1, source_target_pairs={{0,32},{32,64},{64,96},{96,128},{128,160},{160,192},{192,224},{224... | collective-permute-start | bytes 61448 | tf_op jit(solution)/shard_map/ppermute | solution.py:574
  44.9 6.1 %collective-permute-start.3 = (f32[40,128]{1,0:T(8,128)S(1)}, f32[40,128]{1,0:T(8,128)S(1)}, u32[]{:S(2)}, u32[]{:S(2)}) collective-permute-start(f32[40,128]{1,0:T(8,128)S(1)} %get-tuple-element.27), channel_id=1, source_target_pairs={{0,480},{32,0},{64,32},{96,64},{128,96},{160,128},{192,160},{224,1... | collective-permute-start | bytes 61448 | tf_op jit(solution)/shard_map/ppermute | solution.py:575
  51.0 0.0 collective-permute-done.2.before_ref
  51.0 0.9 %collective-permute-done.3.after_ref = f32[40,128]{1,0:T(8,128)S(1)} collective-permute-done((f32[40,128]{1,0:T(8,128)S(1)}, f32[40,128]{1,0:T(8,128)S(1)}, u32[]{:S(2)}, u32[]{:S(2)}) %collective-permute-start.3) | collective-permute-done | bytes 20512 | tf_op jit(solution)/shard_map/ppermute | solution.py:575
  51.9 0.0 all-to-all-done.1
  51.9 2.0 %finish.1 = f32[5,8,64,128]{3,2,1,0:T(8,128)} custom-call(f32[384,128]{1,0:T(8,128)S(1)} %bitcast.5, f32[40,128]{1,0:T(8,128)S(1)} %collective-permute-done.2.before_ref, f32[40,128]{1,0:T(8,128)S(1)} %collective-permute-done.3.after_ref, f32[2240,128]{1,0:T(8,128)S(1)} %get-tuple-element.28.rest_ref, f32[11,64,128]{2,1,0:T(8,128)} %collective-permute-done.1.side_ref, ...), custom_call_target="tpu_custom_call" | custom-call | flops 409600 | bytes 3000000 | tf_op jit(solution)/shard_map/finish/pallas_call | solution.py:528
Async XLA Ops:
  0.0 19.7 %copy-start.2 = (f32[8,64,128]{2,1,0:T(8,128)S(1)}, f32[8,64,128]{2,1,0:T(8,128)}, u32[]{:S(2)}) copy-start(f32[8,64,128]{2,1,0:T(8,128)} %p_ref.5) | copy-start | bytes 786436
  0.0 19.7 %copy-start = (f32[3,8,64,128]{3,2,1,0:T(8,128)S(1)}, f32[3,8,64,128]{3,2,1,0:T(8,128)}, u32[]{:S(2)}) copy-start(f32[3,8,64,128]{3,2,1,0:T(8,128)} %v_ref.5) | copy-start | bytes 2359300
  0.0 19.7 %copy-start.1 = (f32[8,64,128]{2,1,0:T(8,128)S(1)}, f32[8,64,128]{2,1,0:T(8,128)}, u32[]{:S(2)}) copy-start(f32[8,64,128]{2,1,0:T(8,128)} %d_ref.5) | copy-start | bytes 786436
  2.2 28.1 %all-to-all-start = ((f32[32,5,4,128]{3,2,1,0:T(4,128)}), f32[32,5,4,128]{3,2,1,0:T(4,128)S(1)}, u32[]{:S(2)}, u32[]{:S(2)}) async-start(f32[32,5,4,128]{3,2,1,0:T(4,128)} %bitcast), calls=%async_computation | async-start | bytes 655360 | tf_op jit(solution)/shard_map/all_to_all | solution.py:554
  20.9 20.9 %collective-permute-start = (f32[11,64,128]{2,1,0:T(8,128)}, f32[11,64,128]{2,1,0:T(8,128)}, u32[]{:S(2)}, u32[]{:S(2)}) collective-permute-start(f32[11,64,128]{2,1,0:T(8,128)} %get-tuple-element.24), channel_id=1, source_target_pairs={{0,31},{1,2},{2,1},{3,4},{4,3},{5,6},{6,5},{7,8},{8,7},{9,10},{10,... | collective-permute-start | bytes 1081352 | tf_op jit(solution)/shard_map/ppermute | solution.py:566
  23.4 18.5 %collective-permute-start.1 = (f32[11,64,128]{2,1,0:T(8,128)}, f32[11,64,128]{2,1,0:T(8,128)}, u32[]{:S(2)}, u32[]{:S(2)}) collective-permute-start(f32[11,64,128]{2,1,0:T(8,128)} %get-tuple-element.25), channel_id=1, source_target_pairs={{0,1},{1,0},{2,3},{3,2},{4,5},{5,4},{6,7},{7,6},{8,9},{9,8},{10,11... | collective-permute-start | bytes 1081352 | tf_op jit(solution)/shard_map/ppermute | solution.py:567
  31.5 20.5 %all-to-all-start.1 = ((f32[32,3,4,128]{3,2,1,0:T(4,128)}), f32[32,3,4,128]{3,2,1,0:T(4,128)S(1)}, u32[]{:S(2)}, u32[]{:S(2)}) async-start(f32[32,3,4,128]{3,2,1,0:T(4,128)} %bitcast.2), calls=%async_computation.1 | async-start | bytes 393216 | tf_op jit(solution)/shard_map/all_to_all | solution.py:554
  41.8 9.2 %collective-permute-start.2 = (f32[40,128]{1,0:T(8,128)S(1)}, f32[40,128]{1,0:T(8,128)S(1)}, u32[]{:S(2)}, u32[]{:S(2)}) collective-permute-start(f32[40,128]{1,0:T(8,128)S(1)} %get-tuple-element.26), channel_id=1, source_target_pairs={{0,32},{32,64},{64,96},{96,128},{128,160},{160,192},{192,224},{224... | collective-permute-start | bytes 61448 | tf_op jit(solution)/shard_map/ppermute | solution.py:574
  44.9 7.0 %collective-permute-start.3 = (f32[40,128]{1,0:T(8,128)S(1)}, f32[40,128]{1,0:T(8,128)S(1)}, u32[]{:S(2)}, u32[]{:S(2)}) collective-permute-start(f32[40,128]{1,0:T(8,128)S(1)} %get-tuple-element.27), channel_id=1, source_target_pairs={{0,480},{32,0},{64,32},{96,64},{128,96},{160,128},{192,160},{224,1... | collective-permute-start | bytes 61448 | tf_op jit(solution)/shard_map/ppermute | solution.py:575

commit v7 on v6

--- a/solution.py
+++ b/solution.py
@@ -23,7 +23,7 @@
 PACK_ROWS = SECTOR + NR // 2
 UP_ROWS, DOWN_ROWS = 0, 0
 ORDER = [(23 + n) % N_TH for n in range(N_TH)]
-BACK_ORDER = [(16 + n) % N_TH for n in range(N_TH)]
+BACK_ORDER = [(18 + n) % N_TH for n in range(N_TH)]
 ROW_FIELDS = 11
 
 HALF_STEP = 0.125

time: 54.3 us -> 54.3 us (level)
  no operation moved by 1% of the time
where the time goes in v7:
time: 54.3 us; the launch traced here: 53.9 us
  starting transfers between devices  43.6 us (80%)
  Pallas kernels  8.42 us (16%)
  waiting for transfers between devices  1.76 us (3%)
    all_to_all x2, starting transfers between devices, transposed(): lax.all_to_all(value, 'th', 0, 0, tiled=True, axis_index_groups=[order])  27.8 us
    ppermute x1, starting transfers between devices, per_device(): after = lax.ppermute(down, 'gz', [(i, (i - 1) % size) for i in range(size)])  6.09 us
    ppermute x1, starting transfers between devices, per_device(): th_near = lax.ppermute(near_row, 'th', pairs(N_TH, 0))  4.17 us
    ppermute x1, starting transfers between devices, per_device(): before = lax.ppermute(up, 'gz', [(i, (i + 1) % size) for i in range(size)])  3.1 us
    ppermute x1, starting transfers between devices, per_device(): th_far = lax.ppermute(far_row, 'th', pairs(N_TH, 1))  2.43 us
    pallas_call x1, Pallas kernels, inner_part(): pl.pallas_call(inner_kernel, grid=(1,), in_specs=[pl.BlockSpec((SECTOR, 1...  2.21 us
    pallas_call x1, Pallas kernels, finish(): pl.pallas_call(finish_kernel, in_specs=[WHOLE] * 4 + [pl.BlockSpec(memory...  1.97 us
    pallas_call x1, Pallas kernels, outer_part(): pl.pallas_call(outer_kernel, in_specs=[pl.BlockSpec(memory_space=pl.ANY)]...  1.87 us
  transfers between devices with their start and end apart: 6, of which 2 were waited for; matrix products, arithmetic and copies ran while one was open for 0% of the time, Pallas kernels for 8%

profile of v7, /device:TPU:1, one launch (start us, length us, event | category | flops | bytes accessed | tf_op | source)
XLA Modules:
  0.0 53.9 jit_solution(17179360661897200192)
XLA Ops:
  0.0 0.0 copy-start.2
  0.0 0.0 copy-start
  0.0 0.0 copy-start.1
  0.0 2.2 %inner_part.1 = f32[640,128]{1,0:T(8,128)} custom-call(f32[8,64,128]{2,1,0:T(8,128)} %d_ref.5, f32[3,8,64,128]{3,2,1,0:T(8,128)} %v_ref.5, f32[3,8,64,128]{3,2,1,0:T(8,128)} %v_ref.5, f32[3,8,64,128]{3,2,1,0:T(8,128)} %v_ref.5, f32[8,64,128]{2,1,0:T(8,128)} %p_ref.5), custom_call_target="tpu_custom_call" | custom-call | flops 1638400 | bytes 600000 | tf_op jit(solution)/shard_map/inner_part/pallas_call | solution.py:205
  2.2 17.5 %all-to-all-start = ((f32[32,5,4,128]{3,2,1,0:T(4,128)}), f32[32,5,4,128]{3,2,1,0:T(4,128)S(1)}, u32[]{:S(2)}, u32[]{:S(2)}) async-start(f32[32,5,4,128]{3,2,1,0:T(4,128)} %bitcast), calls=%async_computation | async-start | bytes 655360 | tf_op jit(solution)/shard_map/all_to_all | solution.py:554
  19.7 0.0 copy-done.2
  19.7 0.0 copy-done
  19.7 0.0 copy-done.1
  19.7 1.2 %edges.1 = (f32[11,64,128]{2,1,0:T(8,128)}, f32[11,64,128]{2,1,0:T(8,128)}, f32[64,128]{1,0:T(8,128)S(1)}) custom-call(f32[8,64,128]{2,1,0:T(8,128)S(1)} %copy-done.1, f32[3,8,64,128]{3,2,1,0:T(8,128)S(1)} %copy-done, f32[8,64,128]{2,1,0:T(8,128)S(1)} %copy-done.2), custom_call_target="tpu_custom_call" | custom-call | flops 983040 | bytes 1800000 | tf_op jit(solution)/shard_map/edges/pallas_call | solution.py:244
  20.9 2.4 %collective-permute-start = (f32[11,64,128]{2,1,0:T(8,128)}, f32[11,64,128]{2,1,0:T(8,128)}, u32[]{:S(2)}, u32[]{:S(2)}) collective-permute-start(f32[11,64,128]{2,1,0:T(8,128)} %get-tuple-element.24), channel_id=1, source_target_pairs={{0,31},{1,2},{2,1},{3,4},{4,3},{5,6},{6,5},{7,8},{8,7},{9,10},{10,... | collective-permute-start | bytes 1081352 | tf_op jit(solution)/shard_map/ppermute | solution.py:566
  23.4 4.2 %collective-permute-start.1 = (f32[11,64,128]{2,1,0:T(8,128)}, f32[11,64,128]{2,1,0:T(8,128)}, u32[]{:S(2)}, u32[]{:S(2)}) collective-permute-start(f32[11,64,128]{2,1,0:T(8,128)} %get-tuple-element.25), channel_id=1, source_target_pairs={{0,1},{1,0},{2,3},{3,2},{4,5},{5,4},{6,7},{7,6},{8,9},{9,8},{10,11... | collective-permute-start | bytes 1081352 | tf_op jit(solution)/shard_map/ppermute | solution.py:567
  27.5 1.9 %outer_part.1 = (f32[2240,128]{1,0:T(8,128)S(1)}, bf16[4,256,256]{2,1,0:T(8,128)(2,1)S(1)}, f32[256,128]{1,0:T(8,128)S(1)}) custom-call(bf16[9,256,256]{2,1,0:T(8,128)(2,1)} %constant.6.clone.high_ref, bf16[9,256,256]{2,1,0:T(8,128)(2,1)} %constant.7.clone.low_ref, f32[512,128]{1,0:T(8,128)} %constant.8.clone.table_ref, f32[8,64,128]{2,1,0:T(8,128)S(1)} %copy-done.1, ...), custom_call_target="tpu_custom_call" | custom-call | flops 16384000 | bytes 3000000 | tf_op jit(solution)/shard_map/outer_part/pallas_call | solution.py:428
  29.4 0.9 %all-to-all-done = f32[32,5,4,128]{3,2,1,0:T(4,128)S(1)} async-done(((f32[32,5,4,128]{3,2,1,0:T(4,128)}), f32[32,5,4,128]{3,2,1,0:T(4,128)S(1)}, u32[]{:S(2)}, u32[]{:S(2)}) %all-to-all-start) | async-done | bytes 327712 | tf_op jit(solution)/shard_map/all_to_all | solution.py:554
  30.3 1.2 %filtered.1 = (f32[384,128]{1,0:T(8,128)}, f32[40,128]{1,0:T(8,128)S(1)}, f32[40,128]{1,0:T(8,128)S(1)}) custom-call(f32[640,128]{1,0:T(8,128)S(1)} %bitcast.4, bf16[4,256,256]{2,1,0:T(8,128)(2,1)S(1)} %get-tuple-element.18.w_ref, f32[256,128]{1,0:T(8,128)S(1)} %get-tuple-element.19.weights_ref, f32[64,128]{1,0:T(8,128)S(1)} %get-tuple-element.20.columns_ref), custom_call_target="tpu_custom_call" | custom-call | flops 100663296 | bytes 1200000 | tf_op jit(solution)/shard_map/filtered/pallas_call | solution.py:334
  31.5 10.3 %all-to-all-start.1 = ((f32[32,3,4,128]{3,2,1,0:T(4,128)}), f32[32,3,4,128]{3,2,1,0:T(4,128)S(1)}, u32[]{:S(2)}, u32[]{:S(2)}) async-start(f32[32,3,4,128]{3,2,1,0:T(4,128)} %bitcast.2), calls=%async_computation.1 | async-start | bytes 393216 | tf_op jit(solution)/shard_map/all_to_all | solution.py:554
  41.8 0.0 collective-permute-done.back_ref
  41.8 0.0 collective-permute-done.1.side_ref
  41.8 3.1 %collective-permute-start.2 = (f32[40,128]{1,0:T(8,128)S(1)}, f32[40,128]{1,0:T(8,128)S(1)}, u32[]{:S(2)}, u32[]{:S(2)}) collective-permute-start(f32[40,128]{1,0:T(8,128)S(1)} %get-tuple-element.26), channel_id=1, source_target_pairs={{0,32},{32,64},{64,96},{96,128},{128,160},{160,192},{192,224},{224... | collective-permute-start | bytes 61448 | tf_op jit(solution)/shard_map/ppermute | solution.py:574
  44.9 6.1 %collective-permute-start.3 = (f32[40,128]{1,0:T(8,128)S(1)}, f32[40,128]{1,0:T(8,128)S(1)}, u32[]{:S(2)}, u32[]{:S(2)}) collective-permute-start(f32[40,128]{1,0:T(8,128)S(1)} %get-tuple-element.27), channel_id=1, source_target_pairs={{0,480},{32,0},{64,32},{96,64},{128,96},{160,128},{192,160},{224,1... | collective-permute-start | bytes 61448 | tf_op jit(solution)/shard_map/ppermute | solution.py:575
  51.0 0.0 collective-permute-done.2.before_ref
  51.0 0.9 %collective-permute-done.3.after_ref = f32[40,128]{1,0:T(8,128)S(1)} collective-permute-done((f32[40,128]{1,0:T(8,128)S(1)}, f32[40,128]{1,0:T(8,128)S(1)}, u32[]{:S(2)}, u32[]{:S(2)}) %collective-permute-start.3) | collective-permute-done | bytes 20512 | tf_op jit(solution)/shard_map/ppermute | solution.py:575
  51.9 0.0 all-to-all-done.1
  51.9 2.0 %finish.1 = f32[5,8,64,128]{3,2,1,0:T(8,128)} custom-call(f32[384,128]{1,0:T(8,128)S(1)} %bitcast.5, f32[40,128]{1,0:T(8,128)S(1)} %collective-permute-done.2.before_ref, f32[40,128]{1,0:T(8,128)S(1)} %collective-permute-done.3.after_ref, f32[2240,128]{1,0:T(8,128)S(1)} %get-tuple-element.28.rest_ref, f32[11,64,128]{2,1,0:T(8,128)} %collective-permute-done.1.side_ref, ...), custom_call_target="tpu_custom_call" | custom-call | flops 409600 | bytes 3000000 | tf_op jit(solution)/shard_map/finish/pallas_call | solution.py:528
Async XLA Ops:
  0.0 19.7 %copy-start.2 = (f32[8,64,128]{2,1,0:T(8,128)S(1)}, f32[8,64,128]{2,1,0:T(8,128)}, u32[]{:S(2)}) copy-start(f32[8,64,128]{2,1,0:T(8,128)} %p_ref.5) | copy-start | bytes 786436
  0.0 19.7 %copy-start = (f32[3,8,64,128]{3,2,1,0:T(8,128)S(1)}, f32[3,8,64,128]{3,2,1,0:T(8,128)}, u32[]{:S(2)}) copy-start(f32[3,8,64,128]{3,2,1,0:T(8,128)} %v_ref.5) | copy-start | bytes 2359300
  0.0 19.7 %copy-start.1 = (f32[8,64,128]{2,1,0:T(8,128)S(1)}, f32[8,64,128]{2,1,0:T(8,128)}, u32[]{:S(2)}) copy-start(f32[8,64,128]{2,1,0:T(8,128)} %d_ref.5) | copy-start | bytes 786436
  2.2 28.1 %all-to-all-start = ((f32[32,5,4,128]{3,2,1,0:T(4,128)}), f32[32,5,4,128]{3,2,1,0:T(4,128)S(1)}, u32[]{:S(2)}, u32[]{:S(2)}) async-start(f32[32,5,4,128]{3,2,1,0:T(4,128)} %bitcast), calls=%async_computation | async-start | bytes 655360 | tf_op jit(solution)/shard_map/all_to_all | solution.py:554
  20.9 20.9 %collective-permute-start = (f32[11,64,128]{2,1,0:T(8,128)}, f32[11,64,128]{2,1,0:T(8,128)}, u32[]{:S(2)}, u32[]{:S(2)}) collective-permute-start(f32[11,64,128]{2,1,0:T(8,128)} %get-tuple-element.24), channel_id=1, source_target_pairs={{0,31},{1,2},{2,1},{3,4},{4,3},{5,6},{6,5},{7,8},{8,7},{9,10},{10,... | collective-permute-start | bytes 1081352 | tf_op jit(solution)/shard_map/ppermute | solution.py:566
  23.4 18.5 %collective-permute-start.1 = (f32[11,64,128]{2,1,0:T(8,128)}, f32[11,64,128]{2,1,0:T(8,128)}, u32[]{:S(2)}, u32[]{:S(2)}) collective-permute-start(f32[11,64,128]{2,1,0:T(8,128)} %get-tuple-element.25), channel_id=1, source_target_pairs={{0,1},{1,0},{2,3},{3,2},{4,5},{5,4},{6,7},{7,6},{8,9},{9,8},{10,11... | collective-permute-start | bytes 1081352 | tf_op jit(solution)/shard_map/ppermute | solution.py:567
  31.5 20.5 %all-to-all-start.1 = ((f32[32,3,4,128]{3,2,1,0:T(4,128)}), f32[32,3,4,128]{3,2,1,0:T(4,128)S(1)}, u32[]{:S(2)}, u32[]{:S(2)}) async-start(f32[32,3,4,128]{3,2,1,0:T(4,128)} %bitcast.2), calls=%async_computation.1 | async-start | bytes 393216 | tf_op jit(solution)/shard_map/all_to_all | solution.py:554
  41.8 9.2 %collective-permute-start.2 = (f32[40,128]{1,0:T(8,128)S(1)}, f32[40,128]{1,0:T(8,128)S(1)}, u32[]{:S(2)}, u32[]{:S(2)}) collective-permute-start(f32[40,128]{1,0:T(8,128)S(1)} %get-tuple-element.26), channel_id=1, source_target_pairs={{0,32},{32,64},{64,96},{96,128},{128,160},{160,192},{192,224},{224... | collective-permute-start | bytes 61448 | tf_op jit(solution)/shard_map/ppermute | solution.py:574
  44.9 7.0 %collective-permute-start.3 = (f32[40,128]{1,0:T(8,128)S(1)}, f32[40,128]{1,0:T(8,128)S(1)}, u32[]{:S(2)}, u32[]{:S(2)}) collective-permute-start(f32[40,128]{1,0:T(8,128)S(1)} %get-tuple-element.27), channel_id=1, source_target_pairs={{0,480},{32,0},{64,32},{96,64},{128,96},{160,128},{192,160},{224,1... | collective-permute-start | bytes 61448 | tf_op jit(solution)/shard_map/ppermute | solution.py:575
